TPU v7x, 32 devices: a whole 2x2x4 slice. The times are simulated.
32 devices in a mesh: groups: 2 (over y), tensor: 4 (over z), dp: 2 (over x), sub: 2 (over core).
Axes of the slice: x: 2, y: 2, z: 4, core: 2. Of those that a mesh axis runs over, the one named last changes fastest.
Arguments:
- tokens: bfloat16 [4, 4, 128, 8192], P(('groups', 'dp'), None, 'tensor', 'sub'), parts along dimension 0, may hold values from -6 to 6
- cotangent: bfloat16 [4, 4, 128, 8192], P(('groups', 'dp'), None, 'tensor', 'sub'), parts along dimension 0, may hold values from -6 to 6
- w_up: bfloat16 [1024, 8192], P(('tensor', 'dp'), 'sub'), may hold values from -0.0625 to 0.0625
- w_down: bfloat16 [1024, 8192], P(('tensor', 'dp'), 'sub'), may hold values from -0.1875 to 0.1875
- active: int32 [4, 4, 1], P(('groups', 'dp')), parts along dimension 0, may hold values from 0 to 3; in each aligned block of 4 rows (0 to 3, 4 to 7, ..., all dimensions but the last counted through in order) at most 3 rows name the same one
Outputs:
- grad_tokens: bfloat16 [4, 4, 128, 8192], P(('groups', 'dp'), None, 'tensor', 'sub'), parts along dimension 0
- grad_up: bfloat16 [2048, 8192], P(('groups', 'tensor', 'dp'), 'sub'), parts along dimension 0
- grad_down: bfloat16 [2048, 8192], P(('groups', 'tensor', 'dp'), 'sub'), parts along dimension 0
There are 2 independent parts, one for each index of `groups`. A program takes and returns all parts, laid end to end along the dimension named above; an argument that names none is the same for every part. Nothing has to cross between parts.
Inputs may be any that keep to these rules, and one draw needn't show every extreme that they name: `active`: each row lists 1 distinct blocks. Among the 4 tiles of one data replica no block is listed by more than 3 tiles, and some block is listed by exactly 3 tiles of some replica.
All inputs are finite; a program needn't handle non-finite values.
Results may differ from a plain program's by a relative error of at most 0.017.
Values may be sent and summed in bfloat16 or wider, within the bound.
No kernel may reach another device: no remote copies, remote signals or barrier semaphores. Data moves between devices by JAX's collectives and lax.ppermute only.
A program may use at most 64 MiB of HBM per device.

v0:
```python
import jax
import jax.numpy as jnp
from jax import lax
from jax.sharding import PartitionSpec as P

MOST = 3


def shards(tokens, cotangent, w_up, w_down, active):
    tile_count = tokens.shape[1]
    part_rows = tokens.shape[2]
    half_width = tokens.shape[3]
    owners = lax.axis_size("tensor")
    block_ids = active[0]
    owner_list = jnp.arange(owners, dtype=jnp.int32)
    listed = jnp.any(block_ids[:, :, None] == owner_list[None, None, :], axis=1).astype(jnp.int32)
    ranking = jnp.cumsum(listed, axis=0) - 1
    slot_ids = jnp.arange(MOST, dtype=jnp.int32)
    choose = (listed.T[:, None, :] == 1) & (ranking.T[:, None, :] == slot_ids[None, :, None])
    choose_half = choose.astype(jnp.bfloat16)
    choose_full = choose.astype(jnp.float32)
    send_tok = jnp.einsum(
        "omt,trd->omrd", choose_half, tokens[0], preferred_element_type=jnp.float32
    ).astype(jnp.bfloat16)
    send_cot = jnp.einsum(
        "omt,trd->omrd", choose_half, cotangent[0], preferred_element_type=jnp.float32
    ).astype(jnp.bfloat16)
    up_weight_block, down_weight_block = (
        lax.all_gather(w_up, "dp", axis=0, tiled=True),
        lax.all_gather(w_down, "dp", axis=0, tiled=True),
    )
    got_tok, got_cot = (
        lax.all_to_all(send_tok, "tensor", split_axis=0, concat_axis=2, tiled=True),
        lax.all_to_all(send_cot, "tensor", split_axis=0, concat_axis=2, tiled=True),
    )
    slot_token = got_tok[0]
    slot_cotangent = got_cot[0]
    partial_hidden = jnp.einsum(
        "bkn,vn->bkv", slot_token, up_weight_block, preferred_element_type=jnp.float32
    )
    partial_grad = jnp.einsum(
        "bkn,vn->bkv", slot_cotangent, down_weight_block, preferred_element_type=jnp.float32
    )
    hidden, grad_act = (
        lax.psum(partial_hidden.astype(jnp.bfloat16), "sub").astype(jnp.float32),
        lax.psum(partial_grad.astype(jnp.bfloat16), "sub").astype(jnp.float32),
    )
    positive = jnp.maximum(hidden, 0.0)
    squared_activation = (positive * positive).astype(jnp.bfloat16)
    hidden_gradient = (2.0 * positive * grad_act).astype(jnp.bfloat16)
    back_rows = jnp.einsum(
        "opl,la->opa", hidden_gradient, up_weight_block, preferred_element_type=jnp.float32
    ).astype(jnp.bfloat16)
    back_rows = back_rows.reshape(MOST, owners, part_rows, half_width)
    received = lax.all_to_all(back_rows, "tensor", split_axis=1, concat_axis=1, tiled=True)
    summed = jnp.einsum(
        "omt,mord->trd", choose_full, received.astype(jnp.float32), precision=lax.Precision.HIGHEST
    )
    grad_tokens = summed.astype(jnp.bfloat16).reshape(1, tile_count, part_rows, half_width)
    up_weight_term = jnp.einsum(
        "epn,epk->nk", hidden_gradient, slot_token, preferred_element_type=jnp.float32
    )
    down_weight_term = jnp.einsum(
        "epn,epk->nk", squared_activation, slot_cotangent, preferred_element_type=jnp.float32
    )
    weight_grads = lax.psum_scatter(
        jnp.concatenate([up_weight_term, down_weight_term], axis=1).astype(jnp.bfloat16),
        "dp",
        scatter_dimension=0,
        tiled=True,
    ).astype(jnp.float32)
    grad_up = weight_grads[:, :half_width].astype(jnp.bfloat16)
    grad_down = weight_grads[:, half_width:].astype(jnp.bfloat16)
    return (grad_tokens, grad_up, grad_down)


def solution(mesh):
    placed = (
        P(("groups", "dp"), None, "tensor", "sub"),
        P(("groups", "dp"), None, "tensor", "sub"),
        P(("tensor", "dp"), "sub"),
        P(("tensor", "dp"), "sub"),
        P(("groups", "dp"), None, None),
    )
    return jax.shard_map(
        shards,
        mesh=mesh,
        in_specs=placed,
        out_specs=(
            P(("groups", "dp"), None, "tensor", "sub"),
            P(("groups", "tensor", "dp"), "sub"),
            P(("groups", "tensor", "dp"), "sub"),
        ),
        check_vma=False,
    )
```

profile of v0, /device:TPU:0, one launch (start us, length us, event | category | flops | bytes accessed | tf_op | source)
XLA Modules:
  0.0 299.4 jit_solution(12726069001462644846)
XLA Ops:
  7.2 0.7 fusion.25
  7.9 0.7 convert_compare_fusion
  8.7 3.4 %convolution_convert_fusion.1 = bf16[4,3,32,4096]{3,0,2,1:T(4,128)(2,1)S(1)} fusion(bf16[4,32,4096]{2,1,0:T(8,128)(2,1)} %bitcast.71, s32[4,4]{0,1:T(4,128)S(1)} %add_bitcast_fusion, pred[4,4]{0,1:T(4,128)(4,1)S(1)} %convert_compare_fusion), kind=kOutput, calls=%fused_computation.1 | convolution fusion | flops 14155872 | bytes 4194384 | tf_op jit(solution)/shard_map/omt,trd->omrd/dot_general | solution.py:22
  12.1 3.4 %copy.41 = bf16[4,3,32,4096]{3,2,1,0:T(8,128)(2,1)} copy(bf16[4,3,32,4096]{3,0,2,1:T(4,128)(2,1)S(1)} %convolution_convert_fusion.1) | data formatting | bytes 6291456 | tf_op jit(solution)/shard_map/convert_element_type | solution.py:24
  15.4 6.3 %all-to-all-start = ((bf16[4,3,32,4096]{3,2,1,0:T(8,128)(2,1)}), bf16[4,3,32,4096]{3,2,1,0:T(8,128)(2,1)S(1)}, u32[]{:S(2)}, u32[]{:S(2)}) async-start(bf16[4,3,32,4096]{3,2,1,0:T(8,128)(2,1)} %copy.41), calls=%async_computation | async-start | bytes 6291456 | tf_op jit(solution)/shard_map/all_to_all | solution.py:33
  21.7 3.4 %convolution_convert_fusion = bf16[4,3,32,4096]{3,0,2,1:T(4,128)(2,1)S(1)} fusion(bf16[4,32,4096]{2,1,0:T(8,128)(2,1)} %bitcast.72, s32[4,4]{0,1:T(4,128)S(1)} %add_bitcast_fusion, pred[4,4]{0,1:T(4,128)(4,1)S(1)} %convert_compare_fusion), kind=kOutput, calls=%fused_computation | convolution fusion | flops 14155872 | bytes 4194384 | tf_op jit(solution)/shard_map/omt,trd->omrd/dot_general | solution.py:25
  25.2 3.4 %copy.45 = bf16[4,3,32,4096]{3,2,1,0:T(8,128)(2,1)} copy(bf16[4,3,32,4096]{3,0,2,1:T(4,128)(2,1)S(1)} %convolution_convert_fusion) | data formatting | bytes 6291456 | tf_op jit(solution)/shard_map/convert_element_type | solution.py:27
  28.5 63.9 %all-to-all-done = bf16[4,3,32,4096]{3,2,1,0:T(8,128)(2,1)S(1)} async-done(((bf16[4,3,32,4096]{3,2,1,0:T(8,128)(2,1)}), bf16[4,3,32,4096]{3,2,1,0:T(8,128)(2,1)S(1)}, u32[]{:S(2)}, u32[]{:S(2)}) %all-to-all-start) | async-done | bytes 3145760 | tf_op jit(solution)/shard_map/all_to_all | solution.py:33
  92.4 4.7 %all-to-all-start.1 = ((bf16[4,3,32,4096]{3,2,1,0:T(8,128)(2,1)}), bf16[4,3,32,4096]{3,2,1,0:T(8,128)(2,1)}, u32[]{:S(2)}, u32[]{:S(2)}) async-start(bf16[4,3,32,4096]{3,2,1,0:T(8,128)(2,1)} %copy.45), calls=%async_computation.1 | async-start | bytes 6291456 | tf_op jit(solution)/shard_map/all_to_all | solution.py:34
  97.1 0.0 all-gather.3.cloned.1.call-start
  97.1 0.7 all-gather.3.cloned.1.call-update
  97.8 0.0 all-gather.5.cloned.1.call-start
  97.9 0.7 all-gather.5.cloned.1.call-update
  98.6 0.0 all-reduce.3.cloned.1.call-start
  98.6 1.9 copy.42
  100.5 66.8 %all-to-all-done.1 = bf16[4,3,32,4096]{3,2,1,0:T(8,128)(2,1)} async-done(((bf16[4,3,32,4096]{3,2,1,0:T(8,128)(2,1)}), bf16[4,3,32,4096]{3,2,1,0:T(8,128)(2,1)}, u32[]{:S(2)}, u32[]{:S(2)}) %all-to-all-start.1) | async-done | bytes 3145760 | tf_op jit(solution)/shard_map/all_to_all | solution.py:34
  167.3 3.9 %copy.46 = bf16[4,3,32,4096]{3,2,0,1:T(8,128)(2,1)} copy(bf16[4,3,32,4096]{3,2,1,0:T(8,128)(2,1)} %all-to-all-done.1) | data formatting | bytes 6291456 | tf_op jit(solution)/shard_map/all_to_all | solution.py:34
  171.2 3.3 %fusion.10 = bf16[3,128,256]{2,1,0:T(8,128)(2,1)} fusion(bf16[3,128,4096]{2,1,0:T(8,128)(2,1)S(1)} %bitcast.67, bf16[256,4096]{1,0:T(8,128)(2,1)} %all-gather.3.cloned.1.call-done), kind=kOutput, calls=%fused_computation.17 | convolution fusion | flops 805404672 | bytes 5439488 | tf_op jit(solution)/shard_map/bkn,vn->bkv/dot_general | solution.py:38
  174.5 4.2 %fusion.13 = bf16[3,128,256]{2,1,0:T(8,128)(2,1)} fusion(bf16[3,128,4096]{2,1,0:T(8,128)(2,1)} %bitcast.69, bf16[256,4096]{1,0:T(8,128)(2,1)} %all-gather.5.cloned.1.call-done), kind=kOutput, calls=%fused_computation.18 | convolution fusion | flops 805404672 | bytes 5439488 | tf_op jit(solution)/shard_map/bkn,vn->bkv/dot_general | solution.py:41
  178.8 0.0 all-reduce.3.cloned.1.call-update
  178.8 0.2 reduce-scatter.2.cloned.1.call-start
  179.0 17.6 %all-reduce.3.cloned.1.call-done = (bf16[3,128,256]{2,1,0:T(8,128)(2,1)}, bf16[3,128,256]{2,1,0:T(8,128)(2,1)}) async-done(((bf16[3,128,256]{2,1,0:T(8,128)(2,1)}, bf16[3,128,256]{2,1,0:T(8,128)(2,1)}), (bf16[3,128,256]{2,1,0:T(8,128)(2,1)}, bf16[3,128,256]{2,1,0:T(8,128)(2,1)})) %all-reduce.3.cloned.1.call-update) | async-done | bytes 393232 | tf_op jit(solution)/shard_map/psum | solution.py:46
  196.6 3.3 %fusion.1 = bf16[256,4096]{1,0:T(8,128)(2,1)S(1)} fusion(bf16[3,128,4096]{2,1,0:T(8,128)(2,1)} %bitcast.70, bf16[3,128,256]{2,1,0:T(8,128)(2,1)} %get-tuple-element.16), kind=kOutput, calls=%fused_computation.6 | convolution fusion | flops 806748160 | bytes 5439488 | tf_op jit(solution)/shard_map/epn,epk->nk/dot_general | solution.py:63
  200.0 1.3 fusion
  201.3 2.4 pad_maximum_fusion
  203.7 1.6 copy-done.2
  205.2 1.0 convolution_convert_fusion.2
  206.2 0.3 copy.47
  206.6 75.8 %all_to_all.35 = bf16[3,4,32,4096]{3,2,0,1:T(8,128)(2,1)S(1)} all-to-all(bf16[3,4,32,4096]{3,2,0,1:T(8,128)(2,1)S(1)} %copy.47), channel_id=1, replica_groups=mesh['groups'=2,'tensor'=4,'dp'=2,'sub'=2] {'tensor'}, dimensions={1} | all-to-all | bytes 6291456 | tf_op jit(solution)/shard_map/all_to_all | solution.py:55
  282.4 5.9 %fusion.3 = bf16[1,4,32,4096]{3,1,2,0:T(4,128)(2,1)S(1)} fusion(bf16[3,4,32,4096]{3,2,0,1:T(8,128)(2,1)S(1)} %all_to_all.35, s32[4,4]{0,1:T(4,128)S(1)} %add_bitcast_fusion, pred[4,4]{0,1:T(4,128)(4,1)S(1)} %convert_compare_fusion), kind=kOutput, calls=%fused_computation.9 | convolution fusion | flops 13107296 | bytes 4194384 | tf_op jit(solution)/shard_map/omt,mord->trd/dot_general | solution.py:56
  288.3 1.6 copy.51
  289.8 3.1 %fusion.34 = (bf16[128,4096]{1,0:T(8,128)(2,1)}, bf16[128,4096]{1,0:T(8,128)(2,1)}) fusion(bf16[128,8192]{1,0:T(8,128)(2,1)} %reduce-scatter.2.cloned.1.call-done), kind=kLoop, calls=%fused_computation.42 | loop fusion | bytes 4194304 | tf_op jit(solution)/shard_map/slice | solution.py:73
  (13 shorter events, 0.1 us)
Async XLA Ops:
  15.4 77.0 %all-to-all-start = ((bf16[4,3,32,4096]{3,2,1,0:T(8,128)(2,1)}), bf16[4,3,32,4096]{3,2,1,0:T(8,128)(2,1)S(1)}, u32[]{:S(2)}, u32[]{:S(2)}) async-start(bf16[4,3,32,4096]{3,2,1,0:T(8,128)(2,1)} %copy.41), calls=%async_computation | async-start | bytes 6291456 | tf_op jit(solution)/shard_map/all_to_all | solution.py:33
  92.4 74.9 %all-to-all-start.1 = ((bf16[4,3,32,4096]{3,2,1,0:T(8,128)(2,1)}), bf16[4,3,32,4096]{3,2,1,0:T(8,128)(2,1)}, u32[]{:S(2)}, u32[]{:S(2)}) async-start(bf16[4,3,32,4096]{3,2,1,0:T(8,128)(2,1)} %copy.45), calls=%async_computation.1 | async-start | bytes 6291456 | tf_op jit(solution)/shard_map/all_to_all | solution.py:34
  97.1 74.1 %all-gather.3.cloned.1.call-start = ((), (), s32[]{:S(2)}) async-start(), calls=%async_computation.4 | async-start | bytes 3145728 | tf_op jit(solution)/shard_map/all_gather | solution.py:29
  97.8 76.7 %all-gather.5.cloned.1.call-start = ((), (), s32[]{:S(2)}) async-start(), calls=%async_computation.5 | async-start | bytes 3145728 | tf_op jit(solution)/shard_map/all_gather | solution.py:30
  98.6 98.0 %all-reduce.3.cloned.1.call-start = ((), (), s32[]{:S(2)}) async-start(), calls=%async_computation.7 | async-start | bytes 786432 | tf_op jit(solution)/shard_map/psum | solution.py:46
  100.5 70.7 %copy-start = (bf16[4,3,32,4096]{3,2,0,1:T(8,128)(2,1)S(1)}, bf16[4,3,32,4096]{3,2,0,1:T(8,128)(2,1)}, u32[]{:S(2)}) copy-start(bf16[4,3,32,4096]{3,2,0,1:T(8,128)(2,1)} %copy.42) | copy-start | bytes 9437188
  178.8 111.0 %reduce-scatter.2.cloned.1.call-start = ((), (), s32[]{:S(2)}) async-start(), calls=%async_computation.6 | async-start | bytes 6291456 | tf_op jit(solution)/shard_map/reduce_scatter | solution.py:66
  196.6 3.3 %copy-start.1 = (bf16[3,128,256]{2,1,0:T(8,128)(2,1)S(1)}, bf16[3,128,256]{2,1,0:T(8,128)(2,1)}, u32[]{:S(2)}) copy-start(bf16[3,128,256]{2,1,0:T(8,128)(2,1)} %get-tuple-element.16) | copy-start | bytes 589828
  196.6 3.3 %copy-start.3 = (bf16[3,128,256]{2,1,0:T(8,128)(2,1)S(1)}, bf16[3,128,256]{2,1,0:T(8,128)(2,1)}, u32[]{:S(2)}) copy-start(bf16[3,128,256]{2,1,0:T(8,128)(2,1)} %get-tuple-element.15) | copy-start | bytes 589828
  203.6 1.6 copy-start.2
Sparse Core Ops, SparseCore 0:
  99.5 34.5 all-gather.2
  135.6 33.1 all-gather.4
  178.9 17.6 all-reduce.2
  203.8 55.4 reduce-scatter.1
where the time goes:
time: 300 us; the launch traced here: 299 us
  waiting for transfers between devices  150 us (50%)
  blocking collectives  75.8 us (25%)
  matrix products  25.8 us (9%)
  local copies, waits for them, and re-layouts  19.1 us (6%)
  between operations  13.8 us (5%)
  starting transfers between devices  11.3 us (4%)
  other arithmetic  3.88 us (1%)
    all_to_all x1, blocking collectives, shards(): lax.all_to_all(back_rows, 'tensor', split_axis=1, concat_axis=1, tiled=True)  75.8 us
    all_to_all x1, waiting for transfers between devices, shards(): lax.all_to_all(send_cot, 'tensor', split_axis=0, concat_axis=2, tiled=True)  66.8 us
    all_to_all x1, waiting for transfers between devices, shards(): lax.all_to_all(send_tok, 'tensor', split_axis=0, concat_axis=2, tiled=True)  63.9 us
    psum x1, waiting for transfers between devices, shards(): lax.psum(partial_grad.astype(jnp.bfloat16), 'sub').astype(jnp.float32)  17.6 us
    all_to_all x1, starting transfers between devices, shards(): lax.all_to_all(send_tok, 'tensor', split_axis=0, concat_axis=2, tiled=True)  6.32 us
  transfers between devices with their start and end apart: 6, of which 3 were waited for; matrix products, arithmetic and copies ran while one was open for 8% of the time, Pallas kernels for 0%

commit v1 on v0

v1 whole, which is shorter than its diff:
```python
import functools

import jax
import jax.numpy as jnp
from jax import lax
from jax.experimental import pallas as pl
from jax.experimental.pallas import tpu as pltpu
from jax.sharding import PartitionSpec as P

MOST = 3
F32 = jnp.float32
BF16 = jnp.bfloat16


def plain(tokens, cotangent, w_up, w_down, active):
    tile_count = tokens.shape[1]
    part_rows = tokens.shape[2]
    half_width = tokens.shape[3]
    owners = lax.axis_size("tensor")
    block_ids = active[0]
    owner_list = jnp.arange(owners, dtype=jnp.int32)
    listed = jnp.any(block_ids[:, :, None] == owner_list[None, None, :], axis=1).astype(jnp.int32)
    ranking = jnp.cumsum(listed, axis=0) - 1
    slot_ids = jnp.arange(MOST, dtype=jnp.int32)
    choose = (listed.T[:, None, :] == 1) & (ranking.T[:, None, :] == slot_ids[None, :, None])
    choose_half = choose.astype(BF16)
    choose_full = choose.astype(F32)
    send_tok = jnp.einsum("omt,trd->omrd", choose_half, tokens[0], preferred_element_type=F32).astype(BF16)
    send_cot = jnp.einsum("omt,trd->omrd", choose_half, cotangent[0], preferred_element_type=F32).astype(BF16)
    up_weight_block = lax.all_gather(w_up, "dp", axis=0, tiled=True)
    down_weight_block = lax.all_gather(w_down, "dp", axis=0, tiled=True)
    slot_token = lax.all_to_all(send_tok, "tensor", split_axis=0, concat_axis=2, tiled=True)[0]
    slot_cotangent = lax.all_to_all(send_cot, "tensor", split_axis=0, concat_axis=2, tiled=True)[0]
    partial_hidden = jnp.einsum("bkn,vn->bkv", slot_token, up_weight_block, preferred_element_type=F32)
    partial_grad = jnp.einsum("bkn,vn->bkv", slot_cotangent, down_weight_block, preferred_element_type=F32)
    hidden = lax.psum(partial_hidden.astype(BF16), "sub").astype(F32)
    grad_act = lax.psum(partial_grad.astype(BF16), "sub").astype(F32)
    positive = jnp.maximum(hidden, 0.0)
    squared_activation = (positive * positive).astype(BF16)
    hidden_gradient = (2.0 * positive * grad_act).astype(BF16)
    back_rows = jnp.einsum("opl,la->opa", hidden_gradient, up_weight_block, preferred_element_type=F32).astype(BF16)
    back_rows = back_rows.reshape(MOST, owners, part_rows, half_width)
    received = lax.all_to_all(back_rows, "tensor", split_axis=1, concat_axis=1, tiled=True)
    summed = jnp.einsum("omt,mord->trd", choose_full, received.astype(F32), precision=lax.Precision.HIGHEST)
    grad_tokens = summed.astype(BF16).reshape(1, tile_count, part_rows, half_width)
    up_weight_term = jnp.einsum("epn,epk->nk", hidden_gradient, slot_token, preferred_element_type=F32)
    down_weight_term = jnp.einsum("epn,epk->nk", squared_activation, slot_cotangent, preferred_element_type=F32)
    weight_grads = lax.psum_scatter(
        jnp.concatenate([up_weight_term, down_weight_term], axis=1).astype(BF16),
        "dp",
        scatter_dimension=0,
        tiled=True,
    )
    return grad_tokens, weight_grads[:, :half_width], weight_grads[:, half_width:]


def swap(x, axis):
    return lax.ppermute(x, axis, [(0, 1), (1, 0)])


def halves(x, side):
    width = x.shape[-1] // 2
    keep = lax.dynamic_slice_in_dim(x, side * width, width, x.ndim - 1)
    pass_on = lax.dynamic_slice_in_dim(x, (1 - side) * width, width, x.ndim - 1)
    return keep, pass_on


def ordered(mine, other, side, axis):
    return jnp.where(
        side == 0,
        jnp.concatenate([mine, other], axis),
        jnp.concatenate([other, mine], axis),
    )


def dispatch_kernel(owners, slots, tiles, meta, keep, got, *outs):
    side, place = meta[0], meta[1]
    for k in range(owners):
        owner = lax.rem(place + k, owners)
        for s in range(slots):
            tile = meta[2 + owner * slots + s]
            own = lax.div(tile, tiles) == side
            at = lax.rem(tile, tiles)

            @pl.when(own)
            def _():
                outs[k][s] = keep[at]

            @pl.when(jnp.logical_not(own))
            def _():
                outs[k][s] = got[at]


def dispatch(meta, keep, got, owners, slots):
    tiles, rows, width = keep.shape
    return pl.pallas_call(
        functools.partial(dispatch_kernel, owners, slots, tiles),
        out_shape=[jax.ShapeDtypeStruct((slots, rows, width), keep.dtype)] * owners,
        in_specs=[
            pl.BlockSpec(memory_space=pltpu.SMEM),
            pl.BlockSpec(memory_space=pltpu.VMEM),
            pl.BlockSpec(memory_space=pltpu.VMEM),
        ],
        out_specs=[pl.BlockSpec(memory_space=pltpu.VMEM)] * owners,
        compiler_params=pltpu.CompilerParams(vmem_limit_bytes=32 << 20),
        cost_estimate=pl.CostEstimate(
            flops=0, bytes_accessed=4 * owners * slots * rows * width, transcendentals=0
        ),
    )(meta, keep, got)


def collect_kernel(owners, slots, tiles, meta, *rest):
    pieces, mine, other = rest[:owners], rest[owners], rest[owners + 1]
    side, place = meta[0], meta[1]
    base = 2 + owners * slots
    for r in range(2):
        out = mine if r == 0 else other
        replica = side if r == 0 else 1 - side
        for t in range(tiles):
            tile = replica * tiles + t
            k = lax.rem(meta[base + tile] - place + owners, owners)
            slot = meta[base + 2 * tiles + tile]
            for kk in range(owners):

                @pl.when(k == kk)
                def _():
                    out[t] = pieces[kk][slot]


def collect(meta, pieces, tiles):
    owners = len(pieces)
    slots, rows, width = pieces[0].shape
    return pl.pallas_call(
        functools.partial(collect_kernel, owners, slots, tiles),
        out_shape=[jax.ShapeDtypeStruct((tiles, rows, width), pieces[0].dtype)] * 2,
        in_specs=[pl.BlockSpec(memory_space=pltpu.SMEM)]
        + [pl.BlockSpec(memory_space=pltpu.VMEM)] * owners,
        out_specs=[pl.BlockSpec(memory_space=pltpu.VMEM)] * 2,
        compiler_params=pltpu.CompilerParams(vmem_limit_bytes=32 << 20),
        cost_estimate=pl.CostEstimate(
            flops=0, bytes_accessed=8 * tiles * rows * width, transcendentals=0
        ),
    )(meta, *pieces)


def shards(tokens, cotangent, w_up, w_down, active):
    owners = lax.axis_size("tensor")
    replicas = lax.axis_size("dp")
    subs = lax.axis_size("sub")
    if replicas != 2 or subs != 2 or active.shape[2] != 1 or tokens.shape[2] % 16:
        return plain(tokens, cotangent, w_up, w_down, active)
    tiles = tokens.shape[1]
    rows = tokens.shape[2]
    slots = MOST + replicas - 1
    side = lax.axis_index("dp")
    place = lax.axis_index("tensor")

    listed = active.reshape(tiles)
    listed_other = swap(jnp.broadcast_to(listed[None, :], (8, tiles)), "dp")[0]
    blocks = ordered(listed, listed_other, side, 0)
    tok_keep, tok_pass = halves(tokens[0], side)
    tok_got = swap(tok_pass, "dp")

    owner_ids = jnp.arange(owners, dtype=jnp.int32)
    hot = (blocks[:, None] == owner_ids[None, :]).astype(jnp.int32)
    counts = jnp.sum(hot, axis=0)
    before = (jnp.arange(2 * tiles)[None, :] < jnp.arange(2 * tiles)[:, None]) & (
        blocks[:, None] == blocks[None, :]
    )
    slot_of = jnp.sum(before.astype(jnp.int32), axis=1)
    match = (
        (blocks[None, None, :] == owner_ids[:, None, None])
        & (slot_of[None, None, :] == jnp.arange(slots, dtype=jnp.int32)[None, :, None])
    )
    table = jnp.sum(match * jnp.arange(2 * tiles, dtype=jnp.int32)[None, None, :], axis=2)
    meta = jnp.concatenate(
        [
            jnp.stack([side, place]).astype(jnp.int32),
            table.reshape(-1).astype(jnp.int32),
            blocks.astype(jnp.int32),
            slot_of.astype(jnp.int32),
        ]
    )
    crowd = jnp.max(counts)
    crowd = jnp.maximum(crowd, swap(jnp.broadcast_to(crowd, (8, 128)), "groups")[0, 0])
    mine_count = jnp.sum(jnp.where(owner_ids == place, counts, 0))

    def balanced(tok_keep, tok_got, cotangent, w_up, w_down, meta, mine_count):
        def send(keep, got):
            pieces = dispatch(meta, keep, got, owners, slots)
            arrived = [pieces[0]] + [
                lax.ppermute(pieces[k], "tensor", [(i, (i + k) % owners) for i in range(owners)])
                for k in range(1, owners)
            ]
            return jnp.concatenate(arrived, 0).reshape(owners * slots * rows, -1)

        def both_rows(w):
            keep, pass_on = halves(w, side)
            return ordered(keep, swap(pass_on, "dp"), side, 0)

        def total(part):
            part = part + swap(part.astype(BF16), "sub").astype(F32)
            return part + swap(part.astype(BF16), "dp").astype(F32)

        cot_keep, cot_pass = halves(cotangent[0], side)
        cot_got = swap(cot_pass, "dp")
        tok = send(tok_keep, tok_got)
        up = both_rows(w_up)
        down = both_rows(w_down)
        cot = send(cot_keep, cot_got)
        dims = (((1,), (1,)), ((), ()))
        hidden = total(lax.dot_general(tok, up, dims, preferred_element_type=F32))
        grad_act = total(lax.dot_general(cot, down, dims, preferred_element_type=F32))
        filled = (jnp.arange(slots) < mine_count)[None, :, None, None]
        filled = jnp.broadcast_to(filled, (owners, slots, rows, 1)).reshape(-1, 1)
        positive = jnp.where(filled, jnp.maximum(hidden, 0.0), 0.0)
        squared = (positive * positive).astype(BF16)
        grad_hidden = (2.0 * positive * grad_act).astype(BF16)
        back = jnp.dot(grad_hidden, up, preferred_element_type=F32).astype(BF16)
        back = back.reshape(owners, slots, rows, -1)
        home = [back[0]] + [
            lax.ppermute(back[k], "tensor", [((i + k) % owners, i) for i in range(owners)])
            for k in range(1, owners)
        ]
        mine, other = collect(meta, home, tiles)
        grad_tokens = ordered(mine, swap(other, "dp"), side, 2)[None]

        def weight_grad(act, data):
            g = lax.dot_general(act, data, (((0,), (0,)), ((), ())), preferred_element_type=F32).astype(BF16)
            n = g.shape[0] // 2
            keep = lax.dynamic_slice_in_dim(g, side * n, n, 0)
            pass_on = lax.dynamic_slice_in_dim(g, (1 - side) * n, n, 0)
            return ordered(keep, swap(pass_on, "dp"), side, 1)

        return grad_tokens, weight_grad(grad_hidden, tok), weight_grad(squared, cot)

    return lax.cond(
        crowd <= slots,
        lambda: balanced(tok_keep, tok_got, cotangent, w_up, w_down, meta, mine_count),
        lambda: plain(tokens, cotangent, w_up, w_down, active),
    )


def solution(mesh):
    placed = (
        P(("groups", "dp"), None, "tensor", "sub"),
        P(("groups", "dp"), None, "tensor", "sub"),
        P(("tensor", "dp"), "sub"),
        P(("tensor", "dp"), "sub"),
        P(("groups", "dp"), None, None),
    )
    return jax.shard_map(
        shards,
        mesh=mesh,
        in_specs=placed,
        out_specs=(
            P(("groups", "dp"), None, "tensor", "sub"),
            P(("groups", "tensor", "dp"), "sub"),
            P(("groups", "tensor", "dp"), "sub"),
        ),
        check_vma=False,
    )
```

time: 300 us -> 212 us (0.71)
  blocking collectives: 75.8 us -> 0 us
  waiting for transfers between devices: 150 us -> 92.2 us
  starting transfers between devices: 11.3 us -> 68.3 us
  matrix products: 25.8 us -> 8.7 us
  other arithmetic: 3.88 us -> 11.8 us
  local copies, waits for them, and re-layouts: 19.1 us -> 11.3 us
  Pallas kernels: 0 us -> 3.17 us
    all_to_all x2 -> x0, waiting for transfers between devices: 131 us -> none  [the longest x1 66.8 us: shards(): lax.all_to_all(send_cot, 'tensor', split_axis=0, concat_axis=2, tiled=True)]
    ppermute x0 -> x22, waiting for transfers between devices: none -> 92.2 us  [the longest x3 43.3 us: balanced(): lax.ppermute(back[k], 'tensor', [((i + k) % owners, i) for i in range(own...]
    all_to_all x1 -> x0, blocking collectives: 75.8 us -> none  [shards(): lax.all_to_all(back_rows, 'tensor', split_axis=1, concat_axis=1, tiled=True)]
    ppermute x0 -> x22, starting transfers between devices: none -> 68.3 us  [the longest x6 48.7 us: send(): lax.ppermute(pieces[k], 'tensor', [(i, (i + k) % owners) for i in range(o...]
    psum x1 -> x0, waiting for transfers between devices: 17.6 us -> none  [shards(): lax.psum(partial_grad.astype(jnp.bfloat16), 'sub').astype(jnp.float32)]
    dot_general x8 -> x5, matrix products: 25.8 us -> 8.7 us  [the longest x1 2.71 us: balanced(): hidden = total(lax.dot_general(tok, up, dims, preferred_element_type=F32))]
    all_to_all x2 -> x0, starting transfers between devices: 11 us -> none  [the longest x1 6.32 us: shards(): lax.all_to_all(send_tok, 'tensor', split_axis=0, concat_axis=2, tiled=True)]
    dynamic_slice x0 -> x7, local copies, waits for them, and re-layouts: none -> 8.35 us  [the longest x3 5.02 us: halves(): keep = lax.dynamic_slice_in_dim(x, side * width, width, x.ndim - 1)]
  transfers between devices with their start and end apart: 6 -> 22, of which waited for: 3 -> 12; matrix products, arithmetic and copies ran while one was open for 8% -> 13% of each run, Pallas kernels for 0% -> 1%
where the time goes in v1:
time: 212 us; the launch traced here: 211 us
  waiting for transfers between devices  92.2 us (43%)
  starting transfers between devices  68.3 us (32%)
  between operations  15.3 us (7%)
  other arithmetic  11.8 us (6%)
  local copies, waits for them, and re-layouts  11.3 us (5%)
  matrix products  8.7 us (4%)
  Pallas kernels  3.17 us (1%)
    ppermute x6, starting transfers between devices, send(): lax.ppermute(pieces[k], 'tensor', [(i, (i + k) % owners) for i in range(o...  48.7 us
    ppermute x3, waiting for transfers between devices, balanced(): lax.ppermute(back[k], 'tensor', [((i + k) % owners, i) for i in range(own...  43.3 us
    ppermute x13, waiting for transfers between devices, swap(): return lax.ppermute(x, axis, [(0, 1), (1, 0)])  33.3 us
    ppermute x6, waiting for transfers between devices, send(): lax.ppermute(pieces[k], 'tensor', [(i, (i + k) % owners) for i in range(o...  15.6 us
    ppermute x13, starting transfers between devices, swap(): return lax.ppermute(x, axis, [(0, 1), (1, 0)])  11.7 us
    ppermute x3, starting transfers between devices, balanced(): lax.ppermute(back[k], 'tensor', [((i + k) % owners, i) for i in range(own...  7.94 us
    dynamic_slice x3, local copies, waits for them, and re-layouts, halves(): keep = lax.dynamic_slice_in_dim(x, side * width, width, x.ndim - 1)  5.02 us
    select_n x4, other arithmetic, ordered(): jnp.where(side == 0, jnp.concatenate([mine, other], axis), jnp.concatenat...  4.45 us
  transfers between devices with their start and end apart: 22, of which 12 were waited for; matrix products, arithmetic and copies ran while one was open for 13% of the time, Pallas kernels for 1%

profile of v1, /device:TPU:0, one launch (start us, length us, event | category | flops | bytes accessed | tf_op | source)
XLA Modules:
  0.0 211.0 jit_solution(1204486884079020517)
XLA Ops:
  7.8 2.9 %collective-permute-start.19 = (s32[8,4]{1,0:T(8,128)S(1)}, s32[8,4]{1,0:T(8,128)S(1)}, u32[]{:S(2)}, u32[]{:S(2)}) collective-permute-start(s32[8,4]{1,0:T(8,128)S(1)} %broadcast_in_dim.18), channel_id=1, source_target_pairs={{0,2},{2,0},{1,3},{3,1},{4,6},{6,4},{5,7},{7,5},{8,10},{10,8},{9,1... | collective-permute-start | bytes 392 | tf_op jit(solution)/shard_map/ppermute | solution.py:58
  14.7 2.1 %collective-permute-start.20 = (s32[8,128]{1,0:T(8,128)S(1)}, s32[8,128]{1,0:T(8,128)S(1)}, u32[]{:S(2)}, u32[]{:S(2)}) collective-permute-start(s32[8,128]{1,0:T(8,128)S(1)} %broadcast_in_dim.19), channel_id=1, source_target_pairs={{0,16},{16,0},{1,17},{17,1},{2,18},{18,2},{3,19},{19,3},{4,20},{20... | collective-permute-start | bytes 12296 | tf_op jit(solution)/shard_map/ppermute | solution.py:58
  20.3 5.0 %collective-permute-done.21 = bf16[4,32,2048]{2,1,0:T(8,128)(2,1)S(1)} collective-permute-done((bf16[4,32,2048]{2,1,0:T(8,128)(2,1)S(1)}, bf16[4,32,2048]{2,1,0:T(8,128)(2,1)S(1)}, u32[]{:S(2)}, u32[]{:S(2)}) %collective-permute-start.21) | collective-permute-done | bytes 524320 | tf_op jit(solution)/shard_map/ppermute | solution.py:58
  25.9 178.3 %conditional.1 = (bf16[1,4,32,4096]{3,2,1,0:T(8,128)(2,1)}, bf16[128,4096]{1,0:T(8,128)(2,1)}, bf16[128,4096]{1,0:T(8,128)(2,1)}) conditional(s32[]{:T(128)} %convert_element_type.90, (s32[1,4,1]{1,2,0:T(1,128)}, bf16[1,4,32,4096]{3,2,1,0:T(8,128)(2,1)}, bf16[128,4096]{1,0:T(8,128)(2,1)}, bf16[1,4,32,4096]{3,2,1,0:T(8,128)(2,1)}, ...), branch_computations={%region_5.10_spmd, %region_10.11_spmd} | conditional | flops 4081975808 | bytes 174130112 | solution.py:237
  25.9 1.4 dynamic-slice_bitcast_fusion.keep
  27.4 1.4 branch_1_fun.3
  28.8 1.6 collective-permute-start
  30.4 2.6 %collective-permute-start.1 = (bf16[4,32,2048]{2,1,0:T(8,128)(2,1)S(1)}, bf16[4,32,2048]{2,1,0:T(8,128)(2,1)}, u32[]{:S(2)}, u32[]{:S(2)}) collective-permute-start(bf16[4,32,2048]{2,1,0:T(8,128)(2,1)S(1)} %get-tuple-element.38), channel_id=1, source_target_pairs={{0,8},{4,12},{8,0},{12,4},{1,9},{5,13},{9,1},{13,5},{2,10},{6,14},... | collective-permute-start | bytes 1572872 | tf_op jit(solution)/shard_map/cond/branch_1_fun/ppermute | solution.py:192
  33.0 1.3 collective-permute-start.2
  34.4 2.1 dynamic-slice_bitcast_fusion.1
  37.0 2.3 %constant_dynamic-slice_fusion.7 = (bf16[128,2048]{1,0:T(8,128)(2,1)}, bf16[128,2048]{1,0:T(8,128)(2,1)}) fusion(bf16[128,4096]{1,0:T(8,128)(2,1)} %get-tuple-element.40, s32[]{:T(128)S(6)} %select_n.75, s32[]{:T(128)S(6)} %select_n.76), kind=kLoop, calls=%fused_computation.77 | loop fusion | bytes 2097160 | tf_op jit(solution)/shard_map/cond/branch_1_fun/dynamic_slice | solution.py:63
  39.2 1.5 collective-permute-start.3
  41.4 1.3 constant_dynamic-slice_fusion.5
  42.7 8.8 %collective-permute-done.6.got = bf16[4,32,2048]{2,1,0:T(8,128)(2,1)S(1)} collective-permute-done((bf16[4,32,2048]{2,1,0:T(8,128)(2,1)}, bf16[4,32,2048]{2,1,0:T(8,128)(2,1)S(1)}, u32[]{:S(2)}, u32[]{:S(2)}) %collective-permute-start.6) | collective-permute-done | bytes 524320 | tf_op jit(solution)/shard_map/cond/branch_1_fun/ppermute | solution.py:58
  53.0 13.4 %collective-permute-start.7 = (bf16[4,32,2048]{2,1,0:T(8,128)(2,1)S(1)}, bf16[4,32,2048]{2,1,0:T(8,128)(2,1)S(1)}, u32[]{:S(2)}, u32[]{:S(2)}) collective-permute-start(bf16[4,32,2048]{2,1,0:T(8,128)(2,1)S(1)} %get-tuple-element.43), channel_id=1, source_target_pairs={{0,4},{4,8},{8,12},{12,0},{1,5},{5,9},{9,13},{13,1},{2,6},{6,10},{... | collective-permute-start | bytes 1572872 | tf_op jit(solution)/shard_map/cond/branch_1_fun/ppermute | solution.py:192
  66.4 1.8 collective-permute-done.1
  68.9 29.0 %collective-permute-start.9 = (bf16[4,32,2048]{2,1,0:T(8,128)(2,1)S(1)}, bf16[4,32,2048]{2,1,0:T(8,128)(2,1)S(1)}, u32[]{:S(2)}, u32[]{:S(2)}) collective-permute-start(bf16[4,32,2048]{2,1,0:T(8,128)(2,1)S(1)} %get-tuple-element.45), channel_id=1, source_target_pairs={{0,12},{4,0},{8,4},{12,8},{1,13},{5,1},{9,5},{13,9},{2,14},{6,2},{... | collective-permute-start | bytes 1572872 | tf_op jit(solution)/shard_map/cond/branch_1_fun/ppermute | solution.py:192
  97.9 1.7 pad_maximum_fusion.1
  99.6 2.7 %fusion.53 = (bf16[512,256]{1,0:T(8,128)(2,1)S(1)}, f32[512,256]{1,0:T(8,128)S(1)}) fusion(bf16[512,2048]{1,0:T(8,128)(2,1)S(1)} %bitcast.103, bf16[128,2048]{1,0:T(8,128)(2,1)} %collective-permute-done.3, bf16[128,2048]{1,0:T(8,128)(2,1)S(1)} %copy-done.7, pred[]{:T(512)S(6)} %eq.104), kind=kOutput, calls=%fused_computation.99 | convolution fusion | flops 541720576 | bytes 3932161 | tf_op jit(solution)/shard_map/cond/branch_1_fun/dot_general | solution.py:212
  102.4 8.4 %collective-permute-done.8 = bf16[4,32,2048]{2,1,0:T(8,128)(2,1)S(1)} collective-permute-done((bf16[4,32,2048]{2,1,0:T(8,128)(2,1)S(1)}, bf16[4,32,2048]{2,1,0:T(8,128)(2,1)S(1)}, u32[]{:S(2)}, u32[]{:S(2)}) %collective-permute-start.8) | collective-permute-done | bytes 524320 | tf_op jit(solution)/shard_map/cond/branch_1_fun/ppermute | solution.py:192
  110.8 5.4 %collective-permute-done.9 = bf16[4,32,2048]{2,1,0:T(8,128)(2,1)S(1)} collective-permute-done((bf16[4,32,2048]{2,1,0:T(8,128)(2,1)S(1)}, bf16[4,32,2048]{2,1,0:T(8,128)(2,1)S(1)}, u32[]{:S(2)}, u32[]{:S(2)}) %collective-permute-start.9) | collective-permute-done | bytes 524320 | tf_op jit(solution)/shard_map/cond/branch_1_fun/ppermute | solution.py:192
  116.5 1.5 fusion.52
  121.2 1.5 collective-permute-start.12
  122.7 5.5 %collective-permute-done.5 = bf16[512,256]{1,0:T(8,128)(2,1)} collective-permute-done((bf16[512,256]{1,0:T(8,128)(2,1)}, bf16[512,256]{1,0:T(8,128)(2,1)}, u32[]{:S(2)}, u32[]{:S(2)}) %collective-permute-start.5) | collective-permute-done | bytes 262176 | tf_op jit(solution)/shard_map/cond/branch_1_fun/ppermute | solution.py:58
  128.2 1.8 convolution_convert_fusion.4
  130.7 3.0 %collective-permute-done.12 = bf16[512,256]{1,0:T(8,128)(2,1)S(1)} collective-permute-done((bf16[512,256]{1,0:T(8,128)(2,1)S(1)}, bf16[512,256]{1,0:T(8,128)(2,1)S(1)}, u32[]{:S(2)}, u32[]{:S(2)}) %collective-permute-start.12) | collective-permute-done | bytes 262176 | tf_op jit(solution)/shard_map/cond/branch_1_fun/ppermute | solution.py:58
  133.7 1.3 multiply_convert_fusion.6
  135.0 2.0 convolution_convert_fusion.3
  137.2 7.3 %collective-permute-start.13 = (bf16[4,32,2048]{2,1,0:T(8,128)(2,1)S(1)}, bf16[4,32,2048]{2,1,0:T(8,128)(2,1)S(1)}, u32[]{:S(2)}, u32[]{:S(2)}) collective-permute-start(bf16[4,32,2048]{2,1,0:T(8,128)(2,1)S(1)} %bitcast.108), channel_id=1, source_target_pairs={{4,0},{8,4},{12,8},{0,12},{5,1},{9,5},{13,9},{1,13},{6,2},{10,6},{... | collective-permute-start | bytes 1572872 | tf_op jit(solution)/shard_map/cond/branch_1_fun/ppermute | solution.py:222
  146.6 10.4 %collective-permute-done.13.rest_1_ = bf16[4,32,2048]{2,1,0:T(8,128)(2,1)S(1)} collective-permute-done((bf16[4,32,2048]{2,1,0:T(8,128)(2,1)S(1)}, bf16[4,32,2048]{2,1,0:T(8,128)(2,1)S(1)}, u32[]{:S(2)}, u32[]{:S(2)}) %collective-permute-start.13) | collective-permute-done | bytes 524320 | tf_op jit(solution)/shard_map/cond/branch_1_fun/ppermute | solution.py:222
  156.9 32.9 %collective-permute-done.14.rest_2_ = bf16[4,32,2048]{2,1,0:T(8,128)(2,1)S(1)} collective-permute-done((bf16[4,32,2048]{2,1,0:T(8,128)(2,1)S(1)}, bf16[4,32,2048]{2,1,0:T(8,128)(2,1)S(1)}, u32[]{:S(2)}, u32[]{:S(2)}) %collective-permute-start.14) | collective-permute-done | bytes 524320 | tf_op jit(solution)/shard_map/cond/branch_1_fun/ppermute | solution.py:222
  193.7 9.2 %collective-permute-done.16 = bf16[4,32,2048]{2,1,0:T(8,128)(2,1)S(1)} collective-permute-done((bf16[4,32,2048]{2,1,0:T(8,128)(2,1)S(1)}, bf16[4,32,2048]{2,1,0:T(8,128)(2,1)S(1)}, u32[]{:S(2)}, u32[]{:S(2)}) %collective-permute-start.16) | collective-permute-done | bytes 524320 | tf_op jit(solution)/shard_map/cond/branch_1_fun/ppermute | solution.py:58
  (67 shorter events, 22.1 us)
Async XLA Ops:
  7.8 4.5 %collective-permute-start.19 = (s32[8,4]{1,0:T(8,128)S(1)}, s32[8,4]{1,0:T(8,128)S(1)}, u32[]{:S(2)}, u32[]{:S(2)}) collective-permute-start(s32[8,4]{1,0:T(8,128)S(1)} %broadcast_in_dim.18), channel_id=1, source_target_pairs={{0,2},{2,0},{1,3},{3,1},{4,6},{6,4},{5,7},{7,5},{8,10},{10,8},{9,1... | collective-permute-start | bytes 392 | tf_op jit(solution)/shard_map/ppermute | solution.py:58
  11.8 13.4 %collective-permute-start.21 = (bf16[4,32,2048]{2,1,0:T(8,128)(2,1)S(1)}, bf16[4,32,2048]{2,1,0:T(8,128)(2,1)S(1)}, u32[]{:S(2)}, u32[]{:S(2)}) collective-permute-start(bf16[4,32,2048]{2,1,0:T(8,128)(2,1)S(1)} %dynamic-slice_bitcast_fusion.3), channel_id=1, source_target_pairs={{0,2},{2,0},{1,3},{3,1},{4,6},{6,4},{5,7},{7,5},{8,10},{10,8},{9,1... | collective-permute-start | bytes 1572872 | tf_op jit(solution)/shard_map/ppermute | solution.py:58
  14.7 3.7 %collective-permute-start.20 = (s32[8,128]{1,0:T(8,128)S(1)}, s32[8,128]{1,0:T(8,128)S(1)}, u32[]{:S(2)}, u32[]{:S(2)}) collective-permute-start(s32[8,128]{1,0:T(8,128)S(1)} %broadcast_in_dim.19), channel_id=1, source_target_pairs={{0,16},{16,0},{1,17},{17,1},{2,18},{18,2},{3,19},{19,3},{4,20},{20... | collective-permute-start | bytes 12296 | tf_op jit(solution)/shard_map/ppermute | solution.py:58
  25.9 1.5 copy-start.6
  28.8 24.2 %collective-permute-start = (bf16[4,32,2048]{2,1,0:T(8,128)(2,1)S(1)}, bf16[4,32,2048]{2,1,0:T(8,128)(2,1)}, u32[]{:S(2)}, u32[]{:S(2)}) collective-permute-start(bf16[4,32,2048]{2,1,0:T(8,128)(2,1)S(1)} %get-tuple-element.37), channel_id=1, source_target_pairs={{0,4},{4,8},{8,12},{12,0},{1,5},{5,9},{9,13},{13,1},{2,6},{6,10},{... | collective-permute-start | bytes 1572872 | tf_op jit(solution)/shard_map/cond/branch_1_fun/ppermute | solution.py:192
  30.4 37.8 %collective-permute-start.1 = (bf16[4,32,2048]{2,1,0:T(8,128)(2,1)S(1)}, bf16[4,32,2048]{2,1,0:T(8,128)(2,1)}, u32[]{:S(2)}, u32[]{:S(2)}) collective-permute-start(bf16[4,32,2048]{2,1,0:T(8,128)(2,1)S(1)} %get-tuple-element.38), channel_id=1, source_target_pairs={{0,8},{4,12},{8,0},{12,4},{1,9},{5,13},{9,1},{13,5},{2,10},{6,14},... | collective-permute-start | bytes 1572872 | tf_op jit(solution)/shard_map/cond/branch_1_fun/ppermute | solution.py:192
  33.0 35.9 %collective-permute-start.2 = (bf16[4,32,2048]{2,1,0:T(8,128)(2,1)S(1)}, bf16[4,32,2048]{2,1,0:T(8,128)(2,1)}, u32[]{:S(2)}, u32[]{:S(2)}) collective-permute-start(bf16[4,32,2048]{2,1,0:T(8,128)(2,1)S(1)} %get-tuple-element.39), channel_id=1, source_target_pairs={{0,12},{4,0},{8,4},{12,8},{1,13},{5,1},{9,5},{13,9},{2,14},{6,2},{... | collective-permute-start | bytes 1572872 | tf_op jit(solution)/shard_map/cond/branch_1_fun/ppermute | solution.py:192
  34.4 6.4 %copy-start.9 = (s32[4]{0:T(128)S(1)}, s32[4]{0:T(128)}, u32[]{:S(2)}) copy-start(s32[4]{0:T(128)} %get-tuple-element.64) | copy-start | bytes 52 | tf_op jit(solution)/shard_map/cond
  36.4 15.1 %collective-permute-start.6 = (bf16[4,32,2048]{2,1,0:T(8,128)(2,1)}, bf16[4,32,2048]{2,1,0:T(8,128)(2,1)S(1)}, u32[]{:S(2)}, u32[]{:S(2)}) collective-permute-start(bf16[4,32,2048]{2,1,0:T(8,128)(2,1)} %get-tuple-element.133), channel_id=1, source_target_pairs={{0,2},{2,0},{1,3},{3,1},{4,6},{6,4},{5,7},{7,5},{8,10},{10,8},{9,1... | collective-permute-start | bytes 1572872 | tf_op jit(solution)/shard_map/cond/branch_1_fun/ppermute | solution.py:58
  39.2 60.4 %collective-permute-start.3 = (bf16[128,2048]{1,0:T(8,128)(2,1)}, bf16[128,2048]{1,0:T(8,128)(2,1)}, u32[]{:S(2)}, u32[]{:S(2)}) collective-permute-start(bf16[128,2048]{1,0:T(8,128)(2,1)} %get-tuple-element.130), channel_id=1, source_target_pairs={{0,2},{2,0},{1,3},{3,1},{4,6},{6,4},{5,7},{7,5},{8,10},{10,8},{9,1... | collective-permute-start | bytes 1572872 | tf_op jit(solution)/shard_map/cond/branch_1_fun/ppermute | solution.py:58
  51.5 65.0 %collective-permute-start.10 = (bf16[128,2048]{1,0:T(8,128)(2,1)S(1)}, bf16[128,2048]{1,0:T(8,128)(2,1)S(1)}, u32[]{:S(2)}, u32[]{:S(2)}) collective-permute-start(bf16[128,2048]{1,0:T(8,128)(2,1)S(1)} %get-tuple-element.132), channel_id=1, source_target_pairs={{0,2},{2,0},{1,3},{3,1},{4,6},{6,4},{5,7},{7,5},{8,10},{10,8},{9,1... | collective-permute-start | bytes 1572872 | tf_op jit(solution)/shard_map/cond/branch_1_fun/ppermute | solution.py:58
  53.0 49.5 %collective-permute-start.7 = (bf16[4,32,2048]{2,1,0:T(8,128)(2,1)S(1)}, bf16[4,32,2048]{2,1,0:T(8,128)(2,1)S(1)}, u32[]{:S(2)}, u32[]{:S(2)}) collective-permute-start(bf16[4,32,2048]{2,1,0:T(8,128)(2,1)S(1)} %get-tuple-element.43), channel_id=1, source_target_pairs={{0,4},{4,8},{8,12},{12,0},{1,5},{5,9},{9,13},{13,1},{2,6},{6,10},{... | collective-permute-start | bytes 1572872 | tf_op jit(solution)/shard_map/cond/branch_1_fun/ppermute | solution.py:192
  68.2 42.6 %collective-permute-start.8 = (bf16[4,32,2048]{2,1,0:T(8,128)(2,1)S(1)}, bf16[4,32,2048]{2,1,0:T(8,128)(2,1)S(1)}, u32[]{:S(2)}, u32[]{:S(2)}) collective-permute-start(bf16[4,32,2048]{2,1,0:T(8,128)(2,1)S(1)} %get-tuple-element.44), channel_id=1, source_target_pairs={{0,8},{4,12},{8,0},{12,4},{1,9},{5,13},{9,1},{13,5},{2,10},{6,14},... | collective-permute-start | bytes 1572872 | tf_op jit(solution)/shard_map/cond/branch_1_fun/ppermute | solution.py:192
  68.9 47.4 %collective-permute-start.9 = (bf16[4,32,2048]{2,1,0:T(8,128)(2,1)S(1)}, bf16[4,32,2048]{2,1,0:T(8,128)(2,1)S(1)}, u32[]{:S(2)}, u32[]{:S(2)}) collective-permute-start(bf16[4,32,2048]{2,1,0:T(8,128)(2,1)S(1)} %get-tuple-element.45), channel_id=1, source_target_pairs={{0,12},{4,0},{8,4},{12,8},{1,13},{5,1},{9,5},{13,9},{2,14},{6,2},{... | collective-permute-start | bytes 1572872 | tf_op jit(solution)/shard_map/cond/branch_1_fun/ppermute | solution.py:192
  97.9 1.7 copy-start.7
  99.6 2.7 %copy-start.1 = (bf16[16,32,2048]{2,1,0:T(8,128)(2,1)}, bf16[16,32,2048]{2,1,0:T(8,128)(2,1)S(1)}, u32[]{:S(2)}) copy-start(bf16[16,32,2048]{2,1,0:T(8,128)(2,1)S(1)} %pad_maximum_fusion.1) | copy-start | bytes 6291460 | tf_op jit(solution)/shard_map/cond
  102.3 15.7 %collective-permute-start.4 = (bf16[512,256]{1,0:T(8,128)(2,1)S(1)}, bf16[512,256]{1,0:T(8,128)(2,1)S(1)}, u32[]{:S(2)}, u32[]{:S(2)}) collective-permute-start(bf16[512,256]{1,0:T(8,128)(2,1)S(1)} %get-tuple-element.137), channel_id=1, source_target_pairs={{0,1},{1,0},{2,3},{3,2},{4,5},{5,4},{6,7},{7,6},{8,9},{9,8},{10,11... | collective-permute-start | bytes 786440 | tf_op jit(solution)/shard_map/cond/branch_1_fun/ppermute | solution.py:58
  118.0 2.1 %collective-permute-start.11 = (bf16[512,256]{1,0:T(8,128)(2,1)}, bf16[512,256]{1,0:T(8,128)(2,1)}, u32[]{:S(2)}, u32[]{:S(2)}) collective-permute-start(bf16[512,256]{1,0:T(8,128)(2,1)} %get-tuple-element.135), channel_id=1, source_target_pairs={{0,1},{1,0},{2,3},{3,2},{4,5},{5,4},{6,7},{7,6},{8,9},{9,8},{10,11... | collective-permute-start | bytes 786440 | tf_op jit(solution)/shard_map/cond/branch_1_fun/ppermute | solution.py:58
  118.8 9.4 %collective-permute-start.5 = (bf16[512,256]{1,0:T(8,128)(2,1)}, bf16[512,256]{1,0:T(8,128)(2,1)}, u32[]{:S(2)}, u32[]{:S(2)}) collective-permute-start(bf16[512,256]{1,0:T(8,128)(2,1)} %fusion.41), channel_id=1, source_target_pairs={{0,2},{2,0},{1,3},{3,1},{4,6},{6,4},{5,7},{7,5},{8,10},{10,8},{9,1... | collective-permute-start | bytes 786440 | tf_op jit(solution)/shard_map/cond/branch_1_fun/ppermute | solution.py:58
  121.2 12.5 %collective-permute-start.12 = (bf16[512,256]{1,0:T(8,128)(2,1)S(1)}, bf16[512,256]{1,0:T(8,128)(2,1)S(1)}, u32[]{:S(2)}, u32[]{:S(2)}) collective-permute-start(bf16[512,256]{1,0:T(8,128)(2,1)S(1)} %fusion.42), channel_id=1, source_target_pairs={{0,2},{2,0},{1,3},{3,1},{4,6},{6,4},{5,7},{7,5},{8,10},{10,8},{9,1... | collective-permute-start | bytes 786440 | tf_op jit(solution)/shard_map/cond/branch_1_fun/ppermute | solution.py:58
  130.0 5.0 %copy-start.8 = (bf16[128,2048]{1,0:T(8,128)(2,1)S(1)}, bf16[128,2048]{1,0:T(8,128)(2,1)}, u32[]{:S(2)}) copy-start(bf16[128,2048]{1,0:T(8,128)(2,1)} %get-tuple-element.129) | copy-start | bytes 1572868 | tf_op jit(solution)/shard_map/cond
  130.1 61.2 %collective-permute-start.18 = (bf16[128,2048]{1,0:T(8,128)(2,1)S(1)}, bf16[128,2048]{1,0:T(8,128)(2,1)S(1)}, u32[]{:S(2)}, u32[]{:S(2)}) collective-permute-start(bf16[128,2048]{1,0:T(8,128)(2,1)S(1)} %get-tuple-element.126), channel_id=1, source_target_pairs={{0,2},{2,0},{1,3},{3,1},{4,6},{6,4},{5,7},{7,5},{8,10},{10,8},{9,1... | collective-permute-start | bytes 1572872 | tf_op jit(solution)/shard_map/cond/branch_1_fun/ppermute | solution.py:58
  137.0 8.1 %copy-start.2 = (bf16[16,32,2048]{2,1,0:T(8,128)(2,1)S(1)}, bf16[16,32,2048]{2,1,0:T(8,128)(2,1)}, u32[]{:S(2)}) copy-start(bf16[16,32,2048]{2,1,0:T(8,128)(2,1)} %copy-done.1) | copy-start | bytes 6291460 | tf_op jit(solution)/shard_map/cond
  137.2 19.7 %collective-permute-start.13 = (bf16[4,32,2048]{2,1,0:T(8,128)(2,1)S(1)}, bf16[4,32,2048]{2,1,0:T(8,128)(2,1)S(1)}, u32[]{:S(2)}, u32[]{:S(2)}) collective-permute-start(bf16[4,32,2048]{2,1,0:T(8,128)(2,1)S(1)} %bitcast.108), channel_id=1, source_target_pairs={{4,0},{8,4},{12,8},{0,12},{5,1},{9,5},{13,9},{1,13},{6,2},{10,6},{... | collective-permute-start | bytes 1572872 | tf_op jit(solution)/shard_map/cond/branch_1_fun/ppermute | solution.py:222
  144.5 45.3 %collective-permute-start.14 = (bf16[4,32,2048]{2,1,0:T(8,128)(2,1)S(1)}, bf16[4,32,2048]{2,1,0:T(8,128)(2,1)S(1)}, u32[]{:S(2)}, u32[]{:S(2)}) collective-permute-start(bf16[4,32,2048]{2,1,0:T(8,128)(2,1)S(1)} %bitcast.107), channel_id=1, source_target_pairs={{8,0},{12,4},{0,8},{4,12},{9,1},{13,5},{1,9},{5,13},{10,2},{14,6},... | collective-permute-start | bytes 1572872 | tf_op jit(solution)/shard_map/cond/branch_1_fun/ppermute | solution.py:222
  145.0 44.8 %collective-permute-start.15 = (bf16[4,32,2048]{2,1,0:T(8,128)(2,1)S(1)}, bf16[4,32,2048]{2,1,0:T(8,128)(2,1)S(1)}, u32[]{:S(2)}, u32[]{:S(2)}) collective-permute-start(bf16[4,32,2048]{2,1,0:T(8,128)(2,1)S(1)} %bitcast.106), channel_id=1, source_target_pairs={{12,0},{0,4},{4,8},{8,12},{13,1},{1,5},{5,9},{9,13},{14,2},{2,6},{... | collective-permute-start | bytes 1572872 | tf_op jit(solution)/shard_map/cond/branch_1_fun/ppermute | solution.py:222
  146.0 46.5 %collective-permute-start.17 = (bf16[128,2048]{1,0:T(8,128)(2,1)S(1)}, bf16[128,2048]{1,0:T(8,128)(2,1)S(1)}, u32[]{:S(2)}, u32[]{:S(2)}) collective-permute-start(bf16[128,2048]{1,0:T(8,128)(2,1)S(1)} %get-tuple-element.128), channel_id=1, source_target_pairs={{0,2},{2,0},{1,3},{3,1},{4,6},{6,4},{5,7},{7,5},{8,10},{10,8},{9,1... | collective-permute-start | bytes 1572872 | tf_op jit(solution)/shard_map/cond/branch_1_fun/ppermute | solution.py:58
  190.7 12.3 %collective-permute-start.16 = (bf16[4,32,2048]{2,1,0:T(8,128)(2,1)S(1)}, bf16[4,32,2048]{2,1,0:T(8,128)(2,1)S(1)}, u32[]{:S(2)}, u32[]{:S(2)}) collective-permute-start(bf16[4,32,2048]{2,1,0:T(8,128)(2,1)S(1)} %get-tuple-element.48), channel_id=1, source_target_pairs={{0,2},{2,0},{1,3},{3,1},{4,6},{6,4},{5,7},{7,5},{8,10},{10,8},{9,1... | collective-permute-start | bytes 1572872 | tf_op jit(solution)/shard_map/cond/branch_1_fun/ppermute | solution.py:58

commit v2 on v0

v2 whole, which is shorter than its diff:
```python
import functools

import jax
import jax.numpy as jnp
from jax import lax
from jax.experimental import pallas as pl
from jax.experimental.pallas import tpu as pltpu
from jax.sharding import PartitionSpec as P

MOST = 3
EVEN = 2
EXTRA = 2
BY_SLOT = 6
SLOTS = 2 * MOST
F32 = jnp.float32
BF16 = jnp.bfloat16


def swap(x, axis):
    return lax.ppermute(x, axis, [(0, 1), (1, 0)])


def ordered(mine, other, side, axis):
    return jnp.where(
        side == 0,
        jnp.concatenate([mine, other], axis),
        jnp.concatenate([other, mine], axis),
    )


def all_rows(w):
    if lax.axis_size("dp") != 2:
        return lax.all_gather(w, "dp", axis=0, tiled=True)
    return ordered(w, swap(w, "dp"), lax.axis_index("dp"), 0)


def sub_total(part):
    if lax.axis_size("sub") != 2:
        return lax.psum(part.astype(BF16), "sub").astype(F32)
    rounded = part.astype(BF16)
    return rounded.astype(F32) + swap(rounded, "sub").astype(F32)


def replica_total(part):
    if lax.axis_size("dp") != 2:
        return lax.psum_scatter(part.astype(BF16), "dp", scatter_dimension=0, tiled=True)
    side = lax.axis_index("dp")
    n = part.shape[0] // 2
    rounded = part.astype(BF16)
    keep = lax.dynamic_slice_in_dim(rounded, side * n, n, 0)
    pass_on = lax.dynamic_slice_in_dim(rounded, (1 - side) * n, n, 0)
    return (keep.astype(F32) + swap(pass_on, "dp").astype(F32)).astype(BF16)


def plain(tokens, cotangent, w_up, w_down, active):
    tile_count = tokens.shape[1]
    part_rows = tokens.shape[2]
    half_width = tokens.shape[3]
    owners = lax.axis_size("tensor")
    block_ids = active[0]
    owner_list = jnp.arange(owners, dtype=jnp.int32)
    listed = jnp.any(block_ids[:, :, None] == owner_list[None, None, :], axis=1).astype(jnp.int32)
    ranking = jnp.cumsum(listed, axis=0) - 1
    slot_ids = jnp.arange(MOST, dtype=jnp.int32)
    choose = (listed.T[:, None, :] == 1) & (ranking.T[:, None, :] == slot_ids[None, :, None])
    choose_half = choose.astype(BF16)
    choose_full = choose.astype(F32)
    send_tok = jnp.einsum("omt,trd->omrd", choose_half, tokens[0], preferred_element_type=F32).astype(BF16)
    send_cot = jnp.einsum("omt,trd->omrd", choose_half, cotangent[0], preferred_element_type=F32).astype(BF16)
    up_weight_block = all_rows(w_up)
    down_weight_block = all_rows(w_down)
    slot_token = lax.all_to_all(send_tok, "tensor", split_axis=0, concat_axis=2, tiled=True)[0]
    slot_cotangent = lax.all_to_all(send_cot, "tensor", split_axis=0, concat_axis=2, tiled=True)[0]
    hidden = sub_total(jnp.einsum("bkn,vn->bkv", slot_token, up_weight_block, preferred_element_type=F32))
    grad_act = sub_total(jnp.einsum("bkn,vn->bkv", slot_cotangent, down_weight_block, preferred_element_type=F32))
    positive = jnp.maximum(hidden, 0.0)
    squared_activation = (positive * positive).astype(BF16)
    hidden_gradient = (2.0 * positive * grad_act).astype(BF16)
    back_rows = jnp.einsum("opl,la->opa", hidden_gradient, up_weight_block, preferred_element_type=F32).astype(BF16)
    back_rows = back_rows.reshape(MOST, owners, part_rows, half_width)
    received = lax.all_to_all(back_rows, "tensor", split_axis=1, concat_axis=1, tiled=True)
    summed = jnp.einsum("omt,mord->trd", choose_full, received.astype(F32), precision=lax.Precision.HIGHEST)
    grad_tokens = summed.astype(BF16).reshape(1, tile_count, part_rows, half_width)
    up_weight_term = jnp.einsum("epn,epk->nk", hidden_gradient, slot_token, preferred_element_type=F32)
    down_weight_term = jnp.einsum("epn,epk->nk", squared_activation, slot_cotangent, preferred_element_type=F32)
    return grad_tokens, replica_total(up_weight_term), replica_total(down_weight_term)


def after(x, *first):
    return lax.optimization_barrier((x, first))[0]


def halves(x, side):
    width = x.shape[-1] // 2
    keep = lax.dynamic_slice_in_dim(x, side * width, width, x.ndim - 1)
    pass_on = lax.dynamic_slice_in_dim(x, (1 - side) * width, width, x.ndim - 1)
    return keep, pass_on


def copy_rows(src, at, dst, to, start=0):
    step = 512

    @pl.loop(0, dst.shape[-1] // step)
    def _(i):
        cols = pl.ds(pl.multiple_of(i * step, step), step)
        dst[to, :, cols] = src[at, :, pl.ds(pl.multiple_of(start + i * step, step), step)]


def plan_kernel(owners, tiles, mine, other, out):
    side, place = lax.axis_index("dp"), lax.axis_index("tensor")
    block = [jnp.where(side == i // tiles, mine[i % tiles], other[i % tiles]) for i in range(2 * tiles)]
    low = [sum((b == o).astype(jnp.int32) for b in block[:tiles]) for o in range(owners)]
    high = [sum((b == o).astype(jnp.int32) for b in block[tiles:]) for o in range(owners)]
    crowded, most = jnp.int32(0), low[0] + high[0]
    for o in range(1, owners):
        more = low[o] + high[o] > most
        crowded, most = jnp.where(more, o, crowded), jnp.where(more, low[o] + high[o], most)
    fits, mine_count, mine_first, first = most <= EVEN + EXTRA, 0, 0, []
    for o in range(owners):
        count = low[o] + high[o]
        fits = fits & ((o == crowded) | (count <= 1) | ((low[o] == 1) & (high[o] == 1)))
        last = jnp.where(o == crowded, EVEN + EXTRA, EVEN) - 1
        local = jnp.where(side == 0, low[o], high[o])
        first.append(jnp.minimum(jnp.where(local > 0, jnp.where(side == 0, 0, low[o]), last), last))
        mine_count = jnp.where(place == o, count, mine_count)
        mine_first = jnp.where(place == o, first[o], mine_first)
    head = (side, place, crowded, mine_count, mine_first, jnp.where(fits, crowded, owners))
    for i, value in enumerate(head):
        out[i] = value
    by_position, by_tile = BY_SLOT + owners * SLOTS, BY_SLOT + 2 * owners * SLOTS
    for i in range(BY_SLOT, by_tile):
        out[i] = 0
    for i, b in enumerate(block):
        slot = jnp.minimum(sum([(b == c).astype(jnp.int32) for c in block[:i]], jnp.int32(0)), SLOTS - 1)
        start = sum(jnp.where(b == o, first[o], 0) for o in range(owners))
        position = jnp.where(slot == start, 0, jnp.where(slot < start, slot + 1, slot))
        out[BY_SLOT + b * SLOTS + slot] = i
        out[by_position + b * SLOTS + position] = i
        out[by_tile + i] = b
        out[by_tile + 2 * tiles + i] = slot


def plan(mine, other, owners, tiles):
    smem = pl.BlockSpec(memory_space=pltpu.SMEM)
    return pl.pallas_call(
        functools.partial(plan_kernel, owners, tiles),
        out_shape=jax.ShapeDtypeStruct((BY_SLOT + 2 * owners * SLOTS + 4 * tiles,), jnp.int32),
        in_specs=[smem, smem],
        out_specs=smem,
    )(mine, other)


def call(kernel, out_shape, n_vmem, scratch=(), flops=0, moved=0):
    vmem = pl.BlockSpec(memory_space=pltpu.VMEM)
    return pl.pallas_call(
        kernel,
        out_shape=out_shape,
        in_specs=[pl.BlockSpec(memory_space=pltpu.SMEM)] + [vmem] * n_vmem,
        out_specs=[vmem] * len(out_shape),
        scratch_shapes=list(scratch),
        compiler_params=pltpu.CompilerParams(vmem_limit_bytes=40 << 20),
        cost_estimate=pl.CostEstimate(flops=flops, bytes_accessed=moved, transcendentals=0),
    )


def dispatch_kernel(owners, tiles, base, groups, meta, keep, got, *outs):
    side, place, crowded = meta[0], meta[1], meta[2]
    n = 0
    for first, count, each in groups:
        for k in range(owners if each else 1):
            owner = lax.rem(place + k, owners) if each else crowded
            out = outs[n]

            @pl.loop(0, count)
            def _(s):
                tile = meta[base + owner * SLOTS + first + s]
                own = lax.div(tile, tiles) == side
                at = lax.rem(tile, tiles)

                @pl.when(own)
                def _():
                    copy_rows(keep, at, out, s, side * out.shape[2])

                @pl.when(jnp.logical_not(own))
                def _():
                    copy_rows(got, at, out, s)

            n += 1


def dispatch(meta, keep, got, owners, base, groups):
    tiles, rows, width = got.shape
    counts = [count for _, count, each in groups for _ in range(owners if each else 1)]
    outs = [jax.ShapeDtypeStruct((c, rows, width), got.dtype) for c in counts]
    kernel = functools.partial(dispatch_kernel, owners, tiles, base, groups)
    return call(kernel, outs, 2, moved=4 * sum(counts) * rows * width)(meta, keep, got)


def first_kernel(owners, tiles, listed, keep, *outs):
    side, place = lax.axis_index("dp"), lax.axis_index("tensor")
    for k in range(owners):
        owner = lax.rem(place + k, owners)
        at = jnp.int32(0)
        for t in reversed(range(tiles)):
            at = jnp.where(listed[t] == owner, t, at)
        copy_rows(keep, at, outs[k], 0, side * outs[k].shape[2])


def rows_of(pieces, counts, owners, cols):
    parts, n = [], 0
    for count in counts:
        for s in range(count):
            parts += [pieces[n + k][s, :, cols] for k in range(owners)]
        n += owners
    return jnp.concatenate(parts, 0)


def product_kernel(counts, owners, moved, meta, *rest):
    pieces, weight, out, total = rest[:-3], rest[-3], rest[-2], rest[-1]
    step = 512
    total[...] = jnp.zeros_like(total)

    @pl.loop(0, weight.shape[1] // step)
    def _(i):
        cols = pl.ds(pl.multiple_of(i * step, step), step)
        total[...] += lax.dot_general(
            rows_of(pieces, counts, owners, cols),
            weight[:, cols],
            (((1,), (1,)), ((), ())),
            preferred_element_type=F32,
        )

    n = out.shape[1]
    for p in range(sum(counts)):
        out[slot_at(meta[4], p) if moved else p] = total[p * n : (p + 1) * n].astype(BF16)


def slot_at(first, p):
    return first if p == 0 else jnp.where(p <= first, p - 1, p)


def product(meta, groups, weight, moved):
    owners = len(groups[0])
    counts = [g[0].shape[0] for g in groups]
    pieces = [p for g in groups for p in g]
    n, m, rows = sum(counts), weight.shape[0], pieces[0].shape[1] * owners
    return call(
        functools.partial(product_kernel, counts, owners, moved),
        [jax.ShapeDtypeStruct((n, rows, m), BF16)],
        len(pieces) + 1,
        [pltpu.VMEM((n * rows, m), F32)],
        flops=2 * n * rows * m * weight.shape[1],
        moved=2 * (n * rows + m) * weight.shape[1],
    )(meta, *pieces, weight)[0]


def squared_kernel(meta, h1, h2, positive, squared):
    for s in range(h1.shape[0]):
        h = jnp.maximum(h1[s].astype(F32) + h2[s].astype(F32), 0.0)
        h = jnp.where(s < meta[3], h, 0.0)
        positive[s] = h
        squared[s] = (h * h).astype(BF16)


def back_kernel(first, count, owners, meta, positive, g1, g2, up, grad_hidden, *outs):
    n, m = g1.shape[1], g1.shape[2]
    rows = n // owners
    for s in range(count):
        grad_act = g1[s].astype(F32) + g2[s].astype(F32)
        grad_hidden[s] = (2.0 * positive[first + s] * grad_act).astype(BF16)
    step = 512

    @pl.loop(0, up.shape[1] // step)
    def _(i):
        cols = pl.ds(pl.multiple_of(i * step, step), step)
        out = jnp.dot(
            grad_hidden[...].reshape(count * n, m), up[:, cols], preferred_element_type=F32
        ).astype(BF16)
        for s in range(count):
            for k in range(owners):
                at = s * n + k * rows
                outs[k][s, :, cols] = out[at : at + rows]


def back(meta, positive, g, up, first, owners):
    count, n, m = g[0].shape
    width = up.shape[1]
    outs = call(
        functools.partial(back_kernel, first, count, owners),
        [jax.ShapeDtypeStruct((count, n, m), BF16)]
        + [jax.ShapeDtypeStruct((count, n // owners, width), BF16)] * owners,
        4,
        flops=2 * count * n * m * width,
        moved=2 * (count * n + m) * width,
    )(meta, positive, *g, up)
    return outs[0], list(outs[1:])


def weights_kernel(owners, act_counts, counts, moved, meta, *rest):
    acts, data, rest = rest[: len(act_counts)], rest[len(act_counts) : -4], rest[-4:]
    keep, pass_on, by_slot, turned = rest
    side = meta[0]
    n, m = acts[0].shape[1], acts[0].shape[2]
    p = 0
    for act, count in zip(acts, act_counts):
        by_slot[p : p + count] = act[...]
        p += count
    for p in range(sum(counts)):
        turned[:, p * n : (p + 1) * n] = by_slot[slot_at(meta[4], p) if moved else p].T
    step = 256

    @pl.loop(0, keep.shape[1] // step)
    def _(i):
        cols = pl.ds(pl.multiple_of(i * step, step), step)
        g = jnp.dot(turned[...], rows_of(data, counts, owners, cols), preferred_element_type=F32)
        low, high = g[: m // 2].astype(BF16), g[m // 2 :].astype(BF16)
        keep[:, cols] = jnp.where(side == 0, low, high)
        pass_on[:, cols] = jnp.where(side == 0, high, low)


def weights(meta, acts, groups, moved):
    owners = len(groups[0])
    act_counts, counts = [a.shape[0] for a in acts], [g[0].shape[0] for g in groups]
    data = [p for g in groups for p in g]
    _, n, m = acts[0].shape
    slots, width = sum(counts), data[0].shape[2]
    return call(
        functools.partial(weights_kernel, owners, act_counts, counts, moved),
        [jax.ShapeDtypeStruct((m // 2, width), BF16)] * 2,
        len(acts) + len(data),
        [pltpu.VMEM((slots, n, m), BF16), pltpu.VMEM((m, slots * n), BF16)],
        flops=2 * slots * n * m * width,
        moved=2 * (slots * n + m) * width,
    )(meta, *acts, *data)


def collect_kernel(owners, tiles, base, meta, *rest):
    pieces, (mine, other) = rest[:-2], rest[-2:]
    side, place = meta[0], meta[1]
    even = pieces[0].shape[0]
    for r, out in enumerate((mine, other)):
        replica = side if r == 0 else 1 - side

        @pl.loop(0, tiles)
        def _(t):
            tile = replica * tiles + t
            k = lax.rem(meta[base + tile] - place + owners, owners)
            slot = meta[base + 2 * tiles + tile]
            for kk in range(owners):

                @pl.when((k == kk) & (slot < even))
                def _():
                    copy_rows(pieces[kk], slot, out, t)

                if len(pieces) > owners:

                    @pl.when((k == kk) & (slot >= even))
                    def _():
                        copy_rows(pieces[owners + kk], slot - even, out, t)


def collect(meta, pieces, tiles, owners, base):
    _, rows, width = pieces[0].shape
    kernel = functools.partial(collect_kernel, owners, tiles, base)
    outs = [jax.ShapeDtypeStruct((tiles, rows, width), BF16)] * 2
    return call(kernel, outs, len(pieces), moved=8 * tiles * rows * width)(meta, *pieces)


def shards(tokens, cotangent, w_up, w_down, active):
    owners = lax.axis_size("tensor")
    replicas = lax.axis_size("dp")
    subs = lax.axis_size("sub")
    if replicas != 2 or subs != 2 or active.shape[2] != 1 or tokens.shape[2] % 16:
        return plain(tokens, cotangent, w_up, w_down, active)
    tiles = tokens.shape[1]
    rows = tokens.shape[2]
    side = lax.axis_index("dp")
    place = lax.axis_index("tensor")
    def forth(k):
        return [(i, (i + k) % owners) for i in range(owners)]

    def back_of(pairs):
        return [(b, a) for a, b in pairs]

    def move(pieces, perm_of):
        return [pieces[0]] + [lax.ppermute(pieces[k], "tensor", perm_of(k)) for k in range(1, owners)]

    def other_half(x):
        width = x.shape[-1] // 2
        return lax.dynamic_slice_in_dim(x, (1 - side) * width, width, x.ndim - 1)

    tok_pass = other_half(tokens[0])
    listed_other = swap(after(active, tok_pass), "dp").reshape(tiles)
    tok_got = swap(tok_pass, "dp")
    listed = active.reshape(tiles)
    one = jax.ShapeDtypeStruct((1,) + tok_pass.shape[1:], BF16)
    first = functools.partial(first_kernel, owners, tiles)
    tok_first = move(call(first, [one] * owners, 1, moved=2 * tok_pass.size)(listed, tokens[0]), forth)
    meta = plan(listed, listed_other, owners, tiles)
    by_slot = BY_SLOT
    by_position = by_slot + owners * SLOTS
    by_tile = by_position + owners * SLOTS
    cot_pass = other_half(cotangent[0])
    up_keep, up_pass = halves(w_up, side)
    down_keep, down_pass = halves(w_down, side)
    extra_group = (EVEN, EXTRA, False)
    tok_sent = dispatch(meta, tokens[0], tok_got, owners, by_position, ((1, EVEN - 1, True), extra_group))

    def run(center=None):
        fast = center is not None

        def extra_forth(k):
            return [((center - k) % owners, center)]

        def over_subs(part):
            return (part.astype(F32) + swap(part, "sub").astype(F32)).astype(BF16)

        cot_got = swap(cot_pass, "dp")
        if fast:
            tok = [tok_first, move(tok_sent[:owners], forth), move([tok_sent[owners]] * owners, extra_forth)]
            cot_groups = ((0, EVEN, True), extra_group)
            cot_sent = dispatch(meta, cotangent[0], cot_got, owners, by_slot, cot_groups)
            cot = [move(cot_sent[:owners], forth), move([cot_sent[owners]] * owners, extra_forth)]
        else:
            cot_groups = ((0, SLOTS, True),)
            tok, cot = [
                [move(dispatch(meta, keep, got, owners, by_slot, cot_groups), forth)]
                for keep, got in ((tokens[0], tok_got), (cotangent[0], cot_got))
            ]
        up = ordered(up_keep, swap(up_pass, "dp"), side, 0)
        down = ordered(down_keep, swap(down_pass, "dp"), side, 0)
        hidden = over_subs(product(meta, tok, up, fast))
        shape = hidden.shape
        positive, squared = call(
            squared_kernel,
            [jax.ShapeDtypeStruct(shape, F32), jax.ShapeDtypeStruct(shape, BF16)],
            2,
            moved=8 * hidden.size,
        )(meta, hidden, swap(hidden, "dp"))
        grad_hidden, home = [None] * len(cot), [None] * len(cot)
        for i in reversed(range(len(cot))):
            first, _, each = cot_groups[i]
            grad_act = over_subs(product(meta, [cot[i]], down, False))
            sums = (grad_act, swap(grad_act, "dp"))
            grad_hidden[i], out = back(meta, positive, sums, up, first, owners)
            perm_of = forth if each else extra_forth
            home[i] = move(out, lambda k: back_of(perm_of(k)))
            down = after(down, grad_hidden[i])
        down_grad, down_other = weights(meta, [squared], cot, False)
        down_got = swap(after(down_other, sums[1]), "dp")
        up_grad, up_other = weights(meta, grad_hidden, tok, fast)
        up_got = swap(up_other, "dp")
        home = [piece for group in home for piece in group]
        mine, other = collect(meta, home, tiles, owners, by_tile)
        return (
            ordered(mine, swap(other, "dp"), side, 2)[None],
            ordered(up_grad, up_got, side, 1),
            ordered(down_grad, down_got, side, 1),
        )

    return lax.switch(
        meta[5],
        [functools.partial(run, center) for center in range(owners)] + [run],
    )


def solution(mesh):
    placed = (
        P(("groups", "dp"), None, "tensor", "sub"),
        P(("groups", "dp"), None, "tensor", "sub"),
        P(("tensor", "dp"), "sub"),
        P(("tensor", "dp"), "sub"),
        P(("groups", "dp"), None, None),
    )
    return jax.shard_map(
        shards,
        mesh=mesh,
        in_specs=placed,
        out_specs=(
            P(("groups", "dp"), None, "tensor", "sub"),
            P(("groups", "tensor", "dp"), "sub"),
            P(("groups", "tensor", "dp"), "sub"),
        ),
        check_vma=False,
    )
```

time: 300 us -> 158 us (0.53)
  waiting for transfers between devices: 150 us -> 55.4 us
  blocking collectives: 75.8 us -> 0 us
  starting transfers between devices: 11.3 us -> 63.9 us
  matrix products: 25.8 us -> 0 us
  Pallas kernels: 0 us -> 21.4 us
  local copies, waits for them, and re-layouts: 19.1 us -> 5.93 us
  between operations: 13.8 us -> 1.35 us
  other arithmetic: 3.88 us -> 6.94 us
    all_to_all x2 -> x0, waiting for transfers between devices: 131 us -> none  [the longest x1 66.8 us: shards(): lax.all_to_all(send_cot, 'tensor', split_axis=0, concat_axis=2, tiled=True)]
    all_to_all x1 -> x0, blocking collectives: 75.8 us -> none  [shards(): lax.all_to_all(back_rows, 'tensor', split_axis=1, concat_axis=1, tiled=True)]
    ppermute x0 -> x35, starting transfers between devices: none -> 63.9 us  [the longest x21 49.3 us: move(): lax.ppermute(pieces[k], 'tensor', perm_of(k))]
    ppermute x0 -> x35, waiting for transfers between devices: none -> 55.4 us  [the longest x14 28.8 us: swap(): return lax.ppermute(x, axis, [(0, 1), (1, 0)])]
    dot_general x8 -> x0, matrix products: 25.8 us -> none  [the longest x1 5.88 us: shards(): jnp.einsum('omt,mord->trd', choose_full, received.astype(jnp.float32), pr...]
    pallas_call x0 -> x13, Pallas kernels: none -> 21.4 us  [the longest x2 5.21 us: weights(): call(functools.partial(weights_kernel, owners, act_counts, counts, moved)...]
    psum x1 -> x0, waiting for transfers between devices: 17.6 us -> none  [shards(): lax.psum(partial_grad.astype(jnp.bfloat16), 'sub').astype(jnp.float32)]
    all_to_all x2 -> x0, starting transfers between devices: 11 us -> none  [the longest x1 6.32 us: shards(): lax.all_to_all(send_tok, 'tensor', split_axis=0, concat_axis=2, tiled=True)]
  transfers between devices with their start and end apart: 6 -> 35, of which waited for: 3 -> 12; matrix products, arithmetic and copies ran while one was open for 8% -> 6% of each run, Pallas kernels for 0% -> 13%
where the time goes in v2:
time: 158 us; the launch traced here: 156 us
  starting transfers between devices  63.9 us (40%)
  waiting for transfers between devices  55.4 us (35%)
  Pallas kernels  21.4 us (14%)
  other arithmetic  6.94 us (4%)
  local copies, waits for them, and re-layouts  5.93 us (4%)
    ppermute x21, starting transfers between devices, move(): lax.ppermute(pieces[k], 'tensor', perm_of(k))  49.3 us
    ppermute x14, waiting for transfers between devices, swap(): return lax.ppermute(x, axis, [(0, 1), (1, 0)])  28.8 us
    ppermute x21, waiting for transfers between devices, move(): lax.ppermute(pieces[k], 'tensor', perm_of(k))  26.5 us
    ppermute x14, starting transfers between devices, swap(): return lax.ppermute(x, axis, [(0, 1), (1, 0)])  14.7 us
    select_n x5, other arithmetic, ordered(): jnp.where(side == 0, jnp.concatenate([mine, other], axis), jnp.concatenat...  6.81 us
    pallas_call x2, Pallas kernels, weights(): call(functools.partial(weights_kernel, owners, act_counts, counts, moved)...  5.21 us
    pallas_call x3, Pallas kernels, product(): call(functools.partial(product_kernel, counts, owners, moved), [jax.Shape...  5.18 us
    pallas_call x2, Pallas kernels, dispatch(): call(kernel, outs, 2, moved=4 * sum(counts) * rows * width)(meta, keep, got)  3.31 us
  transfers between devices with their start and end apart: 35, of which 12 were waited for; matrix products, arithmetic and copies ran while one was open for 6% of the time, Pallas kernels for 13%

profile of v2, /device:TPU:0, one launch (start us, length us, event | category | flops | bytes accessed | tf_op | source)
XLA Modules:
  0.0 155.6 jit_solution(11086554084255224982)
XLA Ops:
  1.7 3.0 %collective-permute-start.140 = (bf16[4,32,2048]{2,1,0:T(8,128)(2,1)S(1)}, bf16[4,32,2048]{2,1,0:T(8,128)(2,1)S(1)}, u32[]{:S(2)}, u32[]{:S(2)}) collective-permute-start(bf16[4,32,2048]{2,1,0:T(8,128)(2,1)S(1)} %dynamic-slice_bitcast_fusion.1), channel_id=1, source_target_pairs={{0,2},{2,0},{1,3},{3,1},{4,6},{6,4},{5,7},{7,5},{8,10},{10,8},{9,1... | collective-permute-start | bytes 1572872 | tf_op jit(solution)/shard_map/ppermute | solution.py:20
  6.2 2.1 %collective-permute-start.141 = (bf16[1,32,2048]{2,1,0:T(8,128)(2,1)S(1)}, bf16[1,32,2048]{2,1,0:T(8,128)(2,1)}, u32[]{:S(2)}, u32[]{:S(2)}) collective-permute-start(bf16[1,32,2048]{2,1,0:T(8,128)(2,1)S(1)} %get-tuple-element.375), channel_id=1, source_target_pairs={{0,4},{4,8},{8,12},{12,0},{1,5},{5,9},{9,13},{13,1},{2,6},{6,10},{... | collective-permute-start | bytes 393224 | tf_op jit(solution)/shard_map/ppermute | solution.py:386
  8.3 2.6 %collective-permute-start.142 = (bf16[1,32,2048]{2,1,0:T(8,128)(2,1)S(1)}, bf16[1,32,2048]{2,1,0:T(8,128)(2,1)}, u32[]{:S(2)}, u32[]{:S(2)}) collective-permute-start(bf16[1,32,2048]{2,1,0:T(8,128)(2,1)S(1)} %get-tuple-element.376), channel_id=1, source_target_pairs={{0,8},{4,12},{8,0},{12,4},{1,9},{5,13},{9,1},{13,5},{2,10},{6,14},... | collective-permute-start | bytes 393224 | tf_op jit(solution)/shard_map/ppermute | solution.py:386
  12.2 2.9 %constant_dynamic-slice_fusion = (bf16[128,2048]{1,0:T(8,128)(2,1)S(1)}, bf16[128,2048]{1,0:T(8,128)(2,1)}, bf16[128,2048]{1,0:T(8,128)(2,1)}, bf16[128,2048]{1,0:T(8,128)(2,1)}) fusion(bf16[128,4096]{1,0:T(8,128)(2,1)} %param.13, s32[]{:T(128)S(6)} %select_n.182, s32[]{:T(128)S(6)} %select_n.181, bf16[128,4096]{1,0:T(8,128)(2,1)} %param.12), kind=kLoop, calls=%fused_computation.41 | loop fusion | bytes 4194312 | tf_op jit(solution)/shard_map/dynamic_slice | solution.py:95
  20.0 2.3 %shard_map.92 = (bf16[1,32,2048]{2,1,0:T(8,128)(2,1)}, bf16[1,32,2048]{2,1,0:T(8,128)(2,1)S(1)}, bf16[1,32,2048]{2,1,0:T(8,128)(2,1)S(1)}, bf16[1,32,2048]{2,1,0:T(8,128)(2,1)}, bf16[2,32,2048]{2,1,0:T(8,128)(2,1)S(1)}) custom-call(s32[70]{0:T(128)S(1)} %shard_map.91.meta, bf16[4,32,4096]{2,1,0:T(8,128)(2,1)} %bitcast.20.keep, ...), custom_call_target="tpu_custom_call" | custom-call | bytes 1572864 | tf_op jit(solution)/shard_map/pallas_call | solution.py:196
  22.2 133.3 %conditional.1 = (bf16[1,4,32,4096]{3,2,1,0:T(8,128)(2,1)}, bf16[128,4096]{1,0:T(8,128)(2,1)}, bf16[128,4096]{1,0:T(8,128)(2,1)}) conditional(s32[]{:T(128)} %bitcast.19, (s32[]{:T(128)}, bf16[1,32,2048]{2,1,0:T(8,128)(2,1)S(1)}, bf16[1,32,2048]{2,1,0:T(8,128)(2,1)S(1)}, bf16[1,32,2048]{2,1,0:T(8,128)(2,1)}, ...), branch_computations={%region_0.1_spmd, %region_1.2_spmd, %region_2.3_spmd, %region_3.4_... | conditional | flops 4051697664 | bytes 122422320 | solution.py:461
  22.5 1.8 %collective-permute-start.99 = (bf16[4,32,2048]{2,1,0:T(8,128)(2,1)S(1)}, bf16[4,32,2048]{2,1,0:T(8,128)(2,1)S(1)}, u32[]{:S(2)}, u32[]{:S(2)}) collective-permute-start(bf16[4,32,2048]{2,1,0:T(8,128)(2,1)S(1)} %get-tuple-element.297), channel_id=1, source_target_pairs={{0,2},{2,0},{1,3},{3,1},{4,6},{6,4},{5,7},{7,5},{8,10},{10,8},{9,1... | collective-permute-start | bytes 1572872 | tf_op jit(solution)/shard_map/cond/branch_3_fun/ppermute | solution.py:20
  24.6 1.7 %collective-permute-start.103 = (bf16[128,2048]{1,0:T(8,128)(2,1)}, bf16[128,2048]{1,0:T(8,128)(2,1)}, u32[]{:S(2)}, u32[]{:S(2)}) collective-permute-start(bf16[128,2048]{1,0:T(8,128)(2,1)} %get-tuple-element.303), channel_id=1, source_target_pairs={{0,2},{2,0},{1,3},{3,1},{4,6},{6,4},{5,7},{7,5},{8,10},{10,8},{9,1... | collective-permute-start | bytes 1572872 | tf_op jit(solution)/shard_map/cond/branch_3_fun/ppermute | solution.py:20
  26.3 1.6 %collective-permute-start.90 = (bf16[1,32,2048]{2,1,0:T(8,128)(2,1)S(1)}, bf16[1,32,2048]{2,1,0:T(8,128)(2,1)S(1)}, u32[]{:S(2)}, u32[]{:S(2)}) collective-permute-start(bf16[1,32,2048]{2,1,0:T(8,128)(2,1)S(1)} %get-tuple-element.289), channel_id=1, source_target_pairs={{0,4},{4,8},{8,12},{12,0},{1,5},{5,9},{9,13},{13,1},{2,6},{6,10},{... | collective-permute-start | bytes 393224 | tf_op jit(solution)/shard_map/cond/branch_3_fun/ppermute | solution.py:386
  27.9 2.6 %collective-permute-start.91 = (bf16[1,32,2048]{2,1,0:T(8,128)(2,1)S(1)}, bf16[1,32,2048]{2,1,0:T(8,128)(2,1)S(1)}, u32[]{:S(2)}, u32[]{:S(2)}) collective-permute-start(bf16[1,32,2048]{2,1,0:T(8,128)(2,1)S(1)} %get-tuple-element.290), channel_id=1, source_target_pairs={{0,8},{4,12},{8,0},{12,4},{1,9},{5,13},{9,1},{13,5},{2,10},{6,14},... | collective-permute-start | bytes 393224 | tf_op jit(solution)/shard_map/cond/branch_3_fun/ppermute | solution.py:386
  30.5 2.8 %collective-permute-done.90.rest_5_.rest_7_ = bf16[1,32,2048]{2,1,0:T(8,128)(2,1)S(1)} collective-permute-done((bf16[1,32,2048]{2,1,0:T(8,128)(2,1)S(1)}, bf16[1,32,2048]{2,1,0:T(8,128)(2,1)S(1)}, u32[]{:S(2)}, u32[]{:S(2)}) %collective-permute-start.90) | collective-permute-done | bytes 131104 | tf_op jit(solution)/shard_map/cond/branch_3_fun/ppermute | solution.py:386
  33.2 4.0 %collective-permute-start.95 = (bf16[2,32,2048]{2,1,0:T(8,128)(2,1)S(1)}, bf16[2,32,2048]{2,1,0:T(8,128)(2,1)S(1)}, u32[]{:S(2)}, u32[]{:S(2)}) collective-permute-start(bf16[2,32,2048]{2,1,0:T(8,128)(2,1)S(1)} %get-tuple-element.292.rest_8_.rest_10_), channel_id=1, source_target_pairs={{0,12},{1,13},{2,14},{3,15},{16,28},{17,29},{18,30},{19,31}} | collective-permute-start | bytes 786440 | tf_op jit(solution)/shard_map/cond/branch_3_fun/ppermute | solution.py:386
  39.8 8.9 %collective-permute-done.96 = bf16[128,2048]{1,0:T(8,128)(2,1)} collective-permute-done((bf16[128,2048]{1,0:T(8,128)(2,1)}, bf16[128,2048]{1,0:T(8,128)(2,1)}, u32[]{:S(2)}, u32[]{:S(2)}) %collective-permute-start.96) | collective-permute-done | bytes 524320 | tf_op jit(solution)/shard_map/cond/branch_3_fun/ppermute | solution.py:20
  48.7 3.9 %collective-permute-start.92 = (bf16[1,32,2048]{2,1,0:T(8,128)(2,1)S(1)}, bf16[1,32,2048]{2,1,0:T(8,128)(2,1)S(1)}, u32[]{:S(2)}, u32[]{:S(2)}) collective-permute-start(bf16[1,32,2048]{2,1,0:T(8,128)(2,1)S(1)} %copy-done.36), channel_id=1, source_target_pairs={{0,12},{4,0},{8,4},{12,8},{1,13},{5,1},{9,5},{13,9},{2,14},{6,2},{... | collective-permute-start | bytes 393224 | tf_op jit(solution)/shard_map/cond/branch_3_fun/ppermute | solution.py:386
  52.6 1.6 %maximum_select_fusion.15.rest_12_.up = bf16[256,2048]{1,0:T(8,128)(2,1)S(1)} fusion(bf16[128,2048]{1,0:T(8,128)(2,1)} %collective-permute-done.96, bf16[128,2048]{1,0:T(8,128)(2,1)S(1)} %copy-done.10, pred[]{:T(512)S(6)} %eq.13), kind=kLoop, calls=%fused_computation.24 | loop fusion | flops 4718592 | bytes 2097153 | tf_op jit(solution)/shard_map/cond/branch_3_fun/jit(_where)/select_n | solution.py:24
  55.1 6.2 %collective-permute-start.106 = (bf16[2,32,2048]{2,1,0:T(8,128)(2,1)S(1)}, bf16[2,32,2048]{2,1,0:T(8,128)(2,1)S(1)}, u32[]{:S(2)}, u32[]{:S(2)}) collective-permute-start(bf16[2,32,2048]{2,1,0:T(8,128)(2,1)S(1)} %get-tuple-element.304.rest_0_.rest_5_), channel_id=1, source_target_pairs={{0,12},{1,13},{2,14},{3,15},{16,28},{17,29},{18,30},{19,31}} | collective-permute-start | bytes 786440 | tf_op jit(solution)/shard_map/cond/branch_3_fun/ppermute | solution.py:386
  62.7 1.9 %branch_3_fun.10 = bf16[4,128,256]{2,1,0:T(8,128)(2,1)S(1)} custom-call(s32[70]{0:T(128)S(1)} %get-tuple-element.283.meta, bf16[1,32,2048]{2,1,0:T(8,128)(2,1)S(1)} %get-tuple-element.284.rest_0_.rest_2_, bf16[1,32,2048]{2,1,0:T(8,128)(2,1)S(1)} %copy-done.14, bf16[1,32,2048]{2,1,0:T(8,128)(2,1)S(1)} %copy-done.18, bf16[1,32,2048]{2,1,0:T(8,128)(2,1)S(1)} %copy-done.22, ...), custom_call_target="tpu_custom_call" | custom-call | flops 536870912 | bytes 3145728 | tf_op jit(solution)/shard_map/cond/branch_3_fun/pallas_call | solution.py:247
  66.0 1.6 maximum_select_fusion.16.rest_4_
  68.2 5.6 %collective-permute-start.102 = (bf16[2,32,2048]{2,1,0:T(8,128)(2,1)S(1)}, bf16[2,32,2048]{2,1,0:T(8,128)(2,1)S(1)}, u32[]{:S(2)}, u32[]{:S(2)}) collective-permute-start(bf16[2,32,2048]{2,1,0:T(8,128)(2,1)S(1)} %get-tuple-element.301), channel_id=1, source_target_pairs={{0,12},{4,0},{8,4},{12,8},{1,13},{5,1},{9,5},{13,9},{2,14},{6,2},{... | collective-permute-start | bytes 786440 | tf_op jit(solution)/shard_map/cond/branch_3_fun/ppermute | solution.py:386
  73.8 1.6 %branch_3_fun.13 = bf16[2,128,256]{2,1,0:T(8,128)(2,1)S(1)} custom-call(s32[70]{0:T(128)S(1)} %get-tuple-element.283.meta, bf16[2,32,2048]{2,1,0:T(8,128)(2,1)S(1)} %get-tuple-element.304.rest_0_.rest_5_, bf16[2,32,2048]{2,1,0:T(8,128)(2,1)S(1)} %collective-permute-done.104.rest_1_.rest_6_, ...), custom_call_target="tpu_custom_call" | custom-call | flops 268435456 | bytes 2097152 | tf_op jit(solution)/shard_map/cond/branch_3_fun/pallas_call | solution.py:247
  75.6 1.6 %collective-permute-start.98 = (bf16[4,128,256]{2,1,0:T(8,128)(2,1)S(1)}, bf16[4,128,256]{2,1,0:T(8,128)(2,1)S(1)}, u32[]{:S(2)}, u32[]{:S(2)}) collective-permute-start(bf16[4,128,256]{2,1,0:T(8,128)(2,1)S(1)} %add_convert_fusion.9.h1), channel_id=1, source_target_pairs={{0,2},{2,0},{1,3},{3,1},{4,6},{6,4},{5,7},{7,5},{8,10},{10,8},{9,1... | collective-permute-start | bytes 786440 | tf_op jit(solution)/shard_map/cond/branch_3_fun/ppermute | solution.py:20
  78.5 6.3 %collective-permute-done.98.h2 = bf16[4,128,256]{2,1,0:T(8,128)(2,1)S(1)} collective-permute-done((bf16[4,128,256]{2,1,0:T(8,128)(2,1)S(1)}, bf16[4,128,256]{2,1,0:T(8,128)(2,1)S(1)}, u32[]{:S(2)}, u32[]{:S(2)}) %collective-permute-start.98) | collective-permute-done | bytes 262176 | tf_op jit(solution)/shard_map/cond/branch_3_fun/ppermute | solution.py:20
  85.5 1.7 %collective-permute-done.108.g2 = bf16[2,128,256]{2,1,0:T(8,128)(2,1)S(1)} collective-permute-done((bf16[2,128,256]{2,1,0:T(8,128)(2,1)S(1)}, bf16[2,128,256]{2,1,0:T(8,128)(2,1)S(1)}, u32[]{:S(2)}, u32[]{:S(2)}) %collective-permute-start.108) | collective-permute-done | bytes 131104 | tf_op jit(solution)/shard_map/cond/branch_3_fun/ppermute | solution.py:20
  88.8 1.6 %branch_3_fun.15 = bf16[2,128,256]{2,1,0:T(8,128)(2,1)S(1)} custom-call(s32[70]{0:T(128)S(1)} %get-tuple-element.283.meta, bf16[2,32,2048]{2,1,0:T(8,128)(2,1)S(1)} %get-tuple-element.298.rest_0_.rest_1_, bf16[2,32,2048]{2,1,0:T(8,128)(2,1)S(1)} %collective-permute-done.100.rest_1_.rest_2_, ...), custom_call_target="tpu_custom_call" | custom-call | flops 268435456 | bytes 2097152 | tf_op jit(solution)/shard_map/cond/branch_3_fun/pallas_call | solution.py:247
  91.8 1.6 %collective-permute-start.110 = (bf16[2,128,256]{2,1,0:T(8,128)(2,1)S(1)}, bf16[2,128,256]{2,1,0:T(8,128)(2,1)S(1)}, u32[]{:S(2)}, u32[]{:S(2)}) collective-permute-start(bf16[2,128,256]{2,1,0:T(8,128)(2,1)S(1)} %add_convert_fusion.10.g1), channel_id=1, source_target_pairs={{0,2},{2,0},{1,3},{3,1},{4,6},{6,4},{5,7},{7,5},{8,10},{10,8},{9,1... | collective-permute-start | bytes 393224 | tf_op jit(solution)/shard_map/cond/branch_3_fun/ppermute | solution.py:20
  94.8 2.6 %branch_3_fun.19 = (bf16[128,2048]{1,0:T(8,128)(2,1)S(1)}, bf16[128,2048]{1,0:T(8,128)(2,1)S(1)}) custom-call(s32[70]{0:T(128)S(1)} %get-tuple-element.283.meta, bf16[4,128,256]{2,1,0:T(8,128)(2,1)S(1)} %get-tuple-element.320.rest_0_, bf16[2,32,2048]{2,1,0:T(8,128)(2,1)S(1)} %get-tuple-element.298.rest_0_.rest_1_, ...), custom_call_target="tpu_custom_call" | custom-call | flops 536870912 | bytes 3145728 | tf_op jit(solution)/shard_map/cond/branch_3_fun/pallas_call | solution.py:327
  101.8 6.6 %collective-permute-start.111 = (bf16[2,32,2048]{2,1,0:T(8,128)(2,1)S(1)}, bf16[2,32,2048]{2,1,0:T(8,128)(2,1)S(1)}, u32[]{:S(2)}, u32[]{:S(2)}) collective-permute-start(bf16[2,32,2048]{2,1,0:T(8,128)(2,1)S(1)} %get-tuple-element.308), channel_id=1, source_target_pairs={{4,0},{8,4},{12,8},{0,12},{5,1},{9,5},{13,9},{1,13},{6,2},{10,6},{... | collective-permute-start | bytes 786440 | tf_op jit(solution)/shard_map/cond/branch_3_fun/ppermute | solution.py:386
  108.4 5.6 %collective-permute-start.113 = (bf16[2,32,2048]{2,1,0:T(8,128)(2,1)S(1)}, bf16[2,32,2048]{2,1,0:T(8,128)(2,1)S(1)}, u32[]{:S(2)}, u32[]{:S(2)}) collective-permute-start(bf16[2,32,2048]{2,1,0:T(8,128)(2,1)S(1)} %get-tuple-element.310), channel_id=1, source_target_pairs={{12,0},{0,4},{4,8},{8,12},{13,1},{1,5},{5,9},{9,13},{14,2},{2,6},{... | collective-permute-start | bytes 786440 | tf_op jit(solution)/shard_map/cond/branch_3_fun/ppermute | solution.py:386
  114.0 2.6 %branch_3_fun.18 = (bf16[128,2048]{1,0:T(8,128)(2,1)S(1)}, bf16[128,2048]{1,0:T(8,128)(2,1)S(1)}) custom-call(s32[70]{0:T(128)S(1)} %get-tuple-element.283.meta, bf16[2,128,256]{2,1,0:T(8,128)(2,1)S(1)} %get-tuple-element.317.rest_0_, bf16[2,128,256]{2,1,0:T(8,128)(2,1)S(1)} %get-tuple-element.305.rest_1_, ...), custom_call_target="tpu_custom_call" | custom-call | flops 536870912 | bytes 3145728 | tf_op jit(solution)/shard_map/cond/branch_3_fun/pallas_call | solution.py:327
  116.7 2.4 %collective-permute-done.116.rest_7_ = bf16[2,32,2048]{2,1,0:T(8,128)(2,1)S(1)} collective-permute-done((bf16[2,32,2048]{2,1,0:T(8,128)(2,1)S(1)}, bf16[2,32,2048]{2,1,0:T(8,128)(2,1)S(1)}, u32[]{:S(2)}, u32[]{:S(2)}) %collective-permute-start.116) | collective-permute-done | bytes 262176 | tf_op jit(solution)/shard_map/cond/branch_3_fun/ppermute | solution.py:386
  119.6 20.4 %collective-permute-done.112.rest_2_ = bf16[2,32,2048]{2,1,0:T(8,128)(2,1)S(1)} collective-permute-done((bf16[2,32,2048]{2,1,0:T(8,128)(2,1)S(1)}, bf16[2,32,2048]{2,1,0:T(8,128)(2,1)S(1)}, u32[]{:S(2)}, u32[]{:S(2)}) %collective-permute-start.112) | collective-permute-done | bytes 262176 | tf_op jit(solution)/shard_map/cond/branch_3_fun/ppermute | solution.py:386
  144.7 9.6 %collective-permute-done.117 = bf16[4,32,2048]{2,1,0:T(8,128)(2,1)S(1)} collective-permute-done((bf16[4,32,2048]{2,1,0:T(8,128)(2,1)S(1)}, bf16[4,32,2048]{2,1,0:T(8,128)(2,1)S(1)}, u32[]{:S(2)}, u32[]{:S(2)}) %collective-permute-start.117) | collective-permute-done | bytes 524320 | tf_op jit(solution)/shard_map/cond/branch_3_fun/ppermute | solution.py:20
  (84 shorter events, 32.4 us)
Async XLA Ops:
  1.7 18.2 %collective-permute-start.140 = (bf16[4,32,2048]{2,1,0:T(8,128)(2,1)S(1)}, bf16[4,32,2048]{2,1,0:T(8,128)(2,1)S(1)}, u32[]{:S(2)}, u32[]{:S(2)}) collective-permute-start(bf16[4,32,2048]{2,1,0:T(8,128)(2,1)S(1)} %dynamic-slice_bitcast_fusion.1), channel_id=1, source_target_pairs={{0,2},{2,0},{1,3},{3,1},{4,6},{6,4},{5,7},{7,5},{8,10},{10,8},{9,1... | collective-permute-start | bytes 1572872 | tf_op jit(solution)/shard_map/ppermute | solution.py:20
  4.7 12.0 %collective-permute-start.139 = (s32[1,4,1]{1,2,0:T(1,128)S(1)}, s32[1,4,1]{1,2,0:T(1,128)S(1)}, u32[]{:S(2)}, u32[]{:S(2)}) collective-permute-start(s32[1,4,1]{1,2,0:T(1,128)S(1)} %copy-done.2), channel_id=1, source_target_pairs={{0,2},{2,0},{1,3},{3,1},{4,6},{6,4},{5,7},{7,5},{8,10},{10,8},{9,1... | collective-permute-start | bytes 56 | tf_op jit(solution)/shard_map/ppermute | solution.py:20
  6.2 16.0 %collective-permute-start.141 = (bf16[1,32,2048]{2,1,0:T(8,128)(2,1)S(1)}, bf16[1,32,2048]{2,1,0:T(8,128)(2,1)}, u32[]{:S(2)}, u32[]{:S(2)}) collective-permute-start(bf16[1,32,2048]{2,1,0:T(8,128)(2,1)S(1)} %get-tuple-element.375), channel_id=1, source_target_pairs={{0,4},{4,8},{8,12},{12,0},{1,5},{5,9},{9,13},{13,1},{2,6},{6,10},{... | collective-permute-start | bytes 393224 | tf_op jit(solution)/shard_map/ppermute | solution.py:386
  8.3 13.9 %collective-permute-start.142 = (bf16[1,32,2048]{2,1,0:T(8,128)(2,1)S(1)}, bf16[1,32,2048]{2,1,0:T(8,128)(2,1)}, u32[]{:S(2)}, u32[]{:S(2)}) collective-permute-start(bf16[1,32,2048]{2,1,0:T(8,128)(2,1)S(1)} %get-tuple-element.376), channel_id=1, source_target_pairs={{0,8},{4,12},{8,0},{12,4},{1,9},{5,13},{9,1},{13,5},{2,10},{6,14},... | collective-permute-start | bytes 393224 | tf_op jit(solution)/shard_map/ppermute | solution.py:386
  10.9 11.3 %collective-permute-start.143 = (bf16[1,32,2048]{2,1,0:T(8,128)(2,1)S(1)}, bf16[1,32,2048]{2,1,0:T(8,128)(2,1)}, u32[]{:S(2)}, u32[]{:S(2)}) collective-permute-start(bf16[1,32,2048]{2,1,0:T(8,128)(2,1)S(1)} %get-tuple-element.377), channel_id=1, source_target_pairs={{0,12},{4,0},{8,4},{12,8},{1,13},{5,1},{9,5},{13,9},{2,14},{6,2},{... | collective-permute-start | bytes 393224 | tf_op jit(solution)/shard_map/ppermute | solution.py:386
  22.5 15.6 %collective-permute-start.99 = (bf16[4,32,2048]{2,1,0:T(8,128)(2,1)S(1)}, bf16[4,32,2048]{2,1,0:T(8,128)(2,1)S(1)}, u32[]{:S(2)}, u32[]{:S(2)}) collective-permute-start(bf16[4,32,2048]{2,1,0:T(8,128)(2,1)S(1)} %get-tuple-element.297), channel_id=1, source_target_pairs={{0,2},{2,0},{1,3},{3,1},{4,6},{6,4},{5,7},{7,5},{8,10},{10,8},{9,1... | collective-permute-start | bytes 1572872 | tf_op jit(solution)/shard_map/cond/branch_3_fun/ppermute | solution.py:20
  24.3 24.5 %collective-permute-start.96 = (bf16[128,2048]{1,0:T(8,128)(2,1)}, bf16[128,2048]{1,0:T(8,128)(2,1)}, u32[]{:S(2)}, u32[]{:S(2)}) collective-permute-start(bf16[128,2048]{1,0:T(8,128)(2,1)} %get-tuple-element.294), channel_id=1, source_target_pairs={{0,2},{2,0},{1,3},{3,1},{4,6},{6,4},{5,7},{7,5},{8,10},{10,8},{9,1... | collective-permute-start | bytes 1572872 | tf_op jit(solution)/shard_map/cond/branch_3_fun/ppermute | solution.py:20
  24.6 40.2 %collective-permute-start.103 = (bf16[128,2048]{1,0:T(8,128)(2,1)}, bf16[128,2048]{1,0:T(8,128)(2,1)}, u32[]{:S(2)}, u32[]{:S(2)}) collective-permute-start(bf16[128,2048]{1,0:T(8,128)(2,1)} %get-tuple-element.303), channel_id=1, source_target_pairs={{0,2},{2,0},{1,3},{3,1},{4,6},{6,4},{5,7},{7,5},{8,10},{10,8},{9,1... | collective-permute-start | bytes 1572872 | tf_op jit(solution)/shard_map/cond/branch_3_fun/ppermute | solution.py:20
  26.3 6.9 %collective-permute-start.90 = (bf16[1,32,2048]{2,1,0:T(8,128)(2,1)S(1)}, bf16[1,32,2048]{2,1,0:T(8,128)(2,1)S(1)}, u32[]{:S(2)}, u32[]{:S(2)}) collective-permute-start(bf16[1,32,2048]{2,1,0:T(8,128)(2,1)S(1)} %get-tuple-element.289), channel_id=1, source_target_pairs={{0,4},{4,8},{8,12},{12,0},{1,5},{5,9},{9,13},{13,1},{2,6},{6,10},{... | collective-permute-start | bytes 393224 | tf_op jit(solution)/shard_map/cond/branch_3_fun/ppermute | solution.py:386
  27.9 9.5 %collective-permute-start.91 = (bf16[1,32,2048]{2,1,0:T(8,128)(2,1)S(1)}, bf16[1,32,2048]{2,1,0:T(8,128)(2,1)S(1)}, u32[]{:S(2)}, u32[]{:S(2)}) collective-permute-start(bf16[1,32,2048]{2,1,0:T(8,128)(2,1)S(1)} %get-tuple-element.290), channel_id=1, source_target_pairs={{0,8},{4,12},{8,0},{12,4},{1,9},{5,13},{9,1},{13,5},{2,10},{6,14},... | collective-permute-start | bytes 393224 | tf_op jit(solution)/shard_map/cond/branch_3_fun/ppermute | solution.py:386
  33.2 28.0 %collective-permute-start.95 = (bf16[2,32,2048]{2,1,0:T(8,128)(2,1)S(1)}, bf16[2,32,2048]{2,1,0:T(8,128)(2,1)S(1)}, u32[]{:S(2)}, u32[]{:S(2)}) collective-permute-start(bf16[2,32,2048]{2,1,0:T(8,128)(2,1)S(1)} %get-tuple-element.292.rest_8_.rest_10_), channel_id=1, source_target_pairs={{0,12},{1,13},{2,14},{3,15},{16,28},{17,29},{18,30},{19,31}} | collective-permute-start | bytes 786440 | tf_op jit(solution)/shard_map/cond/branch_3_fun/ppermute | solution.py:386
  37.3 24.6 %collective-permute-start.94 = (bf16[2,32,2048]{2,1,0:T(8,128)(2,1)S(1)}, bf16[2,32,2048]{2,1,0:T(8,128)(2,1)S(1)}, u32[]{:S(2)}, u32[]{:S(2)}) collective-permute-start(bf16[2,32,2048]{2,1,0:T(8,128)(2,1)S(1)} %get-tuple-element.292.rest_8_.rest_10_), channel_id=1, source_target_pairs={{4,12},{5,13},{6,14},{7,15},{20,28},{21,29},{22,30},{23,31}} | collective-permute-start | bytes 786440 | tf_op jit(solution)/shard_map/cond/branch_3_fun/ppermute | solution.py:386
  38.0 24.6 %collective-permute-start.93 = (bf16[2,32,2048]{2,1,0:T(8,128)(2,1)S(1)}, bf16[2,32,2048]{2,1,0:T(8,128)(2,1)S(1)}, u32[]{:S(2)}, u32[]{:S(2)}) collective-permute-start(bf16[2,32,2048]{2,1,0:T(8,128)(2,1)S(1)} %get-tuple-element.292.rest_8_.rest_10_), channel_id=1, source_target_pairs={{8,12},{9,13},{10,14},{11,15},{24,28},{25,29},{26,30},{27,31}} | collective-permute-start | bytes 786440 | tf_op jit(solution)/shard_map/cond/branch_3_fun/ppermute | solution.py:386
  48.7 6.4 %collective-permute-start.92 = (bf16[1,32,2048]{2,1,0:T(8,128)(2,1)S(1)}, bf16[1,32,2048]{2,1,0:T(8,128)(2,1)S(1)}, u32[]{:S(2)}, u32[]{:S(2)}) collective-permute-start(bf16[1,32,2048]{2,1,0:T(8,128)(2,1)S(1)} %copy-done.36), channel_id=1, source_target_pairs={{0,12},{4,0},{8,4},{12,8},{1,13},{5,1},{9,5},{13,9},{2,14},{6,2},{... | collective-permute-start | bytes 393224 | tf_op jit(solution)/shard_map/cond/branch_3_fun/ppermute | solution.py:386
  55.1 12.4 %collective-permute-start.106 = (bf16[2,32,2048]{2,1,0:T(8,128)(2,1)S(1)}, bf16[2,32,2048]{2,1,0:T(8,128)(2,1)S(1)}, u32[]{:S(2)}, u32[]{:S(2)}) collective-permute-start(bf16[2,32,2048]{2,1,0:T(8,128)(2,1)S(1)} %get-tuple-element.304.rest_0_.rest_5_), channel_id=1, source_target_pairs={{0,12},{1,13},{2,14},{3,15},{16,28},{17,29},{18,30},{19,31}} | collective-permute-start | bytes 786440 | tf_op jit(solution)/shard_map/cond/branch_3_fun/ppermute | solution.py:386
  61.3 7.0 %collective-permute-start.105 = (bf16[2,32,2048]{2,1,0:T(8,128)(2,1)S(1)}, bf16[2,32,2048]{2,1,0:T(8,128)(2,1)S(1)}, u32[]{:S(2)}, u32[]{:S(2)}) collective-permute-start(bf16[2,32,2048]{2,1,0:T(8,128)(2,1)S(1)} %get-tuple-element.304.rest_0_.rest_5_), channel_id=1, source_target_pairs={{4,12},{5,13},{6,14},{7,15},{20,28},{21,29},{22,30},{23,31}} | collective-permute-start | bytes 786440 | tf_op jit(solution)/shard_map/cond/branch_3_fun/ppermute | solution.py:386
  62.0 11.9 %collective-permute-start.104 = (bf16[2,32,2048]{2,1,0:T(8,128)(2,1)S(1)}, bf16[2,32,2048]{2,1,0:T(8,128)(2,1)S(1)}, u32[]{:S(2)}, u32[]{:S(2)}) collective-permute-start(bf16[2,32,2048]{2,1,0:T(8,128)(2,1)S(1)} %get-tuple-element.304.rest_0_.rest_5_), channel_id=1, source_target_pairs={{8,12},{9,13},{10,14},{11,15},{24,28},{25,29},{26,30},{27,31}} | collective-permute-start | bytes 786440 | tf_op jit(solution)/shard_map/cond/branch_3_fun/ppermute | solution.py:386
  64.7 10.9 %collective-permute-start.97 = (bf16[4,128,256]{2,1,0:T(8,128)(2,1)S(1)}, bf16[4,128,256]{2,1,0:T(8,128)(2,1)S(1)}, u32[]{:S(2)}, u32[]{:S(2)}) collective-permute-start(bf16[4,128,256]{2,1,0:T(8,128)(2,1)S(1)} %branch_3_fun.10), channel_id=1, source_target_pairs={{0,1},{1,0},{2,3},{3,2},{4,5},{5,4},{6,7},{7,6},{8,9},{9,8},{10,11... | collective-permute-start | bytes 786440 | tf_op jit(solution)/shard_map/cond/branch_3_fun/ppermute | solution.py:20
  64.7 24.0 %collective-permute-start.100 = (bf16[2,32,2048]{2,1,0:T(8,128)(2,1)S(1)}, bf16[2,32,2048]{2,1,0:T(8,128)(2,1)S(1)}, u32[]{:S(2)}, u32[]{:S(2)}) collective-permute-start(bf16[2,32,2048]{2,1,0:T(8,128)(2,1)S(1)} %get-tuple-element.299), channel_id=1, source_target_pairs={{0,4},{4,8},{8,12},{12,0},{1,5},{5,9},{9,13},{13,1},{2,6},{6,10},{... | collective-permute-start | bytes 786440 | tf_op jit(solution)/shard_map/cond/branch_3_fun/ppermute | solution.py:386
  67.5 21.2 %collective-permute-start.101 = (bf16[2,32,2048]{2,1,0:T(8,128)(2,1)S(1)}, bf16[2,32,2048]{2,1,0:T(8,128)(2,1)S(1)}, u32[]{:S(2)}, u32[]{:S(2)}) collective-permute-start(bf16[2,32,2048]{2,1,0:T(8,128)(2,1)S(1)} %get-tuple-element.300), channel_id=1, source_target_pairs={{0,8},{4,12},{8,0},{12,4},{1,9},{5,13},{9,1},{13,5},{2,10},{6,14},... | collective-permute-start | bytes 786440 | tf_op jit(solution)/shard_map/cond/branch_3_fun/ppermute | solution.py:386
  68.2 20.5 %collective-permute-start.102 = (bf16[2,32,2048]{2,1,0:T(8,128)(2,1)S(1)}, bf16[2,32,2048]{2,1,0:T(8,128)(2,1)S(1)}, u32[]{:S(2)}, u32[]{:S(2)}) collective-permute-start(bf16[2,32,2048]{2,1,0:T(8,128)(2,1)S(1)} %get-tuple-element.301), channel_id=1, source_target_pairs={{0,12},{4,0},{8,4},{12,8},{1,13},{5,1},{9,5},{13,9},{2,14},{6,2},{... | collective-permute-start | bytes 786440 | tf_op jit(solution)/shard_map/cond/branch_3_fun/ppermute | solution.py:386
  75.6 9.2 %collective-permute-start.98 = (bf16[4,128,256]{2,1,0:T(8,128)(2,1)S(1)}, bf16[4,128,256]{2,1,0:T(8,128)(2,1)S(1)}, u32[]{:S(2)}, u32[]{:S(2)}) collective-permute-start(bf16[4,128,256]{2,1,0:T(8,128)(2,1)S(1)} %add_convert_fusion.9.h1), channel_id=1, source_target_pairs={{0,2},{2,0},{1,3},{3,1},{4,6},{6,4},{5,7},{7,5},{8,10},{10,8},{9,1... | collective-permute-start | bytes 786440 | tf_op jit(solution)/shard_map/cond/branch_3_fun/ppermute | solution.py:20
  77.3 10.0 %collective-permute-start.108 = (bf16[2,128,256]{2,1,0:T(8,128)(2,1)S(1)}, bf16[2,128,256]{2,1,0:T(8,128)(2,1)S(1)}, u32[]{:S(2)}, u32[]{:S(2)}) collective-permute-start(bf16[2,128,256]{2,1,0:T(8,128)(2,1)S(1)} %add_convert_fusion.11.g1), channel_id=1, source_target_pairs={{0,2},{2,0},{1,3},{3,1},{4,6},{6,4},{5,7},{7,5},{8,10},{10,8},{9,1... | collective-permute-start | bytes 393224 | tf_op jit(solution)/shard_map/cond/branch_3_fun/ppermute | solution.py:20
  93.4 15.0 %collective-permute-start.114 = (bf16[2,32,2048]{2,1,0:T(8,128)(2,1)S(1)}, bf16[2,32,2048]{2,1,0:T(8,128)(2,1)S(1)}, u32[]{:S(2)}, u32[]{:S(2)}) collective-permute-start(bf16[2,32,2048]{2,1,0:T(8,128)(2,1)S(1)} %get-tuple-element.312), channel_id=1, source_target_pairs={{12,8},{13,9},{14,10},{15,11},{28,24},{29,25},{30,26},{31,27}} | collective-permute-start | bytes 786440 | tf_op jit(solution)/shard_map/cond/branch_3_fun/ppermute | solution.py:386
  94.1 14.3 %collective-permute-start.115 = (bf16[2,32,2048]{2,1,0:T(8,128)(2,1)S(1)}, bf16[2,32,2048]{2,1,0:T(8,128)(2,1)S(1)}, u32[]{:S(2)}, u32[]{:S(2)}) collective-permute-start(bf16[2,32,2048]{2,1,0:T(8,128)(2,1)S(1)} %get-tuple-element.313), channel_id=1, source_target_pairs={{12,4},{13,5},{14,6},{15,7},{28,20},{29,21},{30,22},{31,23}} | collective-permute-start | bytes 786440 | tf_op jit(solution)/shard_map/cond/branch_3_fun/ppermute | solution.py:386
  97.5 44.8 %collective-permute-start.119 = (bf16[128,2048]{1,0:T(8,128)(2,1)S(1)}, bf16[128,2048]{1,0:T(8,128)(2,1)S(1)}, u32[]{:S(2)}, u32[]{:S(2)}) collective-permute-start(bf16[128,2048]{1,0:T(8,128)(2,1)S(1)} %get-tuple-element.323), channel_id=1, source_target_pairs={{0,2},{2,0},{1,3},{3,1},{4,6},{6,4},{5,7},{7,5},{8,10},{10,8},{9,1... | collective-permute-start | bytes 1572872 | tf_op jit(solution)/shard_map/cond/branch_3_fun/ppermute | solution.py:20
  99.0 20.1 %collective-permute-start.116 = (bf16[2,32,2048]{2,1,0:T(8,128)(2,1)S(1)}, bf16[2,32,2048]{2,1,0:T(8,128)(2,1)S(1)}, u32[]{:S(2)}, u32[]{:S(2)}) collective-permute-start(bf16[2,32,2048]{2,1,0:T(8,128)(2,1)S(1)} %get-tuple-element.314), channel_id=1, source_target_pairs={{12,0},{13,1},{14,2},{15,3},{28,16},{29,17},{30,18},{31,19}} | collective-permute-start | bytes 786440 | tf_op jit(solution)/shard_map/cond/branch_3_fun/ppermute | solution.py:386
  101.8 17.8 %collective-permute-start.111 = (bf16[2,32,2048]{2,1,0:T(8,128)(2,1)S(1)}, bf16[2,32,2048]{2,1,0:T(8,128)(2,1)S(1)}, u32[]{:S(2)}, u32[]{:S(2)}) collective-permute-start(bf16[2,32,2048]{2,1,0:T(8,128)(2,1)S(1)} %get-tuple-element.308), channel_id=1, source_target_pairs={{4,0},{8,4},{12,8},{0,12},{5,1},{9,5},{13,9},{1,13},{6,2},{10,6},{... | collective-permute-start | bytes 786440 | tf_op jit(solution)/shard_map/cond/branch_3_fun/ppermute | solution.py:386
  108.4 31.6 %collective-permute-start.112 = (bf16[2,32,2048]{2,1,0:T(8,128)(2,1)S(1)}, bf16[2,32,2048]{2,1,0:T(8,128)(2,1)S(1)}, u32[]{:S(2)}, u32[]{:S(2)}) collective-permute-start(bf16[2,32,2048]{2,1,0:T(8,128)(2,1)S(1)} %get-tuple-element.309), channel_id=1, source_target_pairs={{8,0},{12,4},{0,8},{4,12},{9,1},{13,5},{1,9},{5,13},{10,2},{14,6},... | collective-permute-start | bytes 786440 | tf_op jit(solution)/shard_map/cond/branch_3_fun/ppermute | solution.py:386
  108.4 31.6 %collective-permute-start.113 = (bf16[2,32,2048]{2,1,0:T(8,128)(2,1)S(1)}, bf16[2,32,2048]{2,1,0:T(8,128)(2,1)S(1)}, u32[]{:S(2)}, u32[]{:S(2)}) collective-permute-start(bf16[2,32,2048]{2,1,0:T(8,128)(2,1)S(1)} %get-tuple-element.310), channel_id=1, source_target_pairs={{12,0},{0,4},{4,8},{8,12},{13,1},{1,5},{5,9},{9,13},{14,2},{2,6},{... | collective-permute-start | bytes 786440 | tf_op jit(solution)/shard_map/cond/branch_3_fun/ppermute | solution.py:386
  119.0 24.5 %collective-permute-start.118 = (bf16[128,2048]{1,0:T(8,128)(2,1)S(1)}, bf16[128,2048]{1,0:T(8,128)(2,1)S(1)}, u32[]{:S(2)}, u32[]{:S(2)}) collective-permute-start(bf16[128,2048]{1,0:T(8,128)(2,1)S(1)} %get-tuple-element.319), channel_id=1, source_target_pairs={{0,2},{2,0},{1,3},{3,1},{4,6},{6,4},{5,7},{7,5},{8,10},{10,8},{9,1... | collective-permute-start | bytes 1572872 | tf_op jit(solution)/shard_map/cond/branch_3_fun/ppermute | solution.py:20
  141.2 13.2 %collective-permute-start.117 = (bf16[4,32,2048]{2,1,0:T(8,128)(2,1)S(1)}, bf16[4,32,2048]{2,1,0:T(8,128)(2,1)S(1)}, u32[]{:S(2)}, u32[]{:S(2)}) collective-permute-start(bf16[4,32,2048]{2,1,0:T(8,128)(2,1)S(1)} %get-tuple-element.316), channel_id=1, source_target_pairs={{0,2},{2,0},{1,3},{3,1},{4,6},{6,4},{5,7},{7,5},{8,10},{10,8},{9,1... | collective-permute-start | bytes 1572872 | tf_op jit(solution)/shard_map/cond/branch_3_fun/ppermute | solution.py:20
  (13 other events, 84.1 us)

commit v3 on v2

--- a/solution.py
+++ b/solution.py
@@ -419,7 +419,7 @@
         if fast:
             tok = [tok_first, move(tok_sent[:owners], forth), move([tok_sent[owners]] * owners, extra_forth)]
             cot_groups = ((0, EVEN, True), extra_group)
-            cot_sent = dispatch(meta, cotangent[0], cot_got, owners, by_slot, cot_groups)
+            cot_sent = dispatch(meta, cotangent[0], after(cot_got, tok[1][-1]), owners, by_slot, cot_groups)
             cot = [move(cot_sent[:owners], forth), move([cot_sent[owners]] * owners, extra_forth)]
         else:
             cot_groups = ((0, SLOTS, True),)

time: 158 us -> 152 us (0.962)
  starting transfers between devices: 63.9 us -> 53.9 us
  waiting for transfers between devices: 55.4 us -> 58.8 us
    ppermute x21, starting transfers between devices: 49.3 us -> 40.2 us  [move(): lax.ppermute(pieces[k], 'tensor', perm_of(k))]
    ppermute x21, waiting for transfers between devices: 26.5 us -> 29.5 us  [move(): lax.ppermute(pieces[k], 'tensor', perm_of(k))]
  transfers between devices with their start and end apart: 35 -> 35, of which waited for: 12 -> 12; matrix products, arithmetic and copies ran while one was open for 6% -> 7% of each run, Pallas kernels for 13% -> 13%
where the time goes in v3:
time: 152 us; the launch traced here: 149 us
  waiting for transfers between devices  58.8 us (39%)
  starting transfers between devices  53.9 us (35%)
  Pallas kernels  21.5 us (14%)
  other arithmetic  6.94 us (5%)
  local copies, waits for them, and re-layouts  5.93 us (4%)
    ppermute x21, starting transfers between devices, move(): lax.ppermute(pieces[k], 'tensor', perm_of(k))  40.2 us
    ppermute x21, waiting for transfers between devices, move(): lax.ppermute(pieces[k], 'tensor', perm_of(k))  29.5 us
    ppermute x14, waiting for transfers between devices, swap(): return lax.ppermute(x, axis, [(0, 1), (1, 0)])  29.3 us
    ppermute x14, starting transfers between devices, swap(): return lax.ppermute(x, axis, [(0, 1), (1, 0)])  13.7 us
    select_n x5, other arithmetic, ordered(): jnp.where(side == 0, jnp.concatenate([mine, other], axis), jnp.concatenat...  6.81 us
    pallas_call x2, Pallas kernels, weights(): call(functools.partial(weights_kernel, owners, act_counts, counts, moved)...  5.21 us
    pallas_call x3, Pallas kernels, product(): call(functools.partial(product_kernel, counts, owners, moved), [jax.Shape...  5.18 us
    pallas_call x2, Pallas kernels, dispatch(): call(kernel, outs, 2, moved=4 * sum(counts) * rows * width)(meta, keep, got)  3.32 us
  transfers between devices with their start and end apart: 35, of which 12 were waited for; matrix products, arithmetic and copies ran while one was open for 7% of the time, Pallas kernels for 13%

profile of v3, /device:TPU:0, one launch (start us, length us, event | category | flops | bytes accessed | tf_op | source)
XLA Modules:
  0.0 149.0 jit_solution(1897016286834451244)
XLA Ops:
  1.7 3.0 %collective-permute-start.140 = (bf16[4,32,2048]{2,1,0:T(8,128)(2,1)S(1)}, bf16[4,32,2048]{2,1,0:T(8,128)(2,1)S(1)}, u32[]{:S(2)}, u32[]{:S(2)}) collective-permute-start(bf16[4,32,2048]{2,1,0:T(8,128)(2,1)S(1)} %dynamic-slice_bitcast_fusion.1), channel_id=1, source_target_pairs={{0,2},{2,0},{1,3},{3,1},{4,6},{6,4},{5,7},{7,5},{8,10},{10,8},{9,1... | collective-permute-start | bytes 1572872 | tf_op jit(solution)/shard_map/ppermute | solution.py:20
  6.2 2.1 %collective-permute-start.141 = (bf16[1,32,2048]{2,1,0:T(8,128)(2,1)S(1)}, bf16[1,32,2048]{2,1,0:T(8,128)(2,1)}, u32[]{:S(2)}, u32[]{:S(2)}) collective-permute-start(bf16[1,32,2048]{2,1,0:T(8,128)(2,1)S(1)} %get-tuple-element.379), channel_id=1, source_target_pairs={{0,4},{4,8},{8,12},{12,0},{1,5},{5,9},{9,13},{13,1},{2,6},{6,10},{... | collective-permute-start | bytes 393224 | tf_op jit(solution)/shard_map/ppermute | solution.py:386
  8.3 2.6 %collective-permute-start.142 = (bf16[1,32,2048]{2,1,0:T(8,128)(2,1)S(1)}, bf16[1,32,2048]{2,1,0:T(8,128)(2,1)}, u32[]{:S(2)}, u32[]{:S(2)}) collective-permute-start(bf16[1,32,2048]{2,1,0:T(8,128)(2,1)S(1)} %get-tuple-element.380), channel_id=1, source_target_pairs={{0,8},{4,12},{8,0},{12,4},{1,9},{5,13},{9,1},{13,5},{2,10},{6,14},... | collective-permute-start | bytes 393224 | tf_op jit(solution)/shard_map/ppermute | solution.py:386
  12.2 2.9 %constant_dynamic-slice_fusion = (bf16[128,2048]{1,0:T(8,128)(2,1)S(1)}, bf16[128,2048]{1,0:T(8,128)(2,1)}, bf16[128,2048]{1,0:T(8,128)(2,1)}, bf16[128,2048]{1,0:T(8,128)(2,1)}) fusion(bf16[128,4096]{1,0:T(8,128)(2,1)} %param.13, s32[]{:T(128)S(6)} %select_n.182, s32[]{:T(128)S(6)} %select_n.181, bf16[128,4096]{1,0:T(8,128)(2,1)} %param.12), kind=kLoop, calls=%fused_computation.41 | loop fusion | bytes 4194312 | tf_op jit(solution)/shard_map/dynamic_slice | solution.py:95
  20.0 2.3 %shard_map.92 = (bf16[1,32,2048]{2,1,0:T(8,128)(2,1)}, bf16[1,32,2048]{2,1,0:T(8,128)(2,1)S(1)}, bf16[1,32,2048]{2,1,0:T(8,128)(2,1)}, bf16[1,32,2048]{2,1,0:T(8,128)(2,1)S(1)}, bf16[2,32,2048]{2,1,0:T(8,128)(2,1)S(1)}) custom-call(s32[70]{0:T(128)S(1)} %shard_map.91.meta, bf16[4,32,4096]{2,1,0:T(8,128)(2,1)} %bitcast.20.keep, ...), custom_call_target="tpu_custom_call" | custom-call | bytes 1572864 | tf_op jit(solution)/shard_map/pallas_call | solution.py:196
  22.2 126.7 %conditional.1 = (bf16[1,4,32,4096]{3,2,1,0:T(8,128)(2,1)}, bf16[128,4096]{1,0:T(8,128)(2,1)}, bf16[128,4096]{1,0:T(8,128)(2,1)}) conditional(s32[]{:T(128)} %bitcast.19, (s32[]{:T(128)}, bf16[1,32,2048]{2,1,0:T(8,128)(2,1)S(1)}, bf16[1,32,2048]{2,1,0:T(8,128)(2,1)}, bf16[1,32,2048]{2,1,0:T(8,128)(2,1)S(1)}, ...), branch_computations={%region_0.1_spmd, %region_1.2_spmd, %region_2.3_spmd, %region_3.4_... | conditional | flops 4051697664 | bytes 122422320 | solution.py:461
  22.5 1.8 %collective-permute-start.69 = (bf16[4,32,2048]{2,1,0:T(8,128)(2,1)S(1)}, bf16[4,32,2048]{2,1,0:T(8,128)(2,1)S(1)}, u32[]{:S(2)}, u32[]{:S(2)}) collective-permute-start(bf16[4,32,2048]{2,1,0:T(8,128)(2,1)S(1)} %get-tuple-element.257), channel_id=1, source_target_pairs={{0,2},{2,0},{1,3},{3,1},{4,6},{6,4},{5,7},{7,5},{8,10},{10,8},{9,1... | collective-permute-start | bytes 1572872 | tf_op jit(solution)/shard_map/cond/branch_2_fun/ppermute | solution.py:20
  24.5 1.7 %collective-permute-start.73 = (bf16[128,2048]{1,0:T(8,128)(2,1)}, bf16[128,2048]{1,0:T(8,128)(2,1)}, u32[]{:S(2)}, u32[]{:S(2)}) collective-permute-start(bf16[128,2048]{1,0:T(8,128)(2,1)} %get-tuple-element.264), channel_id=1, source_target_pairs={{0,2},{2,0},{1,3},{3,1},{4,6},{6,4},{5,7},{7,5},{8,10},{10,8},{9,1... | collective-permute-start | bytes 1572872 | tf_op jit(solution)/shard_map/cond/branch_2_fun/ppermute | solution.py:20
  26.3 1.6 %collective-permute-start.60 = (bf16[1,32,2048]{2,1,0:T(8,128)(2,1)S(1)}, bf16[1,32,2048]{2,1,0:T(8,128)(2,1)S(1)}, u32[]{:S(2)}, u32[]{:S(2)}) collective-permute-start(bf16[1,32,2048]{2,1,0:T(8,128)(2,1)S(1)} %get-tuple-element.249), channel_id=1, source_target_pairs={{0,4},{4,8},{8,12},{12,0},{1,5},{5,9},{9,13},{13,1},{2,6},{6,10},{... | collective-permute-start | bytes 393224 | tf_op jit(solution)/shard_map/cond/branch_2_fun/ppermute | solution.py:386
  27.9 2.2 %collective-permute-start.62 = (bf16[1,32,2048]{2,1,0:T(8,128)(2,1)S(1)}, bf16[1,32,2048]{2,1,0:T(8,128)(2,1)S(1)}, u32[]{:S(2)}, u32[]{:S(2)}) collective-permute-start(bf16[1,32,2048]{2,1,0:T(8,128)(2,1)S(1)} %get-tuple-element.251), channel_id=1, source_target_pairs={{0,12},{4,0},{8,4},{12,8},{1,13},{5,1},{9,5},{13,9},{2,14},{6,2},{... | collective-permute-start | bytes 393224 | tf_op jit(solution)/shard_map/cond/branch_2_fun/ppermute | solution.py:386
  30.1 3.2 %collective-permute-done.60.rest_5_.rest_7_ = bf16[1,32,2048]{2,1,0:T(8,128)(2,1)S(1)} collective-permute-done((bf16[1,32,2048]{2,1,0:T(8,128)(2,1)S(1)}, bf16[1,32,2048]{2,1,0:T(8,128)(2,1)S(1)}, u32[]{:S(2)}, u32[]{:S(2)}) %collective-permute-start.60) | collective-permute-done | bytes 131104 | tf_op jit(solution)/shard_map/cond/branch_2_fun/ppermute | solution.py:386
  34.2 3.4 %collective-permute-start.64 = (bf16[2,32,2048]{2,1,0:T(8,128)(2,1)S(1)}, bf16[2,32,2048]{2,1,0:T(8,128)(2,1)S(1)}, u32[]{:S(2)}, u32[]{:S(2)}) collective-permute-start(bf16[2,32,2048]{2,1,0:T(8,128)(2,1)S(1)} %get-tuple-element.252.rest_8_.rest_10_), channel_id=1, source_target_pairs={{0,8},{1,9},{2,10},{3,11},{16,24},{17,25},{18,26},{19,27}} | collective-permute-start | bytes 786440 | tf_op jit(solution)/shard_map/cond/branch_2_fun/ppermute | solution.py:386
  39.4 9.3 %collective-permute-done.66 = bf16[128,2048]{1,0:T(8,128)(2,1)} collective-permute-done((bf16[128,2048]{1,0:T(8,128)(2,1)}, bf16[128,2048]{1,0:T(8,128)(2,1)}, u32[]{:S(2)}, u32[]{:S(2)}) %collective-permute-start.66) | collective-permute-done | bytes 524320 | tf_op jit(solution)/shard_map/cond/branch_2_fun/ppermute | solution.py:20
  48.7 2.8 %collective-permute-start.61 = (bf16[1,32,2048]{2,1,0:T(8,128)(2,1)S(1)}, bf16[1,32,2048]{2,1,0:T(8,128)(2,1)S(1)}, u32[]{:S(2)}, u32[]{:S(2)}) collective-permute-start(bf16[1,32,2048]{2,1,0:T(8,128)(2,1)S(1)} %copy-done.35), channel_id=1, source_target_pairs={{0,8},{4,12},{8,0},{12,4},{1,9},{5,13},{9,1},{13,5},{2,10},{6,14},... | collective-permute-start | bytes 393224 | tf_op jit(solution)/shard_map/cond/branch_2_fun/ppermute | solution.py:386
  51.6 1.6 %maximum_select_fusion.10.rest_12_.up = bf16[256,2048]{1,0:T(8,128)(2,1)S(1)} fusion(bf16[128,2048]{1,0:T(8,128)(2,1)} %collective-permute-done.66, bf16[128,2048]{1,0:T(8,128)(2,1)S(1)} %copy-done.9, pred[]{:T(512)S(6)} %eq.12), kind=kLoop, calls=%fused_computation.16 | loop fusion | flops 4718592 | bytes 2097153 | tf_op jit(solution)/shard_map/cond/branch_2_fun/jit(_where)/select_n | solution.py:24
  53.2 2.8 %collective-permute-done.61.rest_6_.rest_8_ = bf16[1,32,2048]{2,1,0:T(8,128)(2,1)S(1)} collective-permute-done((bf16[1,32,2048]{2,1,0:T(8,128)(2,1)S(1)}, bf16[1,32,2048]{2,1,0:T(8,128)(2,1)S(1)}, u32[]{:S(2)}, u32[]{:S(2)}) %collective-permute-start.61) | collective-permute-done | bytes 131104 | tf_op jit(solution)/shard_map/cond/branch_2_fun/ppermute | solution.py:386
  56.7 4.1 %collective-permute-start.75 = (bf16[2,32,2048]{2,1,0:T(8,128)(2,1)S(1)}, bf16[2,32,2048]{2,1,0:T(8,128)(2,1)S(1)}, u32[]{:S(2)}, u32[]{:S(2)}) collective-permute-start(bf16[2,32,2048]{2,1,0:T(8,128)(2,1)S(1)} %get-tuple-element.265.rest_0_.rest_5_), channel_id=1, source_target_pairs={{0,8},{1,9},{2,10},{3,11},{16,24},{17,25},{18,26},{19,27}} | collective-permute-start | bytes 786440 | tf_op jit(solution)/shard_map/cond/branch_2_fun/ppermute | solution.py:386
  61.5 1.9 %branch_2_fun.10 = bf16[4,128,256]{2,1,0:T(8,128)(2,1)S(1)} custom-call(s32[70]{0:T(128)S(1)} %get-tuple-element.243.meta, bf16[1,32,2048]{2,1,0:T(8,128)(2,1)S(1)} %get-tuple-element.244.rest_0_.rest_2_, bf16[1,32,2048]{2,1,0:T(8,128)(2,1)S(1)} %copy-done.13, bf16[1,32,2048]{2,1,0:T(8,128)(2,1)S(1)} %copy-done.17, bf16[1,32,2048]{2,1,0:T(8,128)(2,1)S(1)} %copy-done.21, ...), custom_call_target="tpu_custom_call" | custom-call | flops 536870912 | bytes 3145728 | tf_op jit(solution)/shard_map/cond/branch_2_fun/pallas_call | solution.py:247
  64.8 1.6 %maximum_select_fusion.11.rest_4_ = bf16[256,2048]{1,0:T(8,128)(2,1)S(1)} fusion(bf16[128,2048]{1,0:T(8,128)(2,1)} %collective-permute-done.73, bf16[128,2048]{1,0:T(8,128)(2,1)S(1)} %get-tuple-element.263, pred[]{:T(512)S(6)} %eq.12), kind=kLoop, calls=%fused_computation.17 | loop fusion | flops 4718592 | bytes 2097153 | tf_op jit(solution)/shard_map/cond/branch_2_fun/jit(_where)/select_n | solution.py:24
  66.8 2.3 %collective-permute-start.72 = (bf16[2,32,2048]{2,1,0:T(8,128)(2,1)S(1)}, bf16[2,32,2048]{2,1,0:T(8,128)(2,1)S(1)}, u32[]{:S(2)}, u32[]{:S(2)}) collective-permute-start(bf16[2,32,2048]{2,1,0:T(8,128)(2,1)S(1)} %get-tuple-element.262), channel_id=1, source_target_pairs={{0,12},{4,0},{8,4},{12,8},{1,13},{5,1},{9,5},{13,9},{2,14},{6,2},{... | collective-permute-start | bytes 786440 | tf_op jit(solution)/shard_map/cond/branch_2_fun/ppermute | solution.py:386
  69.1 1.6 %branch_2_fun.13 = bf16[2,128,256]{2,1,0:T(8,128)(2,1)S(1)} custom-call(s32[70]{0:T(128)S(1)} %get-tuple-element.243.meta, bf16[2,32,2048]{2,1,0:T(8,128)(2,1)S(1)} %get-tuple-element.265.rest_0_.rest_5_, bf16[2,32,2048]{2,1,0:T(8,128)(2,1)S(1)} %collective-permute-done.74.rest_1_.rest_6_, bf16[2,32,2048]{2,1,0:T(8,128)(2,1)S(1)} %collective-permute-done.75.rest_2_.rest_7_, ...), custom_call_target="tpu_custom_call" | custom-call | flops 268435456 | bytes 2097152 | tf_op jit(solution)/shard_map/cond/branch_2_fun/pallas_call | solution.py:247
  70.9 1.5 %collective-permute-start.68 = (bf16[4,128,256]{2,1,0:T(8,128)(2,1)S(1)}, bf16[4,128,256]{2,1,0:T(8,128)(2,1)S(1)}, u32[]{:S(2)}, u32[]{:S(2)}) collective-permute-start(bf16[4,128,256]{2,1,0:T(8,128)(2,1)S(1)} %add_convert_fusion.6.h1), channel_id=1, source_target_pairs={{0,2},{2,0},{1,3},{3,1},{4,6},{6,4},{5,7},{7,5},{8,10},{10,8},{9,1... | collective-permute-start | bytes 786440 | tf_op jit(solution)/shard_map/cond/branch_2_fun/ppermute | solution.py:20
  73.8 6.3 %collective-permute-done.68.h2 = bf16[4,128,256]{2,1,0:T(8,128)(2,1)S(1)} collective-permute-done((bf16[4,128,256]{2,1,0:T(8,128)(2,1)S(1)}, bf16[4,128,256]{2,1,0:T(8,128)(2,1)S(1)}, u32[]{:S(2)}, u32[]{:S(2)}) %collective-permute-start.68) | collective-permute-done | bytes 262176 | tf_op jit(solution)/shard_map/cond/branch_2_fun/ppermute | solution.py:20
  80.8 1.7 %collective-permute-done.78.g2 = bf16[2,128,256]{2,1,0:T(8,128)(2,1)S(1)} collective-permute-done((bf16[2,128,256]{2,1,0:T(8,128)(2,1)S(1)}, bf16[2,128,256]{2,1,0:T(8,128)(2,1)S(1)}, u32[]{:S(2)}, u32[]{:S(2)}) %collective-permute-start.78) | collective-permute-done | bytes 131104 | tf_op jit(solution)/shard_map/cond/branch_2_fun/ppermute | solution.py:20
  85.4 1.6 %branch_2_fun.15 = bf16[2,128,256]{2,1,0:T(8,128)(2,1)S(1)} custom-call(s32[70]{0:T(128)S(1)} %get-tuple-element.243.meta, bf16[2,32,2048]{2,1,0:T(8,128)(2,1)S(1)} %get-tuple-element.259.rest_0_.rest_1_, bf16[2,32,2048]{2,1,0:T(8,128)(2,1)S(1)} %collective-permute-done.70.rest_1_.rest_2_, bf16[2,32,2048]{2,1,0:T(8,128)(2,1)S(1)} %collective-permute-done.71.rest_2_.rest_3_, ...), custom_call_target="tpu_custom_call" | custom-call | flops 268435456 | bytes 2097152 | tf_op jit(solution)/shard_map/cond/branch_2_fun/pallas_call | solution.py:247
  88.4 1.5 %collective-permute-start.80 = (bf16[2,128,256]{2,1,0:T(8,128)(2,1)S(1)}, bf16[2,128,256]{2,1,0:T(8,128)(2,1)S(1)}, u32[]{:S(2)}, u32[]{:S(2)}) collective-permute-start(bf16[2,128,256]{2,1,0:T(8,128)(2,1)S(1)} %add_convert_fusion.7.g1), channel_id=1, source_target_pairs={{0,2},{2,0},{1,3},{3,1},{4,6},{6,4},{5,7},{7,5},{8,10},{10,8},{9,1... | collective-permute-start | bytes 393224 | tf_op jit(solution)/shard_map/cond/branch_2_fun/ppermute | solution.py:20
  92.0 2.6 %branch_2_fun.19 = (bf16[128,2048]{1,0:T(8,128)(2,1)S(1)}, bf16[128,2048]{1,0:T(8,128)(2,1)S(1)}) custom-call(s32[70]{0:T(128)S(1)} %get-tuple-element.243.meta, bf16[4,128,256]{2,1,0:T(8,128)(2,1)S(1)} %get-tuple-element.281.rest_0_, bf16[2,32,2048]{2,1,0:T(8,128)(2,1)S(1)} %get-tuple-element.259.rest_0_.rest_1_, ...), custom_call_target="tpu_custom_call" | custom-call | flops 536870912 | bytes 3145728 | tf_op jit(solution)/shard_map/cond/branch_2_fun/pallas_call | solution.py:327
  97.7 9.5 %collective-permute-start.81 = (bf16[2,32,2048]{2,1,0:T(8,128)(2,1)S(1)}, bf16[2,32,2048]{2,1,0:T(8,128)(2,1)S(1)}, u32[]{:S(2)}, u32[]{:S(2)}) collective-permute-start(bf16[2,32,2048]{2,1,0:T(8,128)(2,1)S(1)} %get-tuple-element.269), channel_id=1, source_target_pairs={{4,0},{8,4},{12,8},{0,12},{5,1},{9,5},{13,9},{1,13},{6,2},{10,6},{... | collective-permute-start | bytes 786440 | tf_op jit(solution)/shard_map/cond/branch_2_fun/ppermute | solution.py:386
  108.5 3.8 %collective-permute-done.85.rest_6_ = bf16[2,32,2048]{2,1,0:T(8,128)(2,1)S(1)} collective-permute-done((bf16[2,32,2048]{2,1,0:T(8,128)(2,1)S(1)}, bf16[2,32,2048]{2,1,0:T(8,128)(2,1)S(1)}, u32[]{:S(2)}, u32[]{:S(2)}) %collective-permute-start.85) | collective-permute-done | bytes 262176 | tf_op jit(solution)/shard_map/cond/branch_2_fun/ppermute | solution.py:386
  112.3 2.6 %branch_2_fun.18 = (bf16[128,2048]{1,0:T(8,128)(2,1)S(1)}, bf16[128,2048]{1,0:T(8,128)(2,1)S(1)}) custom-call(s32[70]{0:T(128)S(1)} %get-tuple-element.243.meta, bf16[2,128,256]{2,1,0:T(8,128)(2,1)S(1)} %get-tuple-element.278.rest_0_, bf16[2,128,256]{2,1,0:T(8,128)(2,1)S(1)} %get-tuple-element.266.rest_1_, ...), custom_call_target="tpu_custom_call" | custom-call | flops 536870912 | bytes 3145728 | tf_op jit(solution)/shard_map/cond/branch_2_fun/pallas_call | solution.py:327
  115.5 18.1 %collective-permute-done.82.rest_2_ = bf16[2,32,2048]{2,1,0:T(8,128)(2,1)S(1)} collective-permute-done((bf16[2,32,2048]{2,1,0:T(8,128)(2,1)S(1)}, bf16[2,32,2048]{2,1,0:T(8,128)(2,1)S(1)}, u32[]{:S(2)}, u32[]{:S(2)}) %collective-permute-start.82) | collective-permute-done | bytes 262176 | tf_op jit(solution)/shard_map/cond/branch_2_fun/ppermute | solution.py:386
  137.9 9.8 %collective-permute-done.87 = bf16[4,32,2048]{2,1,0:T(8,128)(2,1)S(1)} collective-permute-done((bf16[4,32,2048]{2,1,0:T(8,128)(2,1)S(1)}, bf16[4,32,2048]{2,1,0:T(8,128)(2,1)S(1)}, u32[]{:S(2)}, u32[]{:S(2)}) %collective-permute-start.87) | collective-permute-done | bytes 524320 | tf_op jit(solution)/shard_map/cond/branch_2_fun/ppermute | solution.py:20
  (84 shorter events, 33.0 us)
Async XLA Ops:
  1.7 18.2 %collective-permute-start.140 = (bf16[4,32,2048]{2,1,0:T(8,128)(2,1)S(1)}, bf16[4,32,2048]{2,1,0:T(8,128)(2,1)S(1)}, u32[]{:S(2)}, u32[]{:S(2)}) collective-permute-start(bf16[4,32,2048]{2,1,0:T(8,128)(2,1)S(1)} %dynamic-slice_bitcast_fusion.1), channel_id=1, source_target_pairs={{0,2},{2,0},{1,3},{3,1},{4,6},{6,4},{5,7},{7,5},{8,10},{10,8},{9,1... | collective-permute-start | bytes 1572872 | tf_op jit(solution)/shard_map/ppermute | solution.py:20
  4.7 12.0 %collective-permute-start.139 = (s32[1,4,1]{1,2,0:T(1,128)S(1)}, s32[1,4,1]{1,2,0:T(1,128)S(1)}, u32[]{:S(2)}, u32[]{:S(2)}) collective-permute-start(s32[1,4,1]{1,2,0:T(1,128)S(1)} %copy-done.2), channel_id=1, source_target_pairs={{0,2},{2,0},{1,3},{3,1},{4,6},{6,4},{5,7},{7,5},{8,10},{10,8},{9,1... | collective-permute-start | bytes 56 | tf_op jit(solution)/shard_map/ppermute | solution.py:20
  6.2 16.0 %collective-permute-start.141 = (bf16[1,32,2048]{2,1,0:T(8,128)(2,1)S(1)}, bf16[1,32,2048]{2,1,0:T(8,128)(2,1)}, u32[]{:S(2)}, u32[]{:S(2)}) collective-permute-start(bf16[1,32,2048]{2,1,0:T(8,128)(2,1)S(1)} %get-tuple-element.379), channel_id=1, source_target_pairs={{0,4},{4,8},{8,12},{12,0},{1,5},{5,9},{9,13},{13,1},{2,6},{6,10},{... | collective-permute-start | bytes 393224 | tf_op jit(solution)/shard_map/ppermute | solution.py:386
  8.3 13.9 %collective-permute-start.142 = (bf16[1,32,2048]{2,1,0:T(8,128)(2,1)S(1)}, bf16[1,32,2048]{2,1,0:T(8,128)(2,1)}, u32[]{:S(2)}, u32[]{:S(2)}) collective-permute-start(bf16[1,32,2048]{2,1,0:T(8,128)(2,1)S(1)} %get-tuple-element.380), channel_id=1, source_target_pairs={{0,8},{4,12},{8,0},{12,4},{1,9},{5,13},{9,1},{13,5},{2,10},{6,14},... | collective-permute-start | bytes 393224 | tf_op jit(solution)/shard_map/ppermute | solution.py:386
  10.9 11.3 %collective-permute-start.143 = (bf16[1,32,2048]{2,1,0:T(8,128)(2,1)S(1)}, bf16[1,32,2048]{2,1,0:T(8,128)(2,1)}, u32[]{:S(2)}, u32[]{:S(2)}) collective-permute-start(bf16[1,32,2048]{2,1,0:T(8,128)(2,1)S(1)} %get-tuple-element.381), channel_id=1, source_target_pairs={{0,12},{4,0},{8,4},{12,8},{1,13},{5,1},{9,5},{13,9},{2,14},{6,2},{... | collective-permute-start | bytes 393224 | tf_op jit(solution)/shard_map/ppermute | solution.py:386
  22.5 15.2 %collective-permute-start.69 = (bf16[4,32,2048]{2,1,0:T(8,128)(2,1)S(1)}, bf16[4,32,2048]{2,1,0:T(8,128)(2,1)S(1)}, u32[]{:S(2)}, u32[]{:S(2)}) collective-permute-start(bf16[4,32,2048]{2,1,0:T(8,128)(2,1)S(1)} %get-tuple-element.257), channel_id=1, source_target_pairs={{0,2},{2,0},{1,3},{3,1},{4,6},{6,4},{5,7},{7,5},{8,10},{10,8},{9,1... | collective-permute-start | bytes 1572872 | tf_op jit(solution)/shard_map/cond/branch_2_fun/ppermute | solution.py:20
  24.3 24.5 %collective-permute-start.66 = (bf16[128,2048]{1,0:T(8,128)(2,1)}, bf16[128,2048]{1,0:T(8,128)(2,1)}, u32[]{:S(2)}, u32[]{:S(2)}) collective-permute-start(bf16[128,2048]{1,0:T(8,128)(2,1)} %get-tuple-element.254), channel_id=1, source_target_pairs={{0,2},{2,0},{1,3},{3,1},{4,6},{6,4},{5,7},{7,5},{8,10},{10,8},{9,1... | collective-permute-start | bytes 1572872 | tf_op jit(solution)/shard_map/cond/branch_2_fun/ppermute | solution.py:20
  24.5 39.0 %collective-permute-start.73 = (bf16[128,2048]{1,0:T(8,128)(2,1)}, bf16[128,2048]{1,0:T(8,128)(2,1)}, u32[]{:S(2)}, u32[]{:S(2)}) collective-permute-start(bf16[128,2048]{1,0:T(8,128)(2,1)} %get-tuple-element.264), channel_id=1, source_target_pairs={{0,2},{2,0},{1,3},{3,1},{4,6},{6,4},{5,7},{7,5},{8,10},{10,8},{9,1... | collective-permute-start | bytes 1572872 | tf_op jit(solution)/shard_map/cond/branch_2_fun/ppermute | solution.py:20
  26.3 7.0 %collective-permute-start.60 = (bf16[1,32,2048]{2,1,0:T(8,128)(2,1)S(1)}, bf16[1,32,2048]{2,1,0:T(8,128)(2,1)S(1)}, u32[]{:S(2)}, u32[]{:S(2)}) collective-permute-start(bf16[1,32,2048]{2,1,0:T(8,128)(2,1)S(1)} %get-tuple-element.249), channel_id=1, source_target_pairs={{0,4},{4,8},{8,12},{12,0},{1,5},{5,9},{9,13},{13,1},{2,6},{6,10},{... | collective-permute-start | bytes 393224 | tf_op jit(solution)/shard_map/cond/branch_2_fun/ppermute | solution.py:386
  27.9 6.4 %collective-permute-start.62 = (bf16[1,32,2048]{2,1,0:T(8,128)(2,1)S(1)}, bf16[1,32,2048]{2,1,0:T(8,128)(2,1)S(1)}, u32[]{:S(2)}, u32[]{:S(2)}) collective-permute-start(bf16[1,32,2048]{2,1,0:T(8,128)(2,1)S(1)} %get-tuple-element.251), channel_id=1, source_target_pairs={{0,12},{4,0},{8,4},{12,8},{1,13},{5,1},{9,5},{13,9},{2,14},{6,2},{... | collective-permute-start | bytes 393224 | tf_op jit(solution)/shard_map/cond/branch_2_fun/ppermute | solution.py:386
  33.3 23.4 %collective-permute-start.65 = (bf16[2,32,2048]{2,1,0:T(8,128)(2,1)S(1)}, bf16[2,32,2048]{2,1,0:T(8,128)(2,1)S(1)}, u32[]{:S(2)}, u32[]{:S(2)}) collective-permute-start(bf16[2,32,2048]{2,1,0:T(8,128)(2,1)S(1)} %get-tuple-element.252.rest_8_.rest_10_), channel_id=1, source_target_pairs={{12,8},{13,9},{14,10},{15,11},{28,24},{29,25},{30,26},{31,27}} | collective-permute-start | bytes 786440 | tf_op jit(solution)/shard_map/cond/branch_2_fun/ppermute | solution.py:386
  34.2 26.5 %collective-permute-start.64 = (bf16[2,32,2048]{2,1,0:T(8,128)(2,1)S(1)}, bf16[2,32,2048]{2,1,0:T(8,128)(2,1)S(1)}, u32[]{:S(2)}, u32[]{:S(2)}) collective-permute-start(bf16[2,32,2048]{2,1,0:T(8,128)(2,1)S(1)} %get-tuple-element.252.rest_8_.rest_10_), channel_id=1, source_target_pairs={{0,8},{1,9},{2,10},{3,11},{16,24},{17,25},{18,26},{19,27}} | collective-permute-start | bytes 786440 | tf_op jit(solution)/shard_map/cond/branch_2_fun/ppermute | solution.py:386
  37.7 23.8 %collective-permute-start.63 = (bf16[2,32,2048]{2,1,0:T(8,128)(2,1)S(1)}, bf16[2,32,2048]{2,1,0:T(8,128)(2,1)S(1)}, u32[]{:S(2)}, u32[]{:S(2)}) collective-permute-start(bf16[2,32,2048]{2,1,0:T(8,128)(2,1)S(1)} %get-tuple-element.252.rest_8_.rest_10_), channel_id=1, source_target_pairs={{4,8},{5,9},{6,10},{7,11},{20,24},{21,25},{22,26},{23,27}} | collective-permute-start | bytes 786440 | tf_op jit(solution)/shard_map/cond/branch_2_fun/ppermute | solution.py:386
  48.7 7.3 %collective-permute-start.61 = (bf16[1,32,2048]{2,1,0:T(8,128)(2,1)S(1)}, bf16[1,32,2048]{2,1,0:T(8,128)(2,1)S(1)}, u32[]{:S(2)}, u32[]{:S(2)}) collective-permute-start(bf16[1,32,2048]{2,1,0:T(8,128)(2,1)S(1)} %copy-done.35), channel_id=1, source_target_pairs={{0,8},{4,12},{8,0},{12,4},{1,9},{5,13},{9,1},{13,5},{2,10},{6,14},... | collective-permute-start | bytes 393224 | tf_op jit(solution)/shard_map/cond/branch_2_fun/ppermute | solution.py:386
  56.0 10.3 %collective-permute-start.76 = (bf16[2,32,2048]{2,1,0:T(8,128)(2,1)S(1)}, bf16[2,32,2048]{2,1,0:T(8,128)(2,1)S(1)}, u32[]{:S(2)}, u32[]{:S(2)}) collective-permute-start(bf16[2,32,2048]{2,1,0:T(8,128)(2,1)S(1)} %get-tuple-element.265.rest_0_.rest_5_), channel_id=1, source_target_pairs={{12,8},{13,9},{14,10},{15,11},{28,24},{29,25},{30,26},{31,27}} | collective-permute-start | bytes 786440 | tf_op jit(solution)/shard_map/cond/branch_2_fun/ppermute | solution.py:386
  56.7 10.1 %collective-permute-start.75 = (bf16[2,32,2048]{2,1,0:T(8,128)(2,1)S(1)}, bf16[2,32,2048]{2,1,0:T(8,128)(2,1)S(1)}, u32[]{:S(2)}, u32[]{:S(2)}) collective-permute-start(bf16[2,32,2048]{2,1,0:T(8,128)(2,1)S(1)} %get-tuple-element.265.rest_0_.rest_5_), channel_id=1, source_target_pairs={{0,8},{1,9},{2,10},{3,11},{16,24},{17,25},{18,26},{19,27}} | collective-permute-start | bytes 786440 | tf_op jit(solution)/shard_map/cond/branch_2_fun/ppermute | solution.py:386
  60.8 8.4 %collective-permute-start.74 = (bf16[2,32,2048]{2,1,0:T(8,128)(2,1)S(1)}, bf16[2,32,2048]{2,1,0:T(8,128)(2,1)S(1)}, u32[]{:S(2)}, u32[]{:S(2)}) collective-permute-start(bf16[2,32,2048]{2,1,0:T(8,128)(2,1)S(1)} %get-tuple-element.265.rest_0_.rest_5_), channel_id=1, source_target_pairs={{4,8},{5,9},{6,10},{7,11},{20,24},{21,25},{22,26},{23,27}} | collective-permute-start | bytes 786440 | tf_op jit(solution)/shard_map/cond/branch_2_fun/ppermute | solution.py:386
  63.4 7.4 %collective-permute-start.67 = (bf16[4,128,256]{2,1,0:T(8,128)(2,1)S(1)}, bf16[4,128,256]{2,1,0:T(8,128)(2,1)S(1)}, u32[]{:S(2)}, u32[]{:S(2)}) collective-permute-start(bf16[4,128,256]{2,1,0:T(8,128)(2,1)S(1)} %branch_2_fun.10), channel_id=1, source_target_pairs={{0,1},{1,0},{2,3},{3,2},{4,5},{5,4},{6,7},{7,6},{8,9},{9,8},{10,11... | collective-permute-start | bytes 786440 | tf_op jit(solution)/shard_map/cond/branch_2_fun/ppermute | solution.py:20
  63.5 20.5 %collective-permute-start.70 = (bf16[2,32,2048]{2,1,0:T(8,128)(2,1)S(1)}, bf16[2,32,2048]{2,1,0:T(8,128)(2,1)S(1)}, u32[]{:S(2)}, u32[]{:S(2)}) collective-permute-start(bf16[2,32,2048]{2,1,0:T(8,128)(2,1)S(1)} %get-tuple-element.260), channel_id=1, source_target_pairs={{0,4},{4,8},{8,12},{12,0},{1,5},{5,9},{9,13},{13,1},{2,6},{6,10},{... | collective-permute-start | bytes 786440 | tf_op jit(solution)/shard_map/cond/branch_2_fun/ppermute | solution.py:386
  66.3 19.0 %collective-permute-start.71 = (bf16[2,32,2048]{2,1,0:T(8,128)(2,1)S(1)}, bf16[2,32,2048]{2,1,0:T(8,128)(2,1)S(1)}, u32[]{:S(2)}, u32[]{:S(2)}) collective-permute-start(bf16[2,32,2048]{2,1,0:T(8,128)(2,1)S(1)} %get-tuple-element.261), channel_id=1, source_target_pairs={{0,8},{4,12},{8,0},{12,4},{1,9},{5,13},{9,1},{13,5},{2,10},{6,14},... | collective-permute-start | bytes 786440 | tf_op jit(solution)/shard_map/cond/branch_2_fun/ppermute | solution.py:386
  66.8 18.6 %collective-permute-start.72 = (bf16[2,32,2048]{2,1,0:T(8,128)(2,1)S(1)}, bf16[2,32,2048]{2,1,0:T(8,128)(2,1)S(1)}, u32[]{:S(2)}, u32[]{:S(2)}) collective-permute-start(bf16[2,32,2048]{2,1,0:T(8,128)(2,1)S(1)} %get-tuple-element.262), channel_id=1, source_target_pairs={{0,12},{4,0},{8,4},{12,8},{1,13},{5,1},{9,5},{13,9},{2,14},{6,2},{... | collective-permute-start | bytes 786440 | tf_op jit(solution)/shard_map/cond/branch_2_fun/ppermute | solution.py:386
  70.9 9.2 %collective-permute-start.68 = (bf16[4,128,256]{2,1,0:T(8,128)(2,1)S(1)}, bf16[4,128,256]{2,1,0:T(8,128)(2,1)S(1)}, u32[]{:S(2)}, u32[]{:S(2)}) collective-permute-start(bf16[4,128,256]{2,1,0:T(8,128)(2,1)S(1)} %add_convert_fusion.6.h1), channel_id=1, source_target_pairs={{0,2},{2,0},{1,3},{3,1},{4,6},{6,4},{5,7},{7,5},{8,10},{10,8},{9,1... | collective-permute-start | bytes 786440 | tf_op jit(solution)/shard_map/cond/branch_2_fun/ppermute | solution.py:20
  72.5 10.0 %collective-permute-start.78 = (bf16[2,128,256]{2,1,0:T(8,128)(2,1)S(1)}, bf16[2,128,256]{2,1,0:T(8,128)(2,1)S(1)}, u32[]{:S(2)}, u32[]{:S(2)}) collective-permute-start(bf16[2,128,256]{2,1,0:T(8,128)(2,1)S(1)} %add_convert_fusion.8.g1), channel_id=1, source_target_pairs={{0,2},{2,0},{1,3},{3,1},{4,6},{6,4},{5,7},{7,5},{8,10},{10,8},{9,1... | collective-permute-start | bytes 393224 | tf_op jit(solution)/shard_map/cond/branch_2_fun/ppermute | solution.py:20
  90.0 17.2 %collective-permute-start.84 = (bf16[2,32,2048]{2,1,0:T(8,128)(2,1)S(1)}, bf16[2,32,2048]{2,1,0:T(8,128)(2,1)S(1)}, u32[]{:S(2)}, u32[]{:S(2)}) collective-permute-start(bf16[2,32,2048]{2,1,0:T(8,128)(2,1)S(1)} %get-tuple-element.273), channel_id=1, source_target_pairs={{8,4},{9,5},{10,6},{11,7},{24,20},{25,21},{26,22},{27,23}} | collective-permute-start | bytes 786440 | tf_op jit(solution)/shard_map/cond/branch_2_fun/ppermute | solution.py:386
  90.7 21.6 %collective-permute-start.85 = (bf16[2,32,2048]{2,1,0:T(8,128)(2,1)S(1)}, bf16[2,32,2048]{2,1,0:T(8,128)(2,1)S(1)}, u32[]{:S(2)}, u32[]{:S(2)}) collective-permute-start(bf16[2,32,2048]{2,1,0:T(8,128)(2,1)S(1)} %get-tuple-element.274), channel_id=1, source_target_pairs={{8,0},{9,1},{10,2},{11,3},{24,16},{25,17},{26,18},{27,19}} | collective-permute-start | bytes 786440 | tf_op jit(solution)/shard_map/cond/branch_2_fun/ppermute | solution.py:386
  94.6 40.9 %collective-permute-start.89 = (bf16[128,2048]{1,0:T(8,128)(2,1)S(1)}, bf16[128,2048]{1,0:T(8,128)(2,1)S(1)}, u32[]{:S(2)}, u32[]{:S(2)}) collective-permute-start(bf16[128,2048]{1,0:T(8,128)(2,1)S(1)} %get-tuple-element.284), channel_id=1, source_target_pairs={{0,2},{2,0},{1,3},{3,1},{4,6},{6,4},{5,7},{7,5},{8,10},{10,8},{9,1... | collective-permute-start | bytes 1572872 | tf_op jit(solution)/shard_map/cond/branch_2_fun/ppermute | solution.py:20
  95.5 19.4 %collective-permute-start.86 = (bf16[2,32,2048]{2,1,0:T(8,128)(2,1)S(1)}, bf16[2,32,2048]{2,1,0:T(8,128)(2,1)S(1)}, u32[]{:S(2)}, u32[]{:S(2)}) collective-permute-start(bf16[2,32,2048]{2,1,0:T(8,128)(2,1)S(1)} %get-tuple-element.275), channel_id=1, source_target_pairs={{8,12},{9,13},{10,14},{11,15},{24,28},{25,29},{26,30},{27,31}} | collective-permute-start | bytes 786440 | tf_op jit(solution)/shard_map/cond/branch_2_fun/ppermute | solution.py:386
  97.7 17.8 %collective-permute-start.81 = (bf16[2,32,2048]{2,1,0:T(8,128)(2,1)S(1)}, bf16[2,32,2048]{2,1,0:T(8,128)(2,1)S(1)}, u32[]{:S(2)}, u32[]{:S(2)}) collective-permute-start(bf16[2,32,2048]{2,1,0:T(8,128)(2,1)S(1)} %get-tuple-element.269), channel_id=1, source_target_pairs={{4,0},{8,4},{12,8},{0,12},{5,1},{9,5},{13,9},{1,13},{6,2},{10,6},{... | collective-permute-start | bytes 786440 | tf_op jit(solution)/shard_map/cond/branch_2_fun/ppermute | solution.py:386
  107.2 26.4 %collective-permute-start.82 = (bf16[2,32,2048]{2,1,0:T(8,128)(2,1)S(1)}, bf16[2,32,2048]{2,1,0:T(8,128)(2,1)S(1)}, u32[]{:S(2)}, u32[]{:S(2)}) collective-permute-start(bf16[2,32,2048]{2,1,0:T(8,128)(2,1)S(1)} %get-tuple-element.270), channel_id=1, source_target_pairs={{8,0},{12,4},{0,8},{4,12},{9,1},{13,5},{1,9},{5,13},{10,2},{14,6},... | collective-permute-start | bytes 786440 | tf_op jit(solution)/shard_map/cond/branch_2_fun/ppermute | solution.py:386
  112.3 21.4 %collective-permute-start.83 = (bf16[2,32,2048]{2,1,0:T(8,128)(2,1)S(1)}, bf16[2,32,2048]{2,1,0:T(8,128)(2,1)S(1)}, u32[]{:S(2)}, u32[]{:S(2)}) collective-permute-start(bf16[2,32,2048]{2,1,0:T(8,128)(2,1)S(1)} %get-tuple-element.271), channel_id=1, source_target_pairs={{12,0},{0,4},{4,8},{8,12},{13,1},{1,5},{5,9},{9,13},{14,2},{2,6},{... | collective-permute-start | bytes 786440 | tf_op jit(solution)/shard_map/cond/branch_2_fun/ppermute | solution.py:386
  114.9 21.8 %collective-permute-start.88 = (bf16[128,2048]{1,0:T(8,128)(2,1)S(1)}, bf16[128,2048]{1,0:T(8,128)(2,1)S(1)}, u32[]{:S(2)}, u32[]{:S(2)}) collective-permute-start(bf16[128,2048]{1,0:T(8,128)(2,1)S(1)} %get-tuple-element.280), channel_id=1, source_target_pairs={{0,2},{2,0},{1,3},{3,1},{4,6},{6,4},{5,7},{7,5},{8,10},{10,8},{9,1... | collective-permute-start | bytes 1572872 | tf_op jit(solution)/shard_map/cond/branch_2_fun/ppermute | solution.py:20
  134.9 12.9 %collective-permute-start.87 = (bf16[4,32,2048]{2,1,0:T(8,128)(2,1)S(1)}, bf16[4,32,2048]{2,1,0:T(8,128)(2,1)S(1)}, u32[]{:S(2)}, u32[]{:S(2)}) collective-permute-start(bf16[4,32,2048]{2,1,0:T(8,128)(2,1)S(1)} %get-tuple-element.277), channel_id=1, source_target_pairs={{0,2},{2,0},{1,3},{3,1},{4,6},{6,4},{5,7},{7,5},{8,10},{10,8},{9,1... | collective-permute-start | bytes 1572872 | tf_op jit(solution)/shard_map/cond/branch_2_fun/ppermute | solution.py:20
  (13 other events, 83.5 us)

commit v4 on v3

--- a/solution.py
+++ b/solution.py
@@ -262,11 +262,12 @@
         squared[s] = (h * h).astype(BF16)
 
 
-def back_kernel(first, count, owners, meta, positive, g1, g2, up, grad_hidden, *outs):
-    n, m = g1.shape[1], g1.shape[2]
+def back_kernel(first, count, owners, parts, meta, positive, *rest):
+    g, up, grad_hidden, outs = rest[:parts], rest[parts], rest[parts + 1], rest[parts + 2 :]
+    n, m = g[0].shape[1], g[0].shape[2]
     rows = n // owners
     for s in range(count):
-        grad_act = g1[s].astype(F32) + g2[s].astype(F32)
+        grad_act = sum(part[s].astype(F32) for part in g)
         grad_hidden[s] = (2.0 * positive[first + s] * grad_act).astype(BF16)
     step = 512
 
@@ -286,10 +287,10 @@
     count, n, m = g[0].shape
     width = up.shape[1]
     outs = call(
-        functools.partial(back_kernel, first, count, owners),
+        functools.partial(back_kernel, first, count, owners, len(g)),
         [jax.ShapeDtypeStruct((count, n, m), BF16)]
         + [jax.ShapeDtypeStruct((count, n // owners, width), BF16)] * owners,
-        4,
+        2 + len(g),
         flops=2 * count * n * m * width,
         moved=2 * (count * n + m) * width,
     )(meta, positive, *g, up)
@@ -437,17 +438,23 @@
             2,
             moved=8 * hidden.size,
         )(meta, hidden, swap(hidden, "dp"))
-        grad_hidden, home = [None] * len(cot), [None] * len(cot)
+        grad_hidden, home, sent_back = [None] * len(cot), [None] * len(cot), ()
         for i in reversed(range(len(cot))):
             first, _, each = cot_groups[i]
-            grad_act = over_subs(product(meta, [cot[i]], down, False))
-            sums = (grad_act, swap(grad_act, "dp"))
-            grad_hidden[i], out = back(meta, positive, sums, up, first, owners)
+            grad_act = product(meta, [cot[i]], down, False)
+            if i == 0:
+                crossed = lax.ppermute(grad_act, ("dp", "sub"), [(0, 3), (3, 0), (1, 2), (2, 1)])
+                sums = (grad_act, swap(grad_act, "dp"), crossed, swap(grad_act, "sub"))
+            else:
+                grad_act = over_subs(grad_act)
+                sums = (grad_act, swap(grad_act, "dp"))
+            grad_hidden[i], out = back(meta, after(positive, sent_back), sums, up, first, owners)
             perm_of = forth if each else extra_forth
             home[i] = move(out, lambda k: back_of(perm_of(k)))
+            sent_back = home[i][1]
             down = after(down, grad_hidden[i])
-        down_grad, down_other = weights(meta, [squared], cot, False)
-        down_got = swap(after(down_other, sums[1]), "dp")
+        down_grad, down_other = weights(meta, [after(squared, *grad_hidden)], cot, False)
+        down_got = swap(down_other, "dp")
         up_grad, up_other = weights(meta, grad_hidden, tok, fast)
         up_got = swap(up_other, "dp")
         home = [piece for group in home for piece in group]

time: 152 us -> 152 us (level)
    ppermute x0 -> x1, waiting for transfers between devices: none -> 1.84 us  [run(): lax.ppermute(grad_act, ('dp', 'sub'), [(0, 3), (3, 0), (1, 2), (2, 1)])]
  transfers between devices with their start and end apart: 35 -> 36, of which waited for: 12 -> 14; matrix products, arithmetic and copies ran while one was open for 7% -> 7% of each run, Pallas kernels for 13% -> 14%
where the time goes in v4:
time: 152 us; the launch traced here: 150 us
  waiting for transfers between devices  59.4 us (39%)
  starting transfers between devices  54.2 us (36%)
  Pallas kernels  21.5 us (14%)
  other arithmetic  6.91 us (5%)
  local copies, waits for them, and re-layouts  5.87 us (4%)
    ppermute x21, starting transfers between devices, move(): lax.ppermute(pieces[k], 'tensor', perm_of(k))  40.1 us
    ppermute x21, waiting for transfers between devices, move(): lax.ppermute(pieces[k], 'tensor', perm_of(k))  29 us
    ppermute x14, waiting for transfers between devices, swap(): return lax.ppermute(x, axis, [(0, 1), (1, 0)])  28.5 us
    ppermute x14, starting transfers between devices, swap(): return lax.ppermute(x, axis, [(0, 1), (1, 0)])  13.2 us
    select_n x5, other arithmetic, ordered(): jnp.where(side == 0, jnp.concatenate([mine, other], axis), jnp.concatenat...  6.81 us
    pallas_call x2, Pallas kernels, weights(): call(functools.partial(weights_kernel, owners, act_counts, counts, moved)...  5.2 us
    pallas_call x3, Pallas kernels, product(): call(functools.partial(product_kernel, counts, owners, moved), [jax.Shape...  5.2 us
    pallas_call x2, Pallas kernels, dispatch(): call(kernel, outs, 2, moved=4 * sum(counts) * rows * width)(meta, keep, got)  3.33 us
  transfers between devices with their start and end apart: 36, of which 14 were waited for; matrix products, arithmetic and copies ran while one was open for 7% of the time, Pallas kernels for 14%

profile of v4, /device:TPU:0, one launch (start us, length us, event | category | flops | bytes accessed | tf_op | source)
XLA Modules:
  0.0 149.8 jit_solution(4373770060079009551)
XLA Ops:
  1.7 3.0 %collective-permute-start.145 = (bf16[4,32,2048]{2,1,0:T(8,128)(2,1)S(1)}, bf16[4,32,2048]{2,1,0:T(8,128)(2,1)S(1)}, u32[]{:S(2)}, u32[]{:S(2)}) collective-permute-start(bf16[4,32,2048]{2,1,0:T(8,128)(2,1)S(1)} %dynamic-slice_bitcast_fusion.1), channel_id=1, source_target_pairs={{0,2},{2,0},{1,3},{3,1},{4,6},{6,4},{5,7},{7,5},{8,10},{10,8},{9,1... | collective-permute-start | bytes 1572872 | tf_op jit(solution)/shard_map/ppermute | solution.py:20
  6.2 2.1 %collective-permute-start.146 = (bf16[1,32,2048]{2,1,0:T(8,128)(2,1)S(1)}, bf16[1,32,2048]{2,1,0:T(8,128)(2,1)}, u32[]{:S(2)}, u32[]{:S(2)}) collective-permute-start(bf16[1,32,2048]{2,1,0:T(8,128)(2,1)S(1)} %get-tuple-element.383), channel_id=1, source_target_pairs={{0,4},{4,8},{8,12},{12,0},{1,5},{5,9},{9,13},{13,1},{2,6},{6,10},{... | collective-permute-start | bytes 393224 | tf_op jit(solution)/shard_map/ppermute | solution.py:387
  8.3 2.6 %collective-permute-start.147 = (bf16[1,32,2048]{2,1,0:T(8,128)(2,1)S(1)}, bf16[1,32,2048]{2,1,0:T(8,128)(2,1)}, u32[]{:S(2)}, u32[]{:S(2)}) collective-permute-start(bf16[1,32,2048]{2,1,0:T(8,128)(2,1)S(1)} %get-tuple-element.384), channel_id=1, source_target_pairs={{0,8},{4,12},{8,0},{12,4},{1,9},{5,13},{9,1},{13,5},{2,10},{6,14},... | collective-permute-start | bytes 393224 | tf_op jit(solution)/shard_map/ppermute | solution.py:387
  12.2 2.8 %constant_dynamic-slice_fusion = (bf16[128,2048]{1,0:T(8,128)(2,1)S(1)}, bf16[128,2048]{1,0:T(8,128)(2,1)}, bf16[128,2048]{1,0:T(8,128)(2,1)}, bf16[128,2048]{1,0:T(8,128)(2,1)}) fusion(bf16[128,4096]{1,0:T(8,128)(2,1)} %param.13, s32[]{:T(128)S(6)} %select_n.182, s32[]{:T(128)S(6)} %select_n.181, bf16[128,4096]{1,0:T(8,128)(2,1)} %param.12), kind=kLoop, calls=%fused_computation.36 | loop fusion | bytes 4194312 | tf_op jit(solution)/shard_map/dynamic_slice | solution.py:95
  20.0 2.3 %shard_map.92 = (bf16[1,32,2048]{2,1,0:T(8,128)(2,1)}, bf16[1,32,2048]{2,1,0:T(8,128)(2,1)S(1)}, bf16[1,32,2048]{2,1,0:T(8,128)(2,1)}, bf16[1,32,2048]{2,1,0:T(8,128)(2,1)S(1)}, bf16[2,32,2048]{2,1,0:T(8,128)(2,1)S(1)}) custom-call(s32[70]{0:T(128)S(1)} %shard_map.91.meta, bf16[4,32,4096]{2,1,0:T(8,128)(2,1)} %bitcast.20.keep, ...), custom_call_target="tpu_custom_call" | custom-call | bytes 1572864 | tf_op jit(solution)/shard_map/pallas_call | solution.py:196
  22.3 127.6 %conditional.1 = (bf16[1,4,32,4096]{3,2,1,0:T(8,128)(2,1)}, bf16[128,4096]{1,0:T(8,128)(2,1)}, bf16[128,4096]{1,0:T(8,128)(2,1)}) conditional(s32[]{:T(128)} %bitcast.19, (s32[]{:T(128)}, bf16[1,32,2048]{2,1,0:T(8,128)(2,1)S(1)}, bf16[1,32,2048]{2,1,0:T(8,128)(2,1)}, bf16[1,32,2048]{2,1,0:T(8,128)(2,1)S(1)}, ...), branch_computations={%region_0.1_spmd, %region_1.2_spmd, %region_2.3_spmd, %region_3.4_... | conditional | flops 4050911232 | bytes 118621240 | solution.py:468
  22.5 1.8 %collective-permute-start.71 = (bf16[4,32,2048]{2,1,0:T(8,128)(2,1)S(1)}, bf16[4,32,2048]{2,1,0:T(8,128)(2,1)S(1)}, u32[]{:S(2)}, u32[]{:S(2)}) collective-permute-start(bf16[4,32,2048]{2,1,0:T(8,128)(2,1)S(1)} %get-tuple-element.259), channel_id=1, source_target_pairs={{0,2},{2,0},{1,3},{3,1},{4,6},{6,4},{5,7},{7,5},{8,10},{10,8},{9,1... | collective-permute-start | bytes 1572872 | tf_op jit(solution)/shard_map/cond/branch_2_fun/ppermute | solution.py:20
  24.6 1.7 %collective-permute-start.75 = (bf16[128,2048]{1,0:T(8,128)(2,1)}, bf16[128,2048]{1,0:T(8,128)(2,1)}, u32[]{:S(2)}, u32[]{:S(2)}) collective-permute-start(bf16[128,2048]{1,0:T(8,128)(2,1)} %get-tuple-element.263), channel_id=1, source_target_pairs={{0,2},{2,0},{1,3},{3,1},{4,6},{6,4},{5,7},{7,5},{8,10},{10,8},{9,1... | collective-permute-start | bytes 1572872 | tf_op jit(solution)/shard_map/cond/branch_2_fun/ppermute | solution.py:20
  27.9 2.2 %collective-permute-start.64 = (bf16[1,32,2048]{2,1,0:T(8,128)(2,1)S(1)}, bf16[1,32,2048]{2,1,0:T(8,128)(2,1)S(1)}, u32[]{:S(2)}, u32[]{:S(2)}) collective-permute-start(bf16[1,32,2048]{2,1,0:T(8,128)(2,1)S(1)} %get-tuple-element.253), channel_id=1, source_target_pairs={{0,12},{4,0},{8,4},{12,8},{1,13},{5,1},{9,5},{13,9},{2,14},{6,2},{... | collective-permute-start | bytes 393224 | tf_op jit(solution)/shard_map/cond/branch_2_fun/ppermute | solution.py:387
  30.1 3.2 %collective-permute-done.62.rest_5_.rest_7_ = bf16[1,32,2048]{2,1,0:T(8,128)(2,1)S(1)} collective-permute-done((bf16[1,32,2048]{2,1,0:T(8,128)(2,1)S(1)}, bf16[1,32,2048]{2,1,0:T(8,128)(2,1)S(1)}, u32[]{:S(2)}, u32[]{:S(2)}) %collective-permute-start.62) | collective-permute-done | bytes 131104 | tf_op jit(solution)/shard_map/cond/branch_2_fun/ppermute | solution.py:387
  34.2 3.4 %collective-permute-start.66 = (bf16[2,32,2048]{2,1,0:T(8,128)(2,1)S(1)}, bf16[2,32,2048]{2,1,0:T(8,128)(2,1)S(1)}, u32[]{:S(2)}, u32[]{:S(2)}) collective-permute-start(bf16[2,32,2048]{2,1,0:T(8,128)(2,1)S(1)} %get-tuple-element.254.rest_8_.rest_10_), channel_id=1, source_target_pairs={{0,8},{1,9},{2,10},{3,11},{16,24},{17,25},{18,26},{19,27}} | collective-permute-start | bytes 786440 | tf_op jit(solution)/shard_map/cond/branch_2_fun/ppermute | solution.py:387
  39.4 9.3 %collective-permute-done.68 = bf16[128,2048]{1,0:T(8,128)(2,1)} collective-permute-done((bf16[128,2048]{1,0:T(8,128)(2,1)}, bf16[128,2048]{1,0:T(8,128)(2,1)}, u32[]{:S(2)}, u32[]{:S(2)}) %collective-permute-start.68) | collective-permute-done | bytes 524320 | tf_op jit(solution)/shard_map/cond/branch_2_fun/ppermute | solution.py:20
  48.7 2.8 %collective-permute-start.63 = (bf16[1,32,2048]{2,1,0:T(8,128)(2,1)S(1)}, bf16[1,32,2048]{2,1,0:T(8,128)(2,1)S(1)}, u32[]{:S(2)}, u32[]{:S(2)}) collective-permute-start(bf16[1,32,2048]{2,1,0:T(8,128)(2,1)S(1)} %copy-done.34), channel_id=1, source_target_pairs={{0,8},{4,12},{8,0},{12,4},{1,9},{5,13},{9,1},{13,5},{2,10},{6,14},... | collective-permute-start | bytes 393224 | tf_op jit(solution)/shard_map/cond/branch_2_fun/ppermute | solution.py:387
  51.6 1.6 %maximum_select_fusion.10.rest_12_.rest_2_.rest_4_ = bf16[256,2048]{1,0:T(8,128)(2,1)S(1)} fusion(bf16[128,2048]{1,0:T(8,128)(2,1)} %collective-permute-done.68, bf16[128,2048]{1,0:T(8,128)(2,1)S(1)} %copy-done.9, pred[]{:T(512)S(6)} %eq.12), kind=kLoop, calls=%fused_computation.14 | loop fusion | flops 4718592 | bytes 2097153 | tf_op jit(solution)/shard_map/cond/branch_2_fun/jit(_where)/select_n | solution.py:24
  53.2 2.8 %collective-permute-done.63.rest_6_.rest_8_ = bf16[1,32,2048]{2,1,0:T(8,128)(2,1)S(1)} collective-permute-done((bf16[1,32,2048]{2,1,0:T(8,128)(2,1)S(1)}, bf16[1,32,2048]{2,1,0:T(8,128)(2,1)S(1)}, u32[]{:S(2)}, u32[]{:S(2)}) %collective-permute-start.63) | collective-permute-done | bytes 131104 | tf_op jit(solution)/shard_map/cond/branch_2_fun/ppermute | solution.py:387
  56.7 4.1 %collective-permute-start.73 = (bf16[2,32,2048]{2,1,0:T(8,128)(2,1)S(1)}, bf16[2,32,2048]{2,1,0:T(8,128)(2,1)S(1)}, u32[]{:S(2)}, u32[]{:S(2)}) collective-permute-start(bf16[2,32,2048]{2,1,0:T(8,128)(2,1)S(1)} %get-tuple-element.261.rest_0_.rest_5_), channel_id=1, source_target_pairs={{0,8},{1,9},{2,10},{3,11},{16,24},{17,25},{18,26},{19,27}} | collective-permute-start | bytes 786440 | tf_op jit(solution)/shard_map/cond/branch_2_fun/ppermute | solution.py:387
  61.5 1.9 %branch_2_fun.10 = bf16[4,128,256]{2,1,0:T(8,128)(2,1)S(1)} custom-call(s32[70]{0:T(128)S(1)} %get-tuple-element.245.meta, bf16[1,32,2048]{2,1,0:T(8,128)(2,1)S(1)} %get-tuple-element.246.rest_0_.rest_2_, bf16[1,32,2048]{2,1,0:T(8,128)(2,1)S(1)} %copy-done.14, bf16[1,32,2048]{2,1,0:T(8,128)(2,1)S(1)} %copy-done.18, bf16[1,32,2048]{2,1,0:T(8,128)(2,1)S(1)} %copy-done.22, ...), custom_call_target="tpu_custom_call" | custom-call | flops 536870912 | bytes 3145728 | tf_op jit(solution)/shard_map/cond/branch_2_fun/pallas_call | solution.py:247
  66.8 1.6 %branch_2_fun.13 = bf16[2,128,256]{2,1,0:T(8,128)(2,1)S(1)} custom-call(s32[70]{0:T(128)S(1)} %get-tuple-element.245.meta, bf16[2,32,2048]{2,1,0:T(8,128)(2,1)S(1)} %get-tuple-element.261.rest_0_.rest_5_, bf16[2,32,2048]{2,1,0:T(8,128)(2,1)S(1)} %collective-permute-done.72.rest_1_.rest_6_, bf16[2,32,2048]{2,1,0:T(8,128)(2,1)S(1)} %collective-permute-done.73.rest_2_.rest_7_, ...), custom_call_target="tpu_custom_call" | custom-call | flops 268435456 | bytes 2097152 | tf_op jit(solution)/shard_map/cond/branch_2_fun/pallas_call | solution.py:247
  71.4 2.4 %collective-permute-start.81 = (bf16[2,32,2048]{2,1,0:T(8,128)(2,1)S(1)}, bf16[2,32,2048]{2,1,0:T(8,128)(2,1)S(1)}, u32[]{:S(2)}, u32[]{:S(2)}) collective-permute-start(bf16[2,32,2048]{2,1,0:T(8,128)(2,1)S(1)} %get-tuple-element.269), channel_id=1, source_target_pairs={{0,12},{4,0},{8,4},{12,8},{1,13},{5,1},{9,5},{13,9},{2,14},{6,2},{... | collective-permute-start | bytes 786440 | tf_op jit(solution)/shard_map/cond/branch_2_fun/ppermute | solution.py:387
  73.7 4.0 %collective-permute-done.70.h2 = bf16[4,128,256]{2,1,0:T(8,128)(2,1)S(1)} collective-permute-done((bf16[4,128,256]{2,1,0:T(8,128)(2,1)S(1)}, bf16[4,128,256]{2,1,0:T(8,128)(2,1)S(1)}, u32[]{:S(2)}, u32[]{:S(2)}) %collective-permute-start.70) | collective-permute-done | bytes 262176 | tf_op jit(solution)/shard_map/cond/branch_2_fun/ppermute | solution.py:20
  78.4 1.7 %collective-permute-done.77.rest_1_ = bf16[2,128,256]{2,1,0:T(8,128)(2,1)S(1)} collective-permute-done((bf16[2,128,256]{2,1,0:T(8,128)(2,1)S(1)}, bf16[2,128,256]{2,1,0:T(8,128)(2,1)S(1)}, u32[]{:S(2)}, u32[]{:S(2)}) %collective-permute-start.77) | collective-permute-done | bytes 131104 | tf_op jit(solution)/shard_map/cond/branch_2_fun/ppermute | solution.py:20
  82.4 3.0 %collective-permute-done.80.rest_2_.rest_3_ = bf16[2,32,2048]{2,1,0:T(8,128)(2,1)S(1)} collective-permute-done((bf16[2,32,2048]{2,1,0:T(8,128)(2,1)S(1)}, bf16[2,32,2048]{2,1,0:T(8,128)(2,1)S(1)}, u32[]{:S(2)}, u32[]{:S(2)}) %collective-permute-start.80) | collective-permute-done | bytes 262176 | tf_op jit(solution)/shard_map/cond/branch_2_fun/ppermute | solution.py:387
  85.4 2.7 %collective-permute-done.81.rest_3_.rest_4_ = bf16[2,32,2048]{2,1,0:T(8,128)(2,1)S(1)} collective-permute-done((bf16[2,32,2048]{2,1,0:T(8,128)(2,1)S(1)}, bf16[2,32,2048]{2,1,0:T(8,128)(2,1)S(1)}, u32[]{:S(2)}, u32[]{:S(2)}) %collective-permute-start.81) | collective-permute-done | bytes 262176 | tf_op jit(solution)/shard_map/cond/branch_2_fun/ppermute | solution.py:387
  88.1 1.6 %branch_2_fun.15.rest_0_ = bf16[2,128,256]{2,1,0:T(8,128)(2,1)S(1)} custom-call(s32[70]{0:T(128)S(1)} %get-tuple-element.245.meta, bf16[2,32,2048]{2,1,0:T(8,128)(2,1)S(1)} %get-tuple-element.266.rest_0_.rest_1_, bf16[2,32,2048]{2,1,0:T(8,128)(2,1)S(1)} %collective-permute-done.79.rest_1_.rest_2_, ...), custom_call_target="tpu_custom_call" | custom-call | flops 268435456 | bytes 2097152 | tf_op jit(solution)/shard_map/cond/branch_2_fun/pallas_call | solution.py:247
  93.3 1.8 %collective-permute-done.83.rest_2_ = bf16[2,128,256]{2,1,0:T(8,128)(2,1)S(1)} collective-permute-done((bf16[2,128,256]{2,1,0:T(8,128)(2,1)S(1)}, bf16[2,128,256]{2,1,0:T(8,128)(2,1)S(1)}, u32[]{:S(2)}, u32[]{:S(2)}) %collective-permute-start.83) | collective-permute-done | bytes 131104 | tf_op jit(solution)/shard_map/cond/branch_2_fun/ppermute | solution.py:446
  95.1 3.4 %collective-permute-done.82.rest_1_ = bf16[2,128,256]{2,1,0:T(8,128)(2,1)S(1)} collective-permute-done((bf16[2,128,256]{2,1,0:T(8,128)(2,1)S(1)}, bf16[2,128,256]{2,1,0:T(8,128)(2,1)S(1)}, u32[]{:S(2)}, u32[]{:S(2)}) %collective-permute-start.82) | collective-permute-done | bytes 131104 | tf_op jit(solution)/shard_map/cond/branch_2_fun/ppermute | solution.py:20
  100.0 2.6 %branch_2_fun.19 = (bf16[128,2048]{1,0:T(8,128)(2,1)S(1)}, bf16[128,2048]{1,0:T(8,128)(2,1)S(1)}) custom-call(s32[70]{0:T(128)S(1)} %get-tuple-element.245.meta, bf16[4,128,256]{2,1,0:T(8,128)(2,1)S(1)} %get-tuple-element.285.rest_0_, bf16[2,32,2048]{2,1,0:T(8,128)(2,1)S(1)} %get-tuple-element.266.rest_0_.rest_1_, ...), custom_call_target="tpu_custom_call" | custom-call | flops 536870912 | bytes 3145728 | tf_op jit(solution)/shard_map/cond/branch_2_fun/pallas_call | solution.py:328
  104.3 7.4 %collective-permute-start.85 = (bf16[2,32,2048]{2,1,0:T(8,128)(2,1)S(1)}, bf16[2,32,2048]{2,1,0:T(8,128)(2,1)S(1)}, u32[]{:S(2)}, u32[]{:S(2)}) collective-permute-start(bf16[2,32,2048]{2,1,0:T(8,128)(2,1)S(1)} %get-tuple-element.273), channel_id=1, source_target_pairs={{4,0},{8,4},{12,8},{0,12},{5,1},{9,5},{13,9},{1,13},{6,2},{10,6},{... | collective-permute-start | bytes 786440 | tf_op jit(solution)/shard_map/cond/branch_2_fun/ppermute | solution.py:387
  112.9 1.9 %collective-permute-start.87 = (bf16[2,32,2048]{2,1,0:T(8,128)(2,1)S(1)}, bf16[2,32,2048]{2,1,0:T(8,128)(2,1)S(1)}, u32[]{:S(2)}, u32[]{:S(2)}) collective-permute-start(bf16[2,32,2048]{2,1,0:T(8,128)(2,1)S(1)} %get-tuple-element.275), channel_id=1, source_target_pairs={{12,0},{0,4},{4,8},{8,12},{13,1},{1,5},{5,9},{9,13},{14,2},{2,6},{... | collective-permute-start | bytes 786440 | tf_op jit(solution)/shard_map/cond/branch_2_fun/ppermute | solution.py:387
  114.8 2.6 %branch_2_fun.18 = (bf16[128,2048]{1,0:T(8,128)(2,1)S(1)}, bf16[128,2048]{1,0:T(8,128)(2,1)S(1)}) custom-call(s32[70]{0:T(128)S(1)} %get-tuple-element.245.meta, bf16[2,128,256]{2,1,0:T(8,128)(2,1)S(1)} %get-tuple-element.281.rest_0_, bf16[2,128,256]{2,1,0:T(8,128)(2,1)S(1)} %get-tuple-element.270.rest_1_, ...), custom_call_target="tpu_custom_call" | custom-call | flops 536870912 | bytes 3145728 | tf_op jit(solution)/shard_map/cond/branch_2_fun/pallas_call | solution.py:328
  118.5 16.7 %collective-permute-done.86.rest_2_ = bf16[2,32,2048]{2,1,0:T(8,128)(2,1)S(1)} collective-permute-done((bf16[2,32,2048]{2,1,0:T(8,128)(2,1)S(1)}, bf16[2,32,2048]{2,1,0:T(8,128)(2,1)S(1)}, u32[]{:S(2)}, u32[]{:S(2)}) %collective-permute-start.86) | collective-permute-done | bytes 262176 | tf_op jit(solution)/shard_map/cond/branch_2_fun/ppermute | solution.py:387
  139.4 9.2 %collective-permute-done.90 = bf16[4,32,2048]{2,1,0:T(8,128)(2,1)S(1)} collective-permute-done((bf16[4,32,2048]{2,1,0:T(8,128)(2,1)S(1)}, bf16[4,32,2048]{2,1,0:T(8,128)(2,1)S(1)}, u32[]{:S(2)}, u32[]{:S(2)}) %collective-permute-start.90) | collective-permute-done | bytes 524320 | tf_op jit(solution)/shard_map/cond/branch_2_fun/ppermute | solution.py:20
  (85 shorter events, 37.5 us)
Async XLA Ops:
  1.7 18.2 %collective-permute-start.145 = (bf16[4,32,2048]{2,1,0:T(8,128)(2,1)S(1)}, bf16[4,32,2048]{2,1,0:T(8,128)(2,1)S(1)}, u32[]{:S(2)}, u32[]{:S(2)}) collective-permute-start(bf16[4,32,2048]{2,1,0:T(8,128)(2,1)S(1)} %dynamic-slice_bitcast_fusion.1), channel_id=1, source_target_pairs={{0,2},{2,0},{1,3},{3,1},{4,6},{6,4},{5,7},{7,5},{8,10},{10,8},{9,1... | collective-permute-start | bytes 1572872 | tf_op jit(solution)/shard_map/ppermute | solution.py:20
  4.7 12.0 %collective-permute-start.144 = (s32[1,4,1]{1,2,0:T(1,128)S(1)}, s32[1,4,1]{1,2,0:T(1,128)S(1)}, u32[]{:S(2)}, u32[]{:S(2)}) collective-permute-start(s32[1,4,1]{1,2,0:T(1,128)S(1)} %copy-done.2), channel_id=1, source_target_pairs={{0,2},{2,0},{1,3},{3,1},{4,6},{6,4},{5,7},{7,5},{8,10},{10,8},{9,1... | collective-permute-start | bytes 56 | tf_op jit(solution)/shard_map/ppermute | solution.py:20
  6.2 16.0 %collective-permute-start.146 = (bf16[1,32,2048]{2,1,0:T(8,128)(2,1)S(1)}, bf16[1,32,2048]{2,1,0:T(8,128)(2,1)}, u32[]{:S(2)}, u32[]{:S(2)}) collective-permute-start(bf16[1,32,2048]{2,1,0:T(8,128)(2,1)S(1)} %get-tuple-element.383), channel_id=1, source_target_pairs={{0,4},{4,8},{8,12},{12,0},{1,5},{5,9},{9,13},{13,1},{2,6},{6,10},{... | collective-permute-start | bytes 393224 | tf_op jit(solution)/shard_map/ppermute | solution.py:387
  8.3 13.9 %collective-permute-start.147 = (bf16[1,32,2048]{2,1,0:T(8,128)(2,1)S(1)}, bf16[1,32,2048]{2,1,0:T(8,128)(2,1)}, u32[]{:S(2)}, u32[]{:S(2)}) collective-permute-start(bf16[1,32,2048]{2,1,0:T(8,128)(2,1)S(1)} %get-tuple-element.384), channel_id=1, source_target_pairs={{0,8},{4,12},{8,0},{12,4},{1,9},{5,13},{9,1},{13,5},{2,10},{6,14},... | collective-permute-start | bytes 393224 | tf_op jit(solution)/shard_map/ppermute | solution.py:387
  10.9 11.4 %collective-permute-start.148 = (bf16[1,32,2048]{2,1,0:T(8,128)(2,1)S(1)}, bf16[1,32,2048]{2,1,0:T(8,128)(2,1)}, u32[]{:S(2)}, u32[]{:S(2)}) collective-permute-start(bf16[1,32,2048]{2,1,0:T(8,128)(2,1)S(1)} %get-tuple-element.385), channel_id=1, source_target_pairs={{0,12},{4,0},{8,4},{12,8},{1,13},{5,1},{9,5},{13,9},{2,14},{6,2},{... | collective-permute-start | bytes 393224 | tf_op jit(solution)/shard_map/ppermute | solution.py:387
  22.5 15.2 %collective-permute-start.71 = (bf16[4,32,2048]{2,1,0:T(8,128)(2,1)S(1)}, bf16[4,32,2048]{2,1,0:T(8,128)(2,1)S(1)}, u32[]{:S(2)}, u32[]{:S(2)}) collective-permute-start(bf16[4,32,2048]{2,1,0:T(8,128)(2,1)S(1)} %get-tuple-element.259), channel_id=1, source_target_pairs={{0,2},{2,0},{1,3},{3,1},{4,6},{6,4},{5,7},{7,5},{8,10},{10,8},{9,1... | collective-permute-start | bytes 1572872 | tf_op jit(solution)/shard_map/cond/branch_2_fun/ppermute | solution.py:20
  24.3 24.5 %collective-permute-start.68 = (bf16[128,2048]{1,0:T(8,128)(2,1)}, bf16[128,2048]{1,0:T(8,128)(2,1)}, u32[]{:S(2)}, u32[]{:S(2)}) collective-permute-start(bf16[128,2048]{1,0:T(8,128)(2,1)} %get-tuple-element.256), channel_id=1, source_target_pairs={{0,2},{2,0},{1,3},{3,1},{4,6},{6,4},{5,7},{7,5},{8,10},{10,8},{9,1... | collective-permute-start | bytes 1572872 | tf_op jit(solution)/shard_map/cond/branch_2_fun/ppermute | solution.py:20
  24.6 39.0 %collective-permute-start.75 = (bf16[128,2048]{1,0:T(8,128)(2,1)}, bf16[128,2048]{1,0:T(8,128)(2,1)}, u32[]{:S(2)}, u32[]{:S(2)}) collective-permute-start(bf16[128,2048]{1,0:T(8,128)(2,1)} %get-tuple-element.263), channel_id=1, source_target_pairs={{0,2},{2,0},{1,3},{3,1},{4,6},{6,4},{5,7},{7,5},{8,10},{10,8},{9,1... | collective-permute-start | bytes 1572872 | tf_op jit(solution)/shard_map/cond/branch_2_fun/ppermute | solution.py:20
  26.3 7.0 %collective-permute-start.62 = (bf16[1,32,2048]{2,1,0:T(8,128)(2,1)S(1)}, bf16[1,32,2048]{2,1,0:T(8,128)(2,1)S(1)}, u32[]{:S(2)}, u32[]{:S(2)}) collective-permute-start(bf16[1,32,2048]{2,1,0:T(8,128)(2,1)S(1)} %get-tuple-element.251), channel_id=1, source_target_pairs={{0,4},{4,8},{8,12},{12,0},{1,5},{5,9},{9,13},{13,1},{2,6},{6,10},{... | collective-permute-start | bytes 393224 | tf_op jit(solution)/shard_map/cond/branch_2_fun/ppermute | solution.py:387
  27.9 6.4 %collective-permute-start.64 = (bf16[1,32,2048]{2,1,0:T(8,128)(2,1)S(1)}, bf16[1,32,2048]{2,1,0:T(8,128)(2,1)S(1)}, u32[]{:S(2)}, u32[]{:S(2)}) collective-permute-start(bf16[1,32,2048]{2,1,0:T(8,128)(2,1)S(1)} %get-tuple-element.253), channel_id=1, source_target_pairs={{0,12},{4,0},{8,4},{12,8},{1,13},{5,1},{9,5},{13,9},{2,14},{6,2},{... | collective-permute-start | bytes 393224 | tf_op jit(solution)/shard_map/cond/branch_2_fun/ppermute | solution.py:387
  33.3 23.4 %collective-permute-start.67 = (bf16[2,32,2048]{2,1,0:T(8,128)(2,1)S(1)}, bf16[2,32,2048]{2,1,0:T(8,128)(2,1)S(1)}, u32[]{:S(2)}, u32[]{:S(2)}) collective-permute-start(bf16[2,32,2048]{2,1,0:T(8,128)(2,1)S(1)} %get-tuple-element.254.rest_8_.rest_10_), channel_id=1, source_target_pairs={{12,8},{13,9},{14,10},{15,11},{28,24},{29,25},{30,26},{31,27}} | collective-permute-start | bytes 786440 | tf_op jit(solution)/shard_map/cond/branch_2_fun/ppermute | solution.py:387
  34.2 26.5 %collective-permute-start.66 = (bf16[2,32,2048]{2,1,0:T(8,128)(2,1)S(1)}, bf16[2,32,2048]{2,1,0:T(8,128)(2,1)S(1)}, u32[]{:S(2)}, u32[]{:S(2)}) collective-permute-start(bf16[2,32,2048]{2,1,0:T(8,128)(2,1)S(1)} %get-tuple-element.254.rest_8_.rest_10_), channel_id=1, source_target_pairs={{0,8},{1,9},{2,10},{3,11},{16,24},{17,25},{18,26},{19,27}} | collective-permute-start | bytes 786440 | tf_op jit(solution)/shard_map/cond/branch_2_fun/ppermute | solution.py:387
  37.7 23.8 %collective-permute-start.65 = (bf16[2,32,2048]{2,1,0:T(8,128)(2,1)S(1)}, bf16[2,32,2048]{2,1,0:T(8,128)(2,1)S(1)}, u32[]{:S(2)}, u32[]{:S(2)}) collective-permute-start(bf16[2,32,2048]{2,1,0:T(8,128)(2,1)S(1)} %get-tuple-element.254.rest_8_.rest_10_), channel_id=1, source_target_pairs={{4,8},{5,9},{6,10},{7,11},{20,24},{21,25},{22,26},{23,27}} | collective-permute-start | bytes 786440 | tf_op jit(solution)/shard_map/cond/branch_2_fun/ppermute | solution.py:387
  48.7 7.3 %collective-permute-start.63 = (bf16[1,32,2048]{2,1,0:T(8,128)(2,1)S(1)}, bf16[1,32,2048]{2,1,0:T(8,128)(2,1)S(1)}, u32[]{:S(2)}, u32[]{:S(2)}) collective-permute-start(bf16[1,32,2048]{2,1,0:T(8,128)(2,1)S(1)} %copy-done.34), channel_id=1, source_target_pairs={{0,8},{4,12},{8,0},{12,4},{1,9},{5,13},{9,1},{13,5},{2,10},{6,14},... | collective-permute-start | bytes 393224 | tf_op jit(solution)/shard_map/cond/branch_2_fun/ppermute | solution.py:387
  56.0 10.3 %collective-permute-start.74 = (bf16[2,32,2048]{2,1,0:T(8,128)(2,1)S(1)}, bf16[2,32,2048]{2,1,0:T(8,128)(2,1)S(1)}, u32[]{:S(2)}, u32[]{:S(2)}) collective-permute-start(bf16[2,32,2048]{2,1,0:T(8,128)(2,1)S(1)} %get-tuple-element.261.rest_0_.rest_5_), channel_id=1, source_target_pairs={{12,8},{13,9},{14,10},{15,11},{28,24},{29,25},{30,26},{31,27}} | collective-permute-start | bytes 786440 | tf_op jit(solution)/shard_map/cond/branch_2_fun/ppermute | solution.py:387
  56.7 10.1 %collective-permute-start.73 = (bf16[2,32,2048]{2,1,0:T(8,128)(2,1)S(1)}, bf16[2,32,2048]{2,1,0:T(8,128)(2,1)S(1)}, u32[]{:S(2)}, u32[]{:S(2)}) collective-permute-start(bf16[2,32,2048]{2,1,0:T(8,128)(2,1)S(1)} %get-tuple-element.261.rest_0_.rest_5_), channel_id=1, source_target_pairs={{0,8},{1,9},{2,10},{3,11},{16,24},{17,25},{18,26},{19,27}} | collective-permute-start | bytes 786440 | tf_op jit(solution)/shard_map/cond/branch_2_fun/ppermute | solution.py:387
  60.8 6.0 %collective-permute-start.72 = (bf16[2,32,2048]{2,1,0:T(8,128)(2,1)S(1)}, bf16[2,32,2048]{2,1,0:T(8,128)(2,1)S(1)}, u32[]{:S(2)}, u32[]{:S(2)}) collective-permute-start(bf16[2,32,2048]{2,1,0:T(8,128)(2,1)S(1)} %get-tuple-element.261.rest_0_.rest_5_), channel_id=1, source_target_pairs={{4,8},{5,9},{6,10},{7,11},{20,24},{21,25},{22,26},{23,27}} | collective-permute-start | bytes 786440 | tf_op jit(solution)/shard_map/cond/branch_2_fun/ppermute | solution.py:387
  63.5 18.8 %collective-permute-start.79 = (bf16[2,32,2048]{2,1,0:T(8,128)(2,1)S(1)}, bf16[2,32,2048]{2,1,0:T(8,128)(2,1)S(1)}, u32[]{:S(2)}, u32[]{:S(2)}) collective-permute-start(bf16[2,32,2048]{2,1,0:T(8,128)(2,1)S(1)} %get-tuple-element.267), channel_id=1, source_target_pairs={{0,4},{4,8},{8,12},{12,0},{1,5},{5,9},{9,13},{13,1},{2,6},{6,10},{... | collective-permute-start | bytes 786440 | tf_op jit(solution)/shard_map/cond/branch_2_fun/ppermute | solution.py:387
  66.3 19.0 %collective-permute-start.80 = (bf16[2,32,2048]{2,1,0:T(8,128)(2,1)S(1)}, bf16[2,32,2048]{2,1,0:T(8,128)(2,1)S(1)}, u32[]{:S(2)}, u32[]{:S(2)}) collective-permute-start(bf16[2,32,2048]{2,1,0:T(8,128)(2,1)S(1)} %get-tuple-element.268), channel_id=1, source_target_pairs={{0,8},{4,12},{8,0},{12,4},{1,9},{5,13},{9,1},{13,5},{2,10},{6,14},... | collective-permute-start | bytes 786440 | tf_op jit(solution)/shard_map/cond/branch_2_fun/ppermute | solution.py:387
  68.6 9.2 %collective-permute-start.70 = (bf16[4,128,256]{2,1,0:T(8,128)(2,1)S(1)}, bf16[4,128,256]{2,1,0:T(8,128)(2,1)S(1)}, u32[]{:S(2)}, u32[]{:S(2)}) collective-permute-start(bf16[4,128,256]{2,1,0:T(8,128)(2,1)S(1)} %add_convert_fusion.4.h1), channel_id=1, source_target_pairs={{0,2},{2,0},{1,3},{3,1},{4,6},{6,4},{5,7},{7,5},{8,10},{10,8},{9,1... | collective-permute-start | bytes 786440 | tf_op jit(solution)/shard_map/cond/branch_2_fun/ppermute | solution.py:20
  70.1 10.0 %collective-permute-start.77 = (bf16[2,128,256]{2,1,0:T(8,128)(2,1)S(1)}, bf16[2,128,256]{2,1,0:T(8,128)(2,1)S(1)}, u32[]{:S(2)}, u32[]{:S(2)}) collective-permute-start(bf16[2,128,256]{2,1,0:T(8,128)(2,1)S(1)} %add_convert_fusion.5.rest_0_), channel_id=1, source_target_pairs={{0,2},{2,0},{1,3},{3,1},{4,6},{6,4},{5,7},{7,5},{8,10},{10,8},{9,1... | collective-permute-start | bytes 393224 | tf_op jit(solution)/shard_map/cond/branch_2_fun/ppermute | solution.py:20
  71.4 16.7 %collective-permute-start.81 = (bf16[2,32,2048]{2,1,0:T(8,128)(2,1)S(1)}, bf16[2,32,2048]{2,1,0:T(8,128)(2,1)S(1)}, u32[]{:S(2)}, u32[]{:S(2)}) collective-permute-start(bf16[2,32,2048]{2,1,0:T(8,128)(2,1)S(1)} %get-tuple-element.269), channel_id=1, source_target_pairs={{0,12},{4,0},{8,4},{12,8},{1,13},{5,1},{9,5},{13,9},{2,14},{6,2},{... | collective-permute-start | bytes 786440 | tf_op jit(solution)/shard_map/cond/branch_2_fun/ppermute | solution.py:387
  81.7 11.6 %collective-permute-start.78 = (bf16[2,32,2048]{2,1,0:T(8,128)(2,1)S(1)}, bf16[2,32,2048]{2,1,0:T(8,128)(2,1)S(1)}, u32[]{:S(2)}, u32[]{:S(2)}) collective-permute-start(bf16[2,32,2048]{2,1,0:T(8,128)(2,1)S(1)} %get-tuple-element.264), channel_id=1, source_target_pairs={{8,4},{9,5},{10,6},{11,7},{24,20},{25,21},{26,22},{27,23}} | collective-permute-start | bytes 786440 | tf_op jit(solution)/shard_map/cond/branch_2_fun/ppermute | solution.py:387
  90.8 7.7 %collective-permute-start.82 = (bf16[2,128,256]{2,1,0:T(8,128)(2,1)S(1)}, bf16[2,128,256]{2,1,0:T(8,128)(2,1)S(1)}, u32[]{:S(2)}, u32[]{:S(2)}) collective-permute-start(bf16[2,128,256]{2,1,0:T(8,128)(2,1)S(1)} %branch_2_fun.15.rest_0_), channel_id=1, source_target_pairs={{0,2},{2,0},{1,3},{3,1},{4,6},{6,4},{5,7},{7,5},{8,10},{10,8},{9,1... | collective-permute-start | bytes 393224 | tf_op jit(solution)/shard_map/cond/branch_2_fun/ppermute | solution.py:20
  92.0 20.9 %collective-permute-start.88 = (bf16[2,32,2048]{2,1,0:T(8,128)(2,1)S(1)}, bf16[2,32,2048]{2,1,0:T(8,128)(2,1)S(1)}, u32[]{:S(2)}, u32[]{:S(2)}) collective-permute-start(bf16[2,32,2048]{2,1,0:T(8,128)(2,1)S(1)} %get-tuple-element.277), channel_id=1, source_target_pairs={{8,0},{9,1},{10,2},{11,3},{24,16},{25,17},{26,18},{27,19}} | collective-permute-start | bytes 786440 | tf_op jit(solution)/shard_map/cond/branch_2_fun/ppermute | solution.py:387
  102.6 34.3 %collective-permute-start.92 = (bf16[128,2048]{1,0:T(8,128)(2,1)S(1)}, bf16[128,2048]{1,0:T(8,128)(2,1)S(1)}, u32[]{:S(2)}, u32[]{:S(2)}) collective-permute-start(bf16[128,2048]{1,0:T(8,128)(2,1)S(1)} %get-tuple-element.287), channel_id=1, source_target_pairs={{0,2},{2,0},{1,3},{3,1},{4,6},{6,4},{5,7},{7,5},{8,10},{10,8},{9,1... | collective-permute-start | bytes 1572872 | tf_op jit(solution)/shard_map/cond/branch_2_fun/ppermute | solution.py:20
  103.6 13.9 %collective-permute-start.89 = (bf16[2,32,2048]{2,1,0:T(8,128)(2,1)S(1)}, bf16[2,32,2048]{2,1,0:T(8,128)(2,1)S(1)}, u32[]{:S(2)}, u32[]{:S(2)}) collective-permute-start(bf16[2,32,2048]{2,1,0:T(8,128)(2,1)S(1)} %get-tuple-element.278), channel_id=1, source_target_pairs={{8,12},{9,13},{10,14},{11,15},{24,28},{25,29},{26,30},{27,31}} | collective-permute-start | bytes 786440 | tf_op jit(solution)/shard_map/cond/branch_2_fun/ppermute | solution.py:387
  104.3 14.2 %collective-permute-start.85 = (bf16[2,32,2048]{2,1,0:T(8,128)(2,1)S(1)}, bf16[2,32,2048]{2,1,0:T(8,128)(2,1)S(1)}, u32[]{:S(2)}, u32[]{:S(2)}) collective-permute-start(bf16[2,32,2048]{2,1,0:T(8,128)(2,1)S(1)} %get-tuple-element.273), channel_id=1, source_target_pairs={{4,0},{8,4},{12,8},{0,12},{5,1},{9,5},{13,9},{1,13},{6,2},{10,6},{... | collective-permute-start | bytes 786440 | tf_op jit(solution)/shard_map/cond/branch_2_fun/ppermute | solution.py:387
  111.6 23.5 %collective-permute-start.86 = (bf16[2,32,2048]{2,1,0:T(8,128)(2,1)S(1)}, bf16[2,32,2048]{2,1,0:T(8,128)(2,1)S(1)}, u32[]{:S(2)}, u32[]{:S(2)}) collective-permute-start(bf16[2,32,2048]{2,1,0:T(8,128)(2,1)S(1)} %get-tuple-element.274), channel_id=1, source_target_pairs={{8,0},{12,4},{0,8},{4,12},{9,1},{13,5},{1,9},{5,13},{10,2},{14,6},... | collective-permute-start | bytes 786440 | tf_op jit(solution)/shard_map/cond/branch_2_fun/ppermute | solution.py:387
  112.9 22.2 %collective-permute-start.87 = (bf16[2,32,2048]{2,1,0:T(8,128)(2,1)S(1)}, bf16[2,32,2048]{2,1,0:T(8,128)(2,1)S(1)}, u32[]{:S(2)}, u32[]{:S(2)}) collective-permute-start(bf16[2,32,2048]{2,1,0:T(8,128)(2,1)S(1)} %get-tuple-element.275), channel_id=1, source_target_pairs={{12,0},{0,4},{4,8},{8,12},{13,1},{1,5},{5,9},{9,13},{14,2},{2,6},{... | collective-permute-start | bytes 786440 | tf_op jit(solution)/shard_map/cond/branch_2_fun/ppermute | solution.py:387
  117.5 20.7 %collective-permute-start.91 = (bf16[128,2048]{1,0:T(8,128)(2,1)S(1)}, bf16[128,2048]{1,0:T(8,128)(2,1)S(1)}, u32[]{:S(2)}, u32[]{:S(2)}) collective-permute-start(bf16[128,2048]{1,0:T(8,128)(2,1)S(1)} %get-tuple-element.283), channel_id=1, source_target_pairs={{0,2},{2,0},{1,3},{3,1},{4,6},{6,4},{5,7},{7,5},{8,10},{10,8},{9,1... | collective-permute-start | bytes 1572872 | tf_op jit(solution)/shard_map/cond/branch_2_fun/ppermute | solution.py:20
  136.3 12.2 %collective-permute-start.90 = (bf16[4,32,2048]{2,1,0:T(8,128)(2,1)S(1)}, bf16[4,32,2048]{2,1,0:T(8,128)(2,1)S(1)}, u32[]{:S(2)}, u32[]{:S(2)}) collective-permute-start(bf16[4,32,2048]{2,1,0:T(8,128)(2,1)S(1)} %get-tuple-element.280), channel_id=1, source_target_pairs={{0,2},{2,0},{1,3},{3,1},{4,6},{6,4},{5,7},{7,5},{8,10},{10,8},{9,1... | collective-permute-start | bytes 1572872 | tf_op jit(solution)/shard_map/cond/branch_2_fun/ppermute | solution.py:20
  (14 other events, 89.7 us)

commit v5 on v3

--- a/solution.py
+++ b/solution.py
@@ -334,36 +334,35 @@
     )(meta, *acts, *data)
 
 
-def collect_kernel(owners, tiles, base, meta, *rest):
-    pieces, (mine, other) = rest[:-2], rest[-2:]
+def collect_kernel(owners, tiles, base, own, meta, *rest):
+    pieces, out = rest[:-1], rest[-1]
     side, place = meta[0], meta[1]
     even = pieces[0].shape[0]
-    for r, out in enumerate((mine, other)):
-        replica = side if r == 0 else 1 - side
-
-        @pl.loop(0, tiles)
-        def _(t):
-            tile = replica * tiles + t
-            k = lax.rem(meta[base + tile] - place + owners, owners)
-            slot = meta[base + 2 * tiles + tile]
-            for kk in range(owners):
-
-                @pl.when((k == kk) & (slot < even))
+    replica = side if own else 1 - side
+
+    @pl.loop(0, tiles)
+    def _(t):
+        tile = replica * tiles + t
+        k = lax.rem(meta[base + tile] - place + owners, owners)
+        slot = meta[base + 2 * tiles + tile]
+        for kk in range(owners):
+
+            @pl.when((k == kk) & (slot < even))
+            def _():
+                copy_rows(pieces[kk], slot, out, t)
+
+            if len(pieces) > owners:
+
+                @pl.when((k == kk) & (slot >= even))
                 def _():
-                    copy_rows(pieces[kk], slot, out, t)
-
-                if len(pieces) > owners:
-
-                    @pl.when((k == kk) & (slot >= even))
-                    def _():
-                        copy_rows(pieces[owners + kk], slot - even, out, t)
-
-
-def collect(meta, pieces, tiles, owners, base):
+                    copy_rows(pieces[owners + kk], slot - even, out, t)
+
+
+def collect(meta, pieces, tiles, owners, base, own):
     _, rows, width = pieces[0].shape
-    kernel = functools.partial(collect_kernel, owners, tiles, base)
-    outs = [jax.ShapeDtypeStruct((tiles, rows, width), BF16)] * 2
-    return call(kernel, outs, len(pieces), moved=8 * tiles * rows * width)(meta, *pieces)
+    kernel = functools.partial(collect_kernel, owners, tiles, base, own)
+    outs = [jax.ShapeDtypeStruct((tiles, rows, width), BF16)]
+    return call(kernel, outs, len(pieces), moved=4 * tiles * rows * width)(meta, *pieces)[0]
 
 
 def shards(tokens, cotangent, w_up, w_down, active):
@@ -451,7 +450,8 @@
         up_grad, up_other = weights(meta, grad_hidden, tok, fast)
         up_got = swap(up_other, "dp")
         home = [piece for group in home for piece in group]
-        mine, other = collect(meta, home, tiles, owners, by_tile)
+        other = collect(meta, home, tiles, owners, by_tile, False)
+        mine = collect(after(meta, other), home, tiles, owners, by_tile, True)
         return (
             ordered(mine, swap(other, "dp"), side, 2)[None],
             ordered(up_grad, up_got, side, 1),

time: 152 us -> 155 us (1.020); the launches traced: 149 us -> 156 us
  starting transfers between devices: 53.9 us -> 62 us
  waiting for transfers between devices: 58.8 us -> 56.8 us
    ppermute x21, starting transfers between devices: 40.2 us -> 47.4 us  [move(): lax.ppermute(pieces[k], 'tensor', perm_of(k))]
  transfers between devices with their start and end apart: 35 -> 35, of which waited for: 12 -> 11; matrix products, arithmetic and copies ran while one was open for 7% -> 6% of each run, Pallas kernels for 13% -> 13%
where the time goes in v5:
time: 155 us; the launch traced here: 156 us
  starting transfers between devices  62 us (40%)
  waiting for transfers between devices  56.8 us (37%)
  Pallas kernels  22 us (14%)
  other arithmetic  6.94 us (4%)
  local copies, waits for them, and re-layouts  5.89 us (4%)
    ppermute x21, starting transfers between devices, move(): lax.ppermute(pieces[k], 'tensor', perm_of(k))  47.4 us
    ppermute x21, waiting for transfers between devices, move(): lax.ppermute(pieces[k], 'tensor', perm_of(k))  28.8 us
    ppermute x14, waiting for transfers between devices, swap(): return lax.ppermute(x, axis, [(0, 1), (1, 0)])  28 us
    ppermute x14, starting transfers between devices, swap(): return lax.ppermute(x, axis, [(0, 1), (1, 0)])  14.6 us
    select_n x5, other arithmetic, ordered(): jnp.where(side == 0, jnp.concatenate([mine, other], axis), jnp.concatenat...  6.81 us
    pallas_call x2, Pallas kernels, weights(): call(functools.partial(weights_kernel, owners, act_counts, counts, moved)...  5.2 us
    pallas_call x3, Pallas kernels, product(): call(functools.partial(product_kernel, counts, owners, moved), [jax.Shape...  5.18 us
    pallas_call x2, Pallas kernels, dispatch(): call(kernel, outs, 2, moved=4 * sum(counts) * rows * width)(meta, keep, got)  3.3 us
  transfers between devices with their start and end apart: 35, of which 11 were waited for; matrix products, arithmetic and copies ran while one was open for 6% of the time, Pallas kernels for 13%

profile of v5, /device:TPU:0, one launch (start us, length us, event | category | flops | bytes accessed | tf_op | source)
XLA Modules:
  0.0 155.6 jit_solution(10363193416028069863)
XLA Ops:
  1.7 3.0 %collective-permute-start.140 = (bf16[4,32,2048]{2,1,0:T(8,128)(2,1)S(1)}, bf16[4,32,2048]{2,1,0:T(8,128)(2,1)S(1)}, u32[]{:S(2)}, u32[]{:S(2)}) collective-permute-start(bf16[4,32,2048]{2,1,0:T(8,128)(2,1)S(1)} %dynamic-slice_bitcast_fusion.1), channel_id=1, source_target_pairs={{0,2},{2,0},{1,3},{3,1},{4,6},{6,4},{5,7},{7,5},{8,10},{10,8},{9,1... | collective-permute-start | bytes 1572872 | tf_op jit(solution)/shard_map/ppermute | solution.py:20
  6.2 2.1 %collective-permute-start.141 = (bf16[1,32,2048]{2,1,0:T(8,128)(2,1)S(1)}, bf16[1,32,2048]{2,1,0:T(8,128)(2,1)}, u32[]{:S(2)}, u32[]{:S(2)}) collective-permute-start(bf16[1,32,2048]{2,1,0:T(8,128)(2,1)S(1)} %get-tuple-element.374), channel_id=1, source_target_pairs={{0,4},{4,8},{8,12},{12,0},{1,5},{5,9},{9,13},{13,1},{2,6},{6,10},{... | collective-permute-start | bytes 393224 | tf_op jit(solution)/shard_map/ppermute | solution.py:385
  8.3 2.6 %collective-permute-start.142 = (bf16[1,32,2048]{2,1,0:T(8,128)(2,1)S(1)}, bf16[1,32,2048]{2,1,0:T(8,128)(2,1)}, u32[]{:S(2)}, u32[]{:S(2)}) collective-permute-start(bf16[1,32,2048]{2,1,0:T(8,128)(2,1)S(1)} %get-tuple-element.375), channel_id=1, source_target_pairs={{0,8},{4,12},{8,0},{12,4},{1,9},{5,13},{9,1},{13,5},{2,10},{6,14},... | collective-permute-start | bytes 393224 | tf_op jit(solution)/shard_map/ppermute | solution.py:385
  12.2 2.8 %constant_dynamic-slice_fusion = (bf16[128,2048]{1,0:T(8,128)(2,1)S(1)}, bf16[128,2048]{1,0:T(8,128)(2,1)}, bf16[128,2048]{1,0:T(8,128)(2,1)}, bf16[128,2048]{1,0:T(8,128)(2,1)}) fusion(bf16[128,4096]{1,0:T(8,128)(2,1)} %param.13, s32[]{:T(128)S(6)} %select_n.182, s32[]{:T(128)S(6)} %select_n.181, bf16[128,4096]{1,0:T(8,128)(2,1)} %param.12), kind=kLoop, calls=%fused_computation.41 | loop fusion | bytes 4194312 | tf_op jit(solution)/shard_map/dynamic_slice | solution.py:95
  20.0 2.2 %shard_map.92 = (bf16[1,32,2048]{2,1,0:T(8,128)(2,1)}, bf16[1,32,2048]{2,1,0:T(8,128)(2,1)S(1)}, bf16[1,32,2048]{2,1,0:T(8,128)(2,1)}, bf16[1,32,2048]{2,1,0:T(8,128)(2,1)S(1)}, bf16[2,32,2048]{2,1,0:T(8,128)(2,1)S(1)}) custom-call(s32[70]{0:T(128)S(1)} %shard_map.91.meta, bf16[4,32,4096]{2,1,0:T(8,128)(2,1)} %bitcast.20.keep, ...), custom_call_target="tpu_custom_call" | custom-call | bytes 1572864 | tf_op jit(solution)/shard_map/pallas_call | solution.py:196
  22.2 133.4 %conditional.1 = (bf16[1,4,32,4096]{3,2,1,0:T(8,128)(2,1)}, bf16[128,4096]{1,0:T(8,128)(2,1)}, bf16[128,4096]{1,0:T(8,128)(2,1)}) conditional(s32[]{:T(128)} %bitcast.19, (s32[]{:T(128)}, bf16[1,32,2048]{2,1,0:T(8,128)(2,1)S(1)}, bf16[1,32,2048]{2,1,0:T(8,128)(2,1)}, bf16[1,32,2048]{2,1,0:T(8,128)(2,1)S(1)}, ...), branch_computations={%region_0.1_spmd, %region_1.2_spmd, %region_2.3_spmd, %region_3.4_... | conditional | flops 4051697664 | bytes 122422320 | solution.py:461
  22.4 1.8 %collective-permute-start.99 = (bf16[4,32,2048]{2,1,0:T(8,128)(2,1)S(1)}, bf16[4,32,2048]{2,1,0:T(8,128)(2,1)S(1)}, u32[]{:S(2)}, u32[]{:S(2)}) collective-permute-start(bf16[4,32,2048]{2,1,0:T(8,128)(2,1)S(1)} %get-tuple-element.297), channel_id=1, source_target_pairs={{0,2},{2,0},{1,3},{3,1},{4,6},{6,4},{5,7},{7,5},{8,10},{10,8},{9,1... | collective-permute-start | bytes 1572872 | tf_op jit(solution)/shard_map/cond/branch_3_fun/ppermute | solution.py:20
  24.5 1.7 %collective-permute-start.103 = (bf16[128,2048]{1,0:T(8,128)(2,1)}, bf16[128,2048]{1,0:T(8,128)(2,1)}, u32[]{:S(2)}, u32[]{:S(2)}) collective-permute-start(bf16[128,2048]{1,0:T(8,128)(2,1)} %get-tuple-element.304), channel_id=1, source_target_pairs={{0,2},{2,0},{1,3},{3,1},{4,6},{6,4},{5,7},{7,5},{8,10},{10,8},{9,1... | collective-permute-start | bytes 1572872 | tf_op jit(solution)/shard_map/cond/branch_3_fun/ppermute | solution.py:20
  26.3 1.6 %collective-permute-start.90 = (bf16[1,32,2048]{2,1,0:T(8,128)(2,1)S(1)}, bf16[1,32,2048]{2,1,0:T(8,128)(2,1)S(1)}, u32[]{:S(2)}, u32[]{:S(2)}) collective-permute-start(bf16[1,32,2048]{2,1,0:T(8,128)(2,1)S(1)} %get-tuple-element.289), channel_id=1, source_target_pairs={{0,4},{4,8},{8,12},{12,0},{1,5},{5,9},{9,13},{13,1},{2,6},{6,10},{... | collective-permute-start | bytes 393224 | tf_op jit(solution)/shard_map/cond/branch_3_fun/ppermute | solution.py:385
  27.8 2.2 %collective-permute-start.92 = (bf16[1,32,2048]{2,1,0:T(8,128)(2,1)S(1)}, bf16[1,32,2048]{2,1,0:T(8,128)(2,1)S(1)}, u32[]{:S(2)}, u32[]{:S(2)}) collective-permute-start(bf16[1,32,2048]{2,1,0:T(8,128)(2,1)S(1)} %get-tuple-element.291), channel_id=1, source_target_pairs={{0,12},{4,0},{8,4},{12,8},{1,13},{5,1},{9,5},{13,9},{2,14},{6,2},{... | collective-permute-start | bytes 393224 | tf_op jit(solution)/shard_map/cond/branch_3_fun/ppermute | solution.py:385
  30.1 3.2 %collective-permute-done.90.rest_5_.rest_7_ = bf16[1,32,2048]{2,1,0:T(8,128)(2,1)S(1)} collective-permute-done((bf16[1,32,2048]{2,1,0:T(8,128)(2,1)S(1)}, bf16[1,32,2048]{2,1,0:T(8,128)(2,1)S(1)}, u32[]{:S(2)}, u32[]{:S(2)}) %collective-permute-start.90) | collective-permute-done | bytes 131104 | tf_op jit(solution)/shard_map/cond/branch_3_fun/ppermute | solution.py:385
  33.3 4.0 %collective-permute-start.95 = (bf16[2,32,2048]{2,1,0:T(8,128)(2,1)S(1)}, bf16[2,32,2048]{2,1,0:T(8,128)(2,1)S(1)}, u32[]{:S(2)}, u32[]{:S(2)}) collective-permute-start(bf16[2,32,2048]{2,1,0:T(8,128)(2,1)S(1)} %get-tuple-element.292.rest_8_.rest_10_), channel_id=1, source_target_pairs={{0,12},{1,13},{2,14},{3,15},{16,28},{17,29},{18,30},{19,31}} | collective-permute-start | bytes 786440 | tf_op jit(solution)/shard_map/cond/branch_3_fun/ppermute | solution.py:385
  39.8 8.9 %collective-permute-done.96 = bf16[128,2048]{1,0:T(8,128)(2,1)} collective-permute-done((bf16[128,2048]{1,0:T(8,128)(2,1)}, bf16[128,2048]{1,0:T(8,128)(2,1)}, u32[]{:S(2)}, u32[]{:S(2)}) %collective-permute-start.96) | collective-permute-done | bytes 524320 | tf_op jit(solution)/shard_map/cond/branch_3_fun/ppermute | solution.py:20
  48.7 2.8 %collective-permute-start.91 = (bf16[1,32,2048]{2,1,0:T(8,128)(2,1)S(1)}, bf16[1,32,2048]{2,1,0:T(8,128)(2,1)S(1)}, u32[]{:S(2)}, u32[]{:S(2)}) collective-permute-start(bf16[1,32,2048]{2,1,0:T(8,128)(2,1)S(1)} %copy-done.36), channel_id=1, source_target_pairs={{0,8},{4,12},{8,0},{12,4},{1,9},{5,13},{9,1},{13,5},{2,10},{6,14},... | collective-permute-start | bytes 393224 | tf_op jit(solution)/shard_map/cond/branch_3_fun/ppermute | solution.py:385
  51.6 1.6 %maximum_select_fusion.15.rest_12_.up = bf16[256,2048]{1,0:T(8,128)(2,1)S(1)} fusion(bf16[128,2048]{1,0:T(8,128)(2,1)} %collective-permute-done.96, bf16[128,2048]{1,0:T(8,128)(2,1)S(1)} %copy-done.10, pred[]{:T(512)S(6)} %eq.13), kind=kLoop, calls=%fused_computation.24 | loop fusion | flops 4718592 | bytes 2097153 | tf_op jit(solution)/shard_map/cond/branch_3_fun/jit(_where)/select_n | solution.py:24
  53.2 2.8 %collective-permute-done.91.rest_6_.rest_8_ = bf16[1,32,2048]{2,1,0:T(8,128)(2,1)S(1)} collective-permute-done((bf16[1,32,2048]{2,1,0:T(8,128)(2,1)S(1)}, bf16[1,32,2048]{2,1,0:T(8,128)(2,1)S(1)}, u32[]{:S(2)}, u32[]{:S(2)}) %collective-permute-start.91) | collective-permute-done | bytes 131104 | tf_op jit(solution)/shard_map/cond/branch_3_fun/ppermute | solution.py:385
  56.0 5.6 %collective-permute-start.106 = (bf16[2,32,2048]{2,1,0:T(8,128)(2,1)S(1)}, bf16[2,32,2048]{2,1,0:T(8,128)(2,1)S(1)}, u32[]{:S(2)}, u32[]{:S(2)}) collective-permute-start(bf16[2,32,2048]{2,1,0:T(8,128)(2,1)S(1)} %get-tuple-element.305.rest_0_.rest_5_), channel_id=1, source_target_pairs={{0,12},{1,13},{2,14},{3,15},{16,28},{17,29},{18,30},{19,31}} | collective-permute-start | bytes 786440 | tf_op jit(solution)/shard_map/cond/branch_3_fun/ppermute | solution.py:385
  63.1 1.9 %branch_3_fun.11 = bf16[4,128,256]{2,1,0:T(8,128)(2,1)S(1)} custom-call(s32[70]{0:T(128)S(1)} %get-tuple-element.316.meta, bf16[1,32,2048]{2,1,0:T(8,128)(2,1)S(1)} %get-tuple-element.284.rest_0_.rest_2_, bf16[1,32,2048]{2,1,0:T(8,128)(2,1)S(1)} %copy-done.14, bf16[1,32,2048]{2,1,0:T(8,128)(2,1)S(1)} %copy-done.18, bf16[1,32,2048]{2,1,0:T(8,128)(2,1)S(1)} %copy-done.22, ...), custom_call_target="tpu_custom_call" | custom-call | flops 536870912 | bytes 3145728 | tf_op jit(solution)/shard_map/cond/branch_3_fun/pallas_call | solution.py:247
  68.6 5.6 %collective-permute-start.102 = (bf16[2,32,2048]{2,1,0:T(8,128)(2,1)S(1)}, bf16[2,32,2048]{2,1,0:T(8,128)(2,1)S(1)}, u32[]{:S(2)}, u32[]{:S(2)}) collective-permute-start(bf16[2,32,2048]{2,1,0:T(8,128)(2,1)S(1)} %get-tuple-element.302), channel_id=1, source_target_pairs={{0,12},{4,0},{8,4},{12,8},{1,13},{5,1},{9,5},{13,9},{2,14},{6,2},{... | collective-permute-start | bytes 786440 | tf_op jit(solution)/shard_map/cond/branch_3_fun/ppermute | solution.py:385
  74.2 1.6 %branch_3_fun.14 = bf16[2,128,256]{2,1,0:T(8,128)(2,1)S(1)} custom-call(s32[70]{0:T(128)S(1)} %get-tuple-element.316.meta, bf16[2,32,2048]{2,1,0:T(8,128)(2,1)S(1)} %get-tuple-element.305.rest_0_.rest_5_, bf16[2,32,2048]{2,1,0:T(8,128)(2,1)S(1)} %collective-permute-done.104.rest_1_.rest_6_, ...), custom_call_target="tpu_custom_call" | custom-call | flops 268435456 | bytes 2097152 | tf_op jit(solution)/shard_map/cond/branch_3_fun/pallas_call | solution.py:247
  76.0 1.6 %collective-permute-start.98 = (bf16[4,128,256]{2,1,0:T(8,128)(2,1)S(1)}, bf16[4,128,256]{2,1,0:T(8,128)(2,1)S(1)}, u32[]{:S(2)}, u32[]{:S(2)}) collective-permute-start(bf16[4,128,256]{2,1,0:T(8,128)(2,1)S(1)} %add_convert_fusion.9.h1), channel_id=1, source_target_pairs={{0,2},{2,0},{1,3},{3,1},{4,6},{6,4},{5,7},{7,5},{8,10},{10,8},{9,1... | collective-permute-start | bytes 786440 | tf_op jit(solution)/shard_map/cond/branch_3_fun/ppermute | solution.py:20
  78.9 6.3 %collective-permute-done.98.h2 = bf16[4,128,256]{2,1,0:T(8,128)(2,1)S(1)} collective-permute-done((bf16[4,128,256]{2,1,0:T(8,128)(2,1)S(1)}, bf16[4,128,256]{2,1,0:T(8,128)(2,1)S(1)}, u32[]{:S(2)}, u32[]{:S(2)}) %collective-permute-start.98) | collective-permute-done | bytes 262176 | tf_op jit(solution)/shard_map/cond/branch_3_fun/ppermute | solution.py:20
  85.8 1.7 %collective-permute-done.108.g2 = bf16[2,128,256]{2,1,0:T(8,128)(2,1)S(1)} collective-permute-done((bf16[2,128,256]{2,1,0:T(8,128)(2,1)S(1)}, bf16[2,128,256]{2,1,0:T(8,128)(2,1)S(1)}, u32[]{:S(2)}, u32[]{:S(2)}) %collective-permute-start.108) | collective-permute-done | bytes 131104 | tf_op jit(solution)/shard_map/cond/branch_3_fun/ppermute | solution.py:20
  89.1 1.6 %branch_3_fun.16 = bf16[2,128,256]{2,1,0:T(8,128)(2,1)S(1)} custom-call(s32[70]{0:T(128)S(1)} %get-tuple-element.316.meta, bf16[2,32,2048]{2,1,0:T(8,128)(2,1)S(1)} %get-tuple-element.299.rest_0_.rest_1_, bf16[2,32,2048]{2,1,0:T(8,128)(2,1)S(1)} %collective-permute-done.100.rest_1_.rest_2_, ...), custom_call_target="tpu_custom_call" | custom-call | flops 268435456 | bytes 2097152 | tf_op jit(solution)/shard_map/cond/branch_3_fun/pallas_call | solution.py:247
  92.2 1.6 %collective-permute-start.110 = (bf16[2,128,256]{2,1,0:T(8,128)(2,1)S(1)}, bf16[2,128,256]{2,1,0:T(8,128)(2,1)S(1)}, u32[]{:S(2)}, u32[]{:S(2)}) collective-permute-start(bf16[2,128,256]{2,1,0:T(8,128)(2,1)S(1)} %add_convert_fusion.10.g1), channel_id=1, source_target_pairs={{0,2},{2,0},{1,3},{3,1},{4,6},{6,4},{5,7},{7,5},{8,10},{10,8},{9,1... | collective-permute-start | bytes 393224 | tf_op jit(solution)/shard_map/cond/branch_3_fun/ppermute | solution.py:20
  95.1 2.6 %branch_3_fun.21 = (bf16[128,2048]{1,0:T(8,128)(2,1)S(1)}, bf16[128,2048]{1,0:T(8,128)(2,1)S(1)}) custom-call(s32[70]{0:T(128)S(1)} %get-tuple-element.316.meta, bf16[4,128,256]{2,1,0:T(8,128)(2,1)S(1)} %get-tuple-element.320.rest_0_, bf16[2,32,2048]{2,1,0:T(8,128)(2,1)S(1)} %get-tuple-element.299.rest_0_.rest_1_, ...), custom_call_target="tpu_custom_call" | custom-call | flops 536870912 | bytes 3145728 | tf_op jit(solution)/shard_map/cond/branch_3_fun/pallas_call | solution.py:327
  102.1 6.6 %collective-permute-start.111 = (bf16[2,32,2048]{2,1,0:T(8,128)(2,1)S(1)}, bf16[2,32,2048]{2,1,0:T(8,128)(2,1)S(1)}, u32[]{:S(2)}, u32[]{:S(2)}) collective-permute-start(bf16[2,32,2048]{2,1,0:T(8,128)(2,1)S(1)} %get-tuple-element.309), channel_id=1, source_target_pairs={{4,0},{8,4},{12,8},{0,12},{5,1},{9,5},{13,9},{1,13},{6,2},{10,6},{... | collective-permute-start | bytes 786440 | tf_op jit(solution)/shard_map/cond/branch_3_fun/ppermute | solution.py:385
  108.8 5.6 %collective-permute-start.113 = (bf16[2,32,2048]{2,1,0:T(8,128)(2,1)S(1)}, bf16[2,32,2048]{2,1,0:T(8,128)(2,1)S(1)}, u32[]{:S(2)}, u32[]{:S(2)}) collective-permute-start(bf16[2,32,2048]{2,1,0:T(8,128)(2,1)S(1)} %get-tuple-element.311), channel_id=1, source_target_pairs={{12,0},{0,4},{4,8},{8,12},{13,1},{1,5},{5,9},{9,13},{14,2},{2,6},{... | collective-permute-start | bytes 786440 | tf_op jit(solution)/shard_map/cond/branch_3_fun/ppermute | solution.py:385
  114.4 2.6 %branch_3_fun.20 = (bf16[128,2048]{1,0:T(8,128)(2,1)S(1)}, bf16[128,2048]{1,0:T(8,128)(2,1)S(1)}) custom-call(s32[70]{0:T(128)S(1)} %get-tuple-element.316.meta, bf16[2,128,256]{2,1,0:T(8,128)(2,1)S(1)} %get-tuple-element.317.rest_0_, bf16[2,128,256]{2,1,0:T(8,128)(2,1)S(1)} %get-tuple-element.306.rest_1_, ...), custom_call_target="tpu_custom_call" | custom-call | flops 536870912 | bytes 3145728 | tf_op jit(solution)/shard_map/cond/branch_3_fun/pallas_call | solution.py:327
  117.0 2.4 %collective-permute-done.116.rest_7_ = bf16[2,32,2048]{2,1,0:T(8,128)(2,1)S(1)} collective-permute-done((bf16[2,32,2048]{2,1,0:T(8,128)(2,1)S(1)}, bf16[2,32,2048]{2,1,0:T(8,128)(2,1)S(1)}, u32[]{:S(2)}, u32[]{:S(2)}) %collective-permute-start.116) | collective-permute-done | bytes 262176 | tf_op jit(solution)/shard_map/cond/branch_3_fun/ppermute | solution.py:385
  120.0 20.4 %collective-permute-done.112.rest_2_ = bf16[2,32,2048]{2,1,0:T(8,128)(2,1)S(1)} collective-permute-done((bf16[2,32,2048]{2,1,0:T(8,128)(2,1)S(1)}, bf16[2,32,2048]{2,1,0:T(8,128)(2,1)S(1)}, u32[]{:S(2)}, u32[]{:S(2)}) %collective-permute-start.112) | collective-permute-done | bytes 262176 | tf_op jit(solution)/shard_map/cond/branch_3_fun/ppermute | solution.py:385
  145.6 8.8 %collective-permute-done.117 = bf16[4,32,2048]{2,1,0:T(8,128)(2,1)S(1)} collective-permute-done((bf16[4,32,2048]{2,1,0:T(8,128)(2,1)S(1)}, bf16[4,32,2048]{2,1,0:T(8,128)(2,1)S(1)}, u32[]{:S(2)}, u32[]{:S(2)}) %collective-permute-start.117) | collective-permute-done | bytes 524320 | tf_op jit(solution)/shard_map/cond/branch_3_fun/ppermute | solution.py:20
  (85 shorter events, 33.6 us)
Async XLA Ops:
  1.7 18.2 %collective-permute-start.140 = (bf16[4,32,2048]{2,1,0:T(8,128)(2,1)S(1)}, bf16[4,32,2048]{2,1,0:T(8,128)(2,1)S(1)}, u32[]{:S(2)}, u32[]{:S(2)}) collective-permute-start(bf16[4,32,2048]{2,1,0:T(8,128)(2,1)S(1)} %dynamic-slice_bitcast_fusion.1), channel_id=1, source_target_pairs={{0,2},{2,0},{1,3},{3,1},{4,6},{6,4},{5,7},{7,5},{8,10},{10,8},{9,1... | collective-permute-start | bytes 1572872 | tf_op jit(solution)/shard_map/ppermute | solution.py:20
  4.7 12.0 %collective-permute-start.139 = (s32[1,4,1]{1,2,0:T(1,128)S(1)}, s32[1,4,1]{1,2,0:T(1,128)S(1)}, u32[]{:S(2)}, u32[]{:S(2)}) collective-permute-start(s32[1,4,1]{1,2,0:T(1,128)S(1)} %copy-done.2), channel_id=1, source_target_pairs={{0,2},{2,0},{1,3},{3,1},{4,6},{6,4},{5,7},{7,5},{8,10},{10,8},{9,1... | collective-permute-start | bytes 56 | tf_op jit(solution)/shard_map/ppermute | solution.py:20
  6.2 16.0 %collective-permute-start.141 = (bf16[1,32,2048]{2,1,0:T(8,128)(2,1)S(1)}, bf16[1,32,2048]{2,1,0:T(8,128)(2,1)}, u32[]{:S(2)}, u32[]{:S(2)}) collective-permute-start(bf16[1,32,2048]{2,1,0:T(8,128)(2,1)S(1)} %get-tuple-element.374), channel_id=1, source_target_pairs={{0,4},{4,8},{8,12},{12,0},{1,5},{5,9},{9,13},{13,1},{2,6},{6,10},{... | collective-permute-start | bytes 393224 | tf_op jit(solution)/shard_map/ppermute | solution.py:385
  8.3 13.9 %collective-permute-start.142 = (bf16[1,32,2048]{2,1,0:T(8,128)(2,1)S(1)}, bf16[1,32,2048]{2,1,0:T(8,128)(2,1)}, u32[]{:S(2)}, u32[]{:S(2)}) collective-permute-start(bf16[1,32,2048]{2,1,0:T(8,128)(2,1)S(1)} %get-tuple-element.375), channel_id=1, source_target_pairs={{0,8},{4,12},{8,0},{12,4},{1,9},{5,13},{9,1},{13,5},{2,10},{6,14},... | collective-permute-start | bytes 393224 | tf_op jit(solution)/shard_map/ppermute | solution.py:385
  10.9 11.3 %collective-permute-start.143 = (bf16[1,32,2048]{2,1,0:T(8,128)(2,1)S(1)}, bf16[1,32,2048]{2,1,0:T(8,128)(2,1)}, u32[]{:S(2)}, u32[]{:S(2)}) collective-permute-start(bf16[1,32,2048]{2,1,0:T(8,128)(2,1)S(1)} %get-tuple-element.376), channel_id=1, source_target_pairs={{0,12},{4,0},{8,4},{12,8},{1,13},{5,1},{9,5},{13,9},{2,14},{6,2},{... | collective-permute-start | bytes 393224 | tf_op jit(solution)/shard_map/ppermute | solution.py:385
  22.4 15.5 %collective-permute-start.99 = (bf16[4,32,2048]{2,1,0:T(8,128)(2,1)S(1)}, bf16[4,32,2048]{2,1,0:T(8,128)(2,1)S(1)}, u32[]{:S(2)}, u32[]{:S(2)}) collective-permute-start(bf16[4,32,2048]{2,1,0:T(8,128)(2,1)S(1)} %get-tuple-element.297), channel_id=1, source_target_pairs={{0,2},{2,0},{1,3},{3,1},{4,6},{6,4},{5,7},{7,5},{8,10},{10,8},{9,1... | collective-permute-start | bytes 1572872 | tf_op jit(solution)/shard_map/cond/branch_3_fun/ppermute | solution.py:20
  24.2 24.5 %collective-permute-start.96 = (bf16[128,2048]{1,0:T(8,128)(2,1)}, bf16[128,2048]{1,0:T(8,128)(2,1)}, u32[]{:S(2)}, u32[]{:S(2)}) collective-permute-start(bf16[128,2048]{1,0:T(8,128)(2,1)} %get-tuple-element.294), channel_id=1, source_target_pairs={{0,2},{2,0},{1,3},{3,1},{4,6},{6,4},{5,7},{7,5},{8,10},{10,8},{9,1... | collective-permute-start | bytes 1572872 | tf_op jit(solution)/shard_map/cond/branch_3_fun/ppermute | solution.py:20
  24.5 40.6 %collective-permute-start.103 = (bf16[128,2048]{1,0:T(8,128)(2,1)}, bf16[128,2048]{1,0:T(8,128)(2,1)}, u32[]{:S(2)}, u32[]{:S(2)}) collective-permute-start(bf16[128,2048]{1,0:T(8,128)(2,1)} %get-tuple-element.304), channel_id=1, source_target_pairs={{0,2},{2,0},{1,3},{3,1},{4,6},{6,4},{5,7},{7,5},{8,10},{10,8},{9,1... | collective-permute-start | bytes 1572872 | tf_op jit(solution)/shard_map/cond/branch_3_fun/ppermute | solution.py:20
  26.3 7.0 %collective-permute-start.90 = (bf16[1,32,2048]{2,1,0:T(8,128)(2,1)S(1)}, bf16[1,32,2048]{2,1,0:T(8,128)(2,1)S(1)}, u32[]{:S(2)}, u32[]{:S(2)}) collective-permute-start(bf16[1,32,2048]{2,1,0:T(8,128)(2,1)S(1)} %get-tuple-element.289), channel_id=1, source_target_pairs={{0,4},{4,8},{8,12},{12,0},{1,5},{5,9},{9,13},{13,1},{2,6},{6,10},{... | collective-permute-start | bytes 393224 | tf_op jit(solution)/shard_map/cond/branch_3_fun/ppermute | solution.py:385
  27.8 9.4 %collective-permute-start.92 = (bf16[1,32,2048]{2,1,0:T(8,128)(2,1)S(1)}, bf16[1,32,2048]{2,1,0:T(8,128)(2,1)S(1)}, u32[]{:S(2)}, u32[]{:S(2)}) collective-permute-start(bf16[1,32,2048]{2,1,0:T(8,128)(2,1)S(1)} %get-tuple-element.291), channel_id=1, source_target_pairs={{0,12},{4,0},{8,4},{12,8},{1,13},{5,1},{9,5},{13,9},{2,14},{6,2},{... | collective-permute-start | bytes 393224 | tf_op jit(solution)/shard_map/cond/branch_3_fun/ppermute | solution.py:385
  33.3 28.3 %collective-permute-start.95 = (bf16[2,32,2048]{2,1,0:T(8,128)(2,1)S(1)}, bf16[2,32,2048]{2,1,0:T(8,128)(2,1)S(1)}, u32[]{:S(2)}, u32[]{:S(2)}) collective-permute-start(bf16[2,32,2048]{2,1,0:T(8,128)(2,1)S(1)} %get-tuple-element.292.rest_8_.rest_10_), channel_id=1, source_target_pairs={{0,12},{1,13},{2,14},{3,15},{16,28},{17,29},{18,30},{19,31}} | collective-permute-start | bytes 786440 | tf_op jit(solution)/shard_map/cond/branch_3_fun/ppermute | solution.py:385
  37.3 25.0 %collective-permute-start.94 = (bf16[2,32,2048]{2,1,0:T(8,128)(2,1)S(1)}, bf16[2,32,2048]{2,1,0:T(8,128)(2,1)S(1)}, u32[]{:S(2)}, u32[]{:S(2)}) collective-permute-start(bf16[2,32,2048]{2,1,0:T(8,128)(2,1)S(1)} %get-tuple-element.292.rest_8_.rest_10_), channel_id=1, source_target_pairs={{4,12},{5,13},{6,14},{7,15},{20,28},{21,29},{22,30},{23,31}} | collective-permute-start | bytes 786440 | tf_op jit(solution)/shard_map/cond/branch_3_fun/ppermute | solution.py:385
  38.0 25.0 %collective-permute-start.93 = (bf16[2,32,2048]{2,1,0:T(8,128)(2,1)S(1)}, bf16[2,32,2048]{2,1,0:T(8,128)(2,1)S(1)}, u32[]{:S(2)}, u32[]{:S(2)}) collective-permute-start(bf16[2,32,2048]{2,1,0:T(8,128)(2,1)S(1)} %get-tuple-element.292.rest_8_.rest_10_), channel_id=1, source_target_pairs={{8,12},{9,13},{10,14},{11,15},{24,28},{25,29},{26,30},{27,31}} | collective-permute-start | bytes 786440 | tf_op jit(solution)/shard_map/cond/branch_3_fun/ppermute | solution.py:385
  48.7 7.3 %collective-permute-start.91 = (bf16[1,32,2048]{2,1,0:T(8,128)(2,1)S(1)}, bf16[1,32,2048]{2,1,0:T(8,128)(2,1)S(1)}, u32[]{:S(2)}, u32[]{:S(2)}) collective-permute-start(bf16[1,32,2048]{2,1,0:T(8,128)(2,1)S(1)} %copy-done.36), channel_id=1, source_target_pairs={{0,8},{4,12},{8,0},{12,4},{1,9},{5,13},{9,1},{13,5},{2,10},{6,14},... | collective-permute-start | bytes 393224 | tf_op jit(solution)/shard_map/cond/branch_3_fun/ppermute | solution.py:385
  56.0 11.9 %collective-permute-start.106 = (bf16[2,32,2048]{2,1,0:T(8,128)(2,1)S(1)}, bf16[2,32,2048]{2,1,0:T(8,128)(2,1)S(1)}, u32[]{:S(2)}, u32[]{:S(2)}) collective-permute-start(bf16[2,32,2048]{2,1,0:T(8,128)(2,1)S(1)} %get-tuple-element.305.rest_0_.rest_5_), channel_id=1, source_target_pairs={{0,12},{1,13},{2,14},{3,15},{16,28},{17,29},{18,30},{19,31}} | collective-permute-start | bytes 786440 | tf_op jit(solution)/shard_map/cond/branch_3_fun/ppermute | solution.py:385
  61.7 7.0 %collective-permute-start.105 = (bf16[2,32,2048]{2,1,0:T(8,128)(2,1)S(1)}, bf16[2,32,2048]{2,1,0:T(8,128)(2,1)S(1)}, u32[]{:S(2)}, u32[]{:S(2)}) collective-permute-start(bf16[2,32,2048]{2,1,0:T(8,128)(2,1)S(1)} %get-tuple-element.305.rest_0_.rest_5_), channel_id=1, source_target_pairs={{4,12},{5,13},{6,14},{7,15},{20,28},{21,29},{22,30},{23,31}} | collective-permute-start | bytes 786440 | tf_op jit(solution)/shard_map/cond/branch_3_fun/ppermute | solution.py:385
  62.3 11.9 %collective-permute-start.104 = (bf16[2,32,2048]{2,1,0:T(8,128)(2,1)S(1)}, bf16[2,32,2048]{2,1,0:T(8,128)(2,1)S(1)}, u32[]{:S(2)}, u32[]{:S(2)}) collective-permute-start(bf16[2,32,2048]{2,1,0:T(8,128)(2,1)S(1)} %get-tuple-element.305.rest_0_.rest_5_), channel_id=1, source_target_pairs={{8,12},{9,13},{10,14},{11,15},{24,28},{25,29},{26,30},{27,31}} | collective-permute-start | bytes 786440 | tf_op jit(solution)/shard_map/cond/branch_3_fun/ppermute | solution.py:385
  65.0 10.9 %collective-permute-start.97 = (bf16[4,128,256]{2,1,0:T(8,128)(2,1)S(1)}, bf16[4,128,256]{2,1,0:T(8,128)(2,1)S(1)}, u32[]{:S(2)}, u32[]{:S(2)}) collective-permute-start(bf16[4,128,256]{2,1,0:T(8,128)(2,1)S(1)} %branch_3_fun.11), channel_id=1, source_target_pairs={{0,1},{1,0},{2,3},{3,2},{4,5},{5,4},{6,7},{7,6},{8,9},{9,8},{10,11... | collective-permute-start | bytes 786440 | tf_op jit(solution)/shard_map/cond/branch_3_fun/ppermute | solution.py:20
  65.1 24.0 %collective-permute-start.100 = (bf16[2,32,2048]{2,1,0:T(8,128)(2,1)S(1)}, bf16[2,32,2048]{2,1,0:T(8,128)(2,1)S(1)}, u32[]{:S(2)}, u32[]{:S(2)}) collective-permute-start(bf16[2,32,2048]{2,1,0:T(8,128)(2,1)S(1)} %get-tuple-element.300), channel_id=1, source_target_pairs={{0,4},{4,8},{8,12},{12,0},{1,5},{5,9},{9,13},{13,1},{2,6},{6,10},{... | collective-permute-start | bytes 786440 | tf_op jit(solution)/shard_map/cond/branch_3_fun/ppermute | solution.py:385
  67.9 21.2 %collective-permute-start.101 = (bf16[2,32,2048]{2,1,0:T(8,128)(2,1)S(1)}, bf16[2,32,2048]{2,1,0:T(8,128)(2,1)S(1)}, u32[]{:S(2)}, u32[]{:S(2)}) collective-permute-start(bf16[2,32,2048]{2,1,0:T(8,128)(2,1)S(1)} %get-tuple-element.301), channel_id=1, source_target_pairs={{0,8},{4,12},{8,0},{12,4},{1,9},{5,13},{9,1},{13,5},{2,10},{6,14},... | collective-permute-start | bytes 786440 | tf_op jit(solution)/shard_map/cond/branch_3_fun/ppermute | solution.py:385
  68.6 20.5 %collective-permute-start.102 = (bf16[2,32,2048]{2,1,0:T(8,128)(2,1)S(1)}, bf16[2,32,2048]{2,1,0:T(8,128)(2,1)S(1)}, u32[]{:S(2)}, u32[]{:S(2)}) collective-permute-start(bf16[2,32,2048]{2,1,0:T(8,128)(2,1)S(1)} %get-tuple-element.302), channel_id=1, source_target_pairs={{0,12},{4,0},{8,4},{12,8},{1,13},{5,1},{9,5},{13,9},{2,14},{6,2},{... | collective-permute-start | bytes 786440 | tf_op jit(solution)/shard_map/cond/branch_3_fun/ppermute | solution.py:385
  76.0 9.2 %collective-permute-start.98 = (bf16[4,128,256]{2,1,0:T(8,128)(2,1)S(1)}, bf16[4,128,256]{2,1,0:T(8,128)(2,1)S(1)}, u32[]{:S(2)}, u32[]{:S(2)}) collective-permute-start(bf16[4,128,256]{2,1,0:T(8,128)(2,1)S(1)} %add_convert_fusion.9.h1), channel_id=1, source_target_pairs={{0,2},{2,0},{1,3},{3,1},{4,6},{6,4},{5,7},{7,5},{8,10},{10,8},{9,1... | collective-permute-start | bytes 786440 | tf_op jit(solution)/shard_map/cond/branch_3_fun/ppermute | solution.py:20
  77.6 10.0 %collective-permute-start.108 = (bf16[2,128,256]{2,1,0:T(8,128)(2,1)S(1)}, bf16[2,128,256]{2,1,0:T(8,128)(2,1)S(1)}, u32[]{:S(2)}, u32[]{:S(2)}) collective-permute-start(bf16[2,128,256]{2,1,0:T(8,128)(2,1)S(1)} %add_convert_fusion.11.g1), channel_id=1, source_target_pairs={{0,2},{2,0},{1,3},{3,1},{4,6},{6,4},{5,7},{7,5},{8,10},{10,8},{9,1... | collective-permute-start | bytes 393224 | tf_op jit(solution)/shard_map/cond/branch_3_fun/ppermute | solution.py:20
  93.8 15.0 %collective-permute-start.114 = (bf16[2,32,2048]{2,1,0:T(8,128)(2,1)S(1)}, bf16[2,32,2048]{2,1,0:T(8,128)(2,1)S(1)}, u32[]{:S(2)}, u32[]{:S(2)}) collective-permute-start(bf16[2,32,2048]{2,1,0:T(8,128)(2,1)S(1)} %get-tuple-element.313), channel_id=1, source_target_pairs={{12,8},{13,9},{14,10},{15,11},{28,24},{29,25},{30,26},{31,27}} | collective-permute-start | bytes 786440 | tf_op jit(solution)/shard_map/cond/branch_3_fun/ppermute | solution.py:385
  94.4 14.3 %collective-permute-start.115 = (bf16[2,32,2048]{2,1,0:T(8,128)(2,1)S(1)}, bf16[2,32,2048]{2,1,0:T(8,128)(2,1)S(1)}, u32[]{:S(2)}, u32[]{:S(2)}) collective-permute-start(bf16[2,32,2048]{2,1,0:T(8,128)(2,1)S(1)} %get-tuple-element.314), channel_id=1, source_target_pairs={{12,4},{13,5},{14,6},{15,7},{28,20},{29,21},{30,22},{31,23}} | collective-permute-start | bytes 786440 | tf_op jit(solution)/shard_map/cond/branch_3_fun/ppermute | solution.py:385
  97.8 45.4 %collective-permute-start.119 = (bf16[128,2048]{1,0:T(8,128)(2,1)S(1)}, bf16[128,2048]{1,0:T(8,128)(2,1)S(1)}, u32[]{:S(2)}, u32[]{:S(2)}) collective-permute-start(bf16[128,2048]{1,0:T(8,128)(2,1)S(1)} %get-tuple-element.323), channel_id=1, source_target_pairs={{0,2},{2,0},{1,3},{3,1},{4,6},{6,4},{5,7},{7,5},{8,10},{10,8},{9,1... | collective-permute-start | bytes 1572872 | tf_op jit(solution)/shard_map/cond/branch_3_fun/ppermute | solution.py:20
  99.3 20.1 %collective-permute-start.116 = (bf16[2,32,2048]{2,1,0:T(8,128)(2,1)S(1)}, bf16[2,32,2048]{2,1,0:T(8,128)(2,1)S(1)}, u32[]{:S(2)}, u32[]{:S(2)}) collective-permute-start(bf16[2,32,2048]{2,1,0:T(8,128)(2,1)S(1)} %get-tuple-element.315), channel_id=1, source_target_pairs={{12,0},{13,1},{14,2},{15,3},{28,16},{29,17},{30,18},{31,19}} | collective-permute-start | bytes 786440 | tf_op jit(solution)/shard_map/cond/branch_3_fun/ppermute | solution.py:385
  102.1 17.8 %collective-permute-start.111 = (bf16[2,32,2048]{2,1,0:T(8,128)(2,1)S(1)}, bf16[2,32,2048]{2,1,0:T(8,128)(2,1)S(1)}, u32[]{:S(2)}, u32[]{:S(2)}) collective-permute-start(bf16[2,32,2048]{2,1,0:T(8,128)(2,1)S(1)} %get-tuple-element.309), channel_id=1, source_target_pairs={{4,0},{8,4},{12,8},{0,12},{5,1},{9,5},{13,9},{1,13},{6,2},{10,6},{... | collective-permute-start | bytes 786440 | tf_op jit(solution)/shard_map/cond/branch_3_fun/ppermute | solution.py:385
  108.8 31.6 %collective-permute-start.112 = (bf16[2,32,2048]{2,1,0:T(8,128)(2,1)S(1)}, bf16[2,32,2048]{2,1,0:T(8,128)(2,1)S(1)}, u32[]{:S(2)}, u32[]{:S(2)}) collective-permute-start(bf16[2,32,2048]{2,1,0:T(8,128)(2,1)S(1)} %get-tuple-element.310), channel_id=1, source_target_pairs={{8,0},{12,4},{0,8},{4,12},{9,1},{13,5},{1,9},{5,13},{10,2},{14,6},... | collective-permute-start | bytes 786440 | tf_op jit(solution)/shard_map/cond/branch_3_fun/ppermute | solution.py:385
  108.8 31.6 %collective-permute-start.113 = (bf16[2,32,2048]{2,1,0:T(8,128)(2,1)S(1)}, bf16[2,32,2048]{2,1,0:T(8,128)(2,1)S(1)}, u32[]{:S(2)}, u32[]{:S(2)}) collective-permute-start(bf16[2,32,2048]{2,1,0:T(8,128)(2,1)S(1)} %get-tuple-element.311), channel_id=1, source_target_pairs={{12,0},{0,4},{4,8},{8,12},{13,1},{1,5},{5,9},{9,13},{14,2},{2,6},{... | collective-permute-start | bytes 786440 | tf_op jit(solution)/shard_map/cond/branch_3_fun/ppermute | solution.py:385
  119.4 25.0 %collective-permute-start.118 = (bf16[128,2048]{1,0:T(8,128)(2,1)S(1)}, bf16[128,2048]{1,0:T(8,128)(2,1)S(1)}, u32[]{:S(2)}, u32[]{:S(2)}) collective-permute-start(bf16[128,2048]{1,0:T(8,128)(2,1)S(1)} %get-tuple-element.319), channel_id=1, source_target_pairs={{0,2},{2,0},{1,3},{3,1},{4,6},{6,4},{5,7},{7,5},{8,10},{10,8},{9,1... | collective-permute-start | bytes 1572872 | tf_op jit(solution)/shard_map/cond/branch_3_fun/ppermute | solution.py:20
  141.3 13.2 %collective-permute-start.117 = (bf16[4,32,2048]{2,1,0:T(8,128)(2,1)S(1)}, bf16[4,32,2048]{2,1,0:T(8,128)(2,1)S(1)}, u32[]{:S(2)}, u32[]{:S(2)}) collective-permute-start(bf16[4,32,2048]{2,1,0:T(8,128)(2,1)S(1)} %branch_3_fun.18), channel_id=1, source_target_pairs={{0,2},{2,0},{1,3},{3,1},{4,6},{6,4},{5,7},{7,5},{8,10},{10,8},{9,1... | collective-permute-start | bytes 1572872 | tf_op jit(solution)/shard_map/cond/branch_3_fun/ppermute | solution.py:20
  (13 other events, 88.6 us)
